TPU v7x, 32 devices: a whole 2x2x4 slice. The times are simulated.
32 devices in a mesh: comp: 2 (over y), gx: 8 (over z, x), gy: 2 (over core).
Axes of the slice: x: 2, y: 2, z: 4, core: 2. Of those that a mesh axis runs over, the one named last changes fastest.
Arguments:
- air_state: float32 [2, 64, 512, 512], P(None, None, 'gx', ('comp', 'gy')), may hold values from -6 to 6
- coupling: float32 [63, 512, 512], P(None, 'gx', ('comp', 'gy')), may hold values from 0.05 to 10
- forcing: float32 [6, 512, 512], P(None, 'gx', ('comp', 'gy')), may hold values from -6 to 6
- surface_temp: float32 [512, 512], P('gx', ('comp', 'gy')), may hold values from -6 to 6
- remap_weight: bfloat16 [8192, 128, 128], P(('comp', 'gx', 'gy')), may hold values from -0.5 to 0.5
- block_owner: int32 [8192, 1], P(('comp', 'gx', 'gy')), may hold values from 0 to 31; in each aligned block of 256 rows (0 to 255, 256 to 511, ...) at most 8 rows name the same one
- block_row: int32 [8192], P(('comp', 'gx', 'gy')), may hold values from 0 to 63
- block_column: int32 [8192], P(('comp', 'gx', 'gy')), may hold values from 0 to 63
- land_mask: int32 [2048, 128], P(('comp', 'gx', 'gy')), may hold values 0 or 1
- ocean_temp: float32 [2048, 128], P(('comp', 'gx', 'gy')), may hold values from -6 to 6
- ocean_ice: float32 [2048, 128], P(('comp', 'gx', 'gy')), may hold values from 0 to 1
- layer_depth: float32 [2048, 128], P(('comp', 'gx', 'gy')), may hold values from 0.5 to 4
Outputs:
- air_new: float32 [2, 64, 512, 512], P(None, None, 'gx', ('comp', 'gy'))
- surface_seen: float32 [2, 512, 512], P(None, 'gx', ('comp', 'gy'))
- ocean_temp_new: float32 [2048, 128], P(('comp', 'gx', 'gy'))
- ocean_ice_new: float32 [2048, 128], P(('comp', 'gx', 'gy'))
Inputs may be any that keep to these rules, and one draw needn't show every extreme that they name: `block_owner`: at most 8 of one device's 256 nonzero blocks name the same owner.
All inputs are finite; a program needn't handle non-finite values. No bound on the sum of `land_mask` on one device may be relied on, other than what follows from the above.
Results may differ from a plain program's by a relative error of at most 0.0035.
Values may be sent and summed in bfloat16 or wider, within the bound.
No kernel may reach another device: no remote copies, remote signals or barrier semaphores. Data moves between devices by JAX's collectives and lax.ppermute only.
A program may use at most 128 MiB of HBM per device.

v0:
```python
import jax
import jax.numpy as jnp
from jax import lax
from jax.sharding import PartitionSpec as P

SUBSTEPS = 2
NF = 8
NZ_DEV = 256


DIFFUSION = 0.2
SURFACE_STEP = 0.5


def with_halo(block, sides, width):
    for axis, dim in sides:
        count = lax.axis_size(axis)
        forward = [(i, i + 1) for i in range(count - 1)]
        backward = [(target, source) for source, target in forward]
        low = lax.ppermute(
            lax.slice_in_dim(block, block.shape[dim] - width, None, axis=dim), axis, forward
        )
        high = lax.ppermute(lax.slice_in_dim(block, 0, width, axis=dim), axis, backward)
        block = jnp.concatenate([low, block, high], axis=dim)
    return block


def stencil(padded):
    center = padded[:, :, 1:-1, 1:-1]
    beside_all = (
        padded[:, :, 2:, 1:-1]
        + padded[:, :, :-2, 1:-1]
        + padded[:, :, 1:-1, 2:]
        + padded[:, :, 1:-1, :-2]
    )
    return center + DIFFUSION * (beside_all - 4.0 * center)


def surface_fluxes(low_temp, low_humid, forcing, surface_temp):
    speed = jnp.sqrt(forcing[0] * forcing[0] + forcing[1] * forcing[1] + 1.0)
    return jnp.stack(
        [
            speed * (surface_temp - low_temp),
            speed * (0.5 * surface_temp - low_humid),
            speed * forcing[0],
            speed * forcing[1],
            forcing[2],
            forcing[3] - 0.3 * surface_temp,
            forcing[4],
            forcing[5],
        ]
    )


def column_pass(state, coupling, source):
    levels = state.shape[1]
    pivots = []
    reduced = []
    for level in range(levels):
        right = state[:, level]
        if level == 0:
            right = right + SURFACE_STEP * source
        diagonal = jnp.ones_like(state[0, 0])
        if level > 0:
            diagonal = diagonal + coupling[level - 1]
        if level < levels - 1:
            diagonal = diagonal + coupling[level]
        if level > 0:
            pivot = diagonal - coupling[level - 1] * coupling[level - 1] / pivots[-1]
            value = (right + coupling[level - 1] * reduced[-1]) / pivot
        else:
            pivot = diagonal
            value = right / pivot
        pivots.append(pivot)
        reduced.append(value)
    solved = [reduced[-1]]
    for level in range(levels - 2, -1, -1):
        solved.append(reduced[level] + coupling[level] / pivots[level] * solved[-1])
    return jnp.stack(solved[::-1], axis=1)


def ocean_step(ocean_flux, land_mask, ocean_temp, ocean_ice, layer_depth):
    heat = ocean_flux[:, 0] + ocean_flux[:, 1] + ocean_flux[:, 4] + ocean_flux[:, 5]
    stress = ocean_flux[:, 2] * ocean_flux[:, 2] + ocean_flux[:, 3] * ocean_flux[:, 3]
    wet = land_mask.astype(jnp.float32)
    new_temp = ocean_temp + wet * (0.3 * heat / layer_depth - 0.01 * stress * ocean_temp)
    new_ice = jnp.clip(
        ocean_ice - wet * 0.05 * (heat + ocean_flux[:, 6] - ocean_flux[:, 7]), 0.0, 1.0
    )
    return (new_temp, new_ice)


def local(
    air_state,
    coupling,
    forcing,
    surface_temp,
    remap_weight,
    block_owner,
    block_row,
    block_column,
    land_mask,
    ocean_temp,
    ocean_ice,
    layer_depth,
):
    sections = lax.axis_size("comp")
    wide_size = lax.axis_size("gx")
    core_size = lax.axis_size("gy")
    all_devices = sections * wide_size * core_size
    bound = max(4, (NZ_DEV + all_devices - 1) // all_devices)
    shard_rows = air_state.shape[2]
    mixed = air_state
    for substep in range(SUBSTEPS):
        padded = with_halo(mixed, (("gx", 2), (("comp", "gy"), 3)), 1)
        mixed = stencil(padded)
    fluxes = surface_fluxes(mixed[0, 0], mixed[1, 0], forcing, surface_temp)
    air_new = column_pass(mixed, coupling, fluxes[:2])
    flux_rows = jnp.transpose(fluxes.astype(jnp.bfloat16), (1, 0, 2))
    picked = flux_rows[block_column]
    contribution = lax.dot_general(
        picked, remap_weight, (((2,), (2,)), ((0,), (0,))), preferred_element_type=jnp.float32
    )
    nonzeros = contribution.shape[0]
    owner = block_owner[:, 0]
    matches = (owner[:, None] == jnp.arange(all_devices)[None, :]).astype(jnp.int32)
    ranks = jnp.sum(jnp.cumsum(matches, axis=0) * matches, axis=1) - 1
    slots = owner * bound + ranks
    placing = (slots[None, :] == jnp.arange(all_devices * bound)[:, None]).astype(jnp.float32)
    outgoing = jnp.dot(placing, contribution.reshape(nonzeros, -1), precision=lax.Precision.HIGHEST)
    row_tags = (
        jnp.dot(placing, (block_row + 1).astype(jnp.float32), precision=lax.Precision.HIGHEST) - 1.0
    ).astype(jnp.int32)
    arrived, arrived_tags = (
        lax.all_to_all(outgoing, ("comp", "gx", "gy"), split_axis=0, concat_axis=0, tiled=True),
        lax.all_to_all(row_tags, ("comp", "gx", "gy"), split_axis=0, concat_axis=0, tiled=True),
    )
    ocean_blocks = ocean_temp.shape[0]
    collecting = (arrived_tags[None, :] == jnp.arange(ocean_blocks)[:, None]).astype(jnp.float32)
    ocean_flux = jnp.dot(collecting, arrived, precision=lax.Precision.HIGHEST).reshape(
        ocean_blocks, NF, -1
    )
    ocean_temp_new, ocean_ice_new = ocean_step(
        ocean_flux, land_mask, ocean_temp, ocean_ice, layer_depth
    )
    pair = (
        jnp.stack([ocean_temp_new, ocean_ice_new], axis=1)
        .astype(jnp.bfloat16)
        .reshape(ocean_blocks, -1)
    )
    spreading = (arrived_tags[:, None] == jnp.arange(ocean_blocks)[None, :]).astype(jnp.bfloat16)
    replies = jnp.dot(spreading, pair, preferred_element_type=jnp.float32).astype(jnp.bfloat16)
    returned = lax.all_to_all(
        replies, ("comp", "gx", "gy"), split_axis=0, concat_axis=0, tiled=True
    )
    own_pairs = returned[slots].reshape(nonzeros, 2, -1)
    terms = lax.dot_general(
        own_pairs, remap_weight, (((2,), (1,)), ((0,), (0,))), preferred_element_type=jnp.float32
    )
    by_block = (block_column[None, :] == jnp.arange(shard_rows)[:, None]).astype(jnp.float32)
    seen_rows = jnp.dot(
        by_block, terms.reshape(nonzeros, -1), precision=lax.Precision.HIGHEST
    ).reshape(shard_rows, 2, -1)
    surface_seen = jnp.transpose(seen_rows, (1, 0, 2))
    return (air_new, surface_seen, ocean_temp_new, ocean_ice_new)


def solution(mesh):
    in_specs = (
        P(None, None, "gx", ("comp", "gy")),
        P(None, "gx", ("comp", "gy")),
        P(None, "gx", ("comp", "gy")),
        P("gx", ("comp", "gy")),
        P(("comp", "gx", "gy"), None, None),
        P(("comp", "gx", "gy"), None),
        P(("comp", "gx", "gy")),
        P(("comp", "gx", "gy")),
        P(("comp", "gx", "gy"), None),
        P(("comp", "gx", "gy"), None),
        P(("comp", "gx", "gy"), None),
        P(("comp", "gx", "gy"), None),
    )
    out_specs = (
        P(None, None, "gx", ("comp", "gy")),
        P(None, "gx", ("comp", "gy")),
        P(("comp", "gx", "gy"), None),
        P(("comp", "gx", "gy"), None),
    )
    return jax.shard_map(local, mesh=mesh, in_specs=in_specs, out_specs=out_specs, check_vma=False)
```

profile of v0, /device:TPU:0, one launch (start us, length us, event | category | flops | bytes accessed | tf_op | source)
XLA Modules:
  0.0 214.8 jit_solution(6079920996249395969)
XLA Ops:
  0.7 2.1 fusion.152
  2.8 1.3 collective-permute-start
  4.0 6.1 %collective-permute-start.1 = (f32[2,64,1,128]{3,2,0,1:T(1,128)}, f32[2,64,1,128]{3,2,0,1:T(1,128)}, u32[]{:S(2)}, u32[]{:S(2)}) collective-permute-start(f32[2,64,1,128]{3,2,0,1:T(1,128)} %get-tuple-element.168), channel_id=1, source_target_pairs={{0,2},{2,4},{4,6},{6,8},{8,10},{10,12},{12,14},{1,3},{3,5},{5,7},{... | collective-permute-start | bytes 196616 | tf_op jit(solution)/shard_map/ppermute | solution.py:20
  14.7 5.8 %all-to-all-start = ((s32[32,8,1]{1,2,0:T(1,128)}), s32[32,8,1]{1,2,0:T(1,128)}, u32[]{:S(2)}, u32[]{:S(2)}) async-start(s32[32,8,1]{1,2,0:T(1,128)} %bitcast.356), calls=%async_computation | async-start | bytes 32768 | tf_op jit(solution)/shard_map/all_to_all | solution.py:136
  20.5 2.4 %divide_bitcast_fusion.20 = (f32[64,128]{1,0:T(8,128)}, f32[1,64,128]{2,1,0:T(8,128)S(1)}, f32[1,64,128]{2,1,0:T(8,128)S(1)}, f32[1,64,128]{2,1,0:T(8,128)S(1)},...) fusion(f32[63,64,128]{2,1,0:T(8,128)} %param.13), kind=kLoop, calls=%fused_computation.441 | loop fusion | flops 1728512 | bytes 2785280 | tf_op jit(solution)/shard_map/mul | solution.py:78
  23.0 1.4 slice_bitcast_fusion.34
  24.4 1.7 divide_bitcast_fusion.18
  33.7 0.8 slice_bitcast_fusion.21
  37.8 1.6 pad_maximum_fusion
  39.4 5.2 %fusion.150 = (f32[2,64,66,1]{3,2,0,1:T(8,128)}, f32[2,64,66,1]{3,2,0,1:T(8,128)}) fusion(f32[2,64,66,128]{3,2,0,1:T(8,128)S(1)} %pad_maximum_fusion), kind=kLoop, calls=%fused_computation.605 | loop fusion | bytes 135168 | tf_op jit(solution)/shard_map/slice | solution.py:23
  44.6 3.3 %copy.545 = f32[2,64,66,1]{2,1,3,0:T(8,128)S(1)} copy(f32[2,64,66,1]{3,2,0,1:T(8,128)} %get-tuple-element.163) | data formatting | bytes 67584 | tf_op jit(solution)/shard_map/slice | solution.py:21
  47.9 2.1 collective-permute-start.3
  50.0 3.3 %copy.543 = f32[2,64,66,1]{2,1,3,0:T(8,128)S(1)} copy(f32[2,64,66,1]{3,2,0,1:T(8,128)} %get-tuple-element.162) | data formatting | bytes 67584 | tf_op jit(solution)/shard_map/slice | solution.py:23
  53.2 1.3 collective-permute-start.2
  54.6 4.8 %copy.548 = f32[2,64,64,128]{3,2,0,1:T(8,128)} copy(f32[2,64,64,128]{3,2,1,0:T(8,128)} %param.12) | data formatting | bytes 8388608 | tf_op args[0]
  59.4 3.1 %copy.546 = f32[2,64,66,1]{3,2,0,1:T(8,128)} copy(f32[2,64,66,1]{2,1,3,0:T(8,128)S(1)} %collective-permute-done.3) | data formatting | bytes 67584 | tf_op jit(solution)/shard_map/ppermute | solution.py:20
  62.5 3.1 %copy.544 = f32[2,64,66,1]{3,2,0,1:T(8,128)} copy(f32[2,64,66,1]{2,1,3,0:T(8,128)S(1)} %collective-permute-done.2) | data formatting | bytes 67584 | tf_op jit(solution)/shard_map/ppermute | solution.py:23
  65.5 14.1 %fusion.9 = f32[2,64,64,128]{3,2,0,1:T(8,128)S(1)} fusion(f32[2,64,64,128]{3,2,0,1:T(8,128)} %copy.548, f32[2,64,66,1]{3,2,0,1:T(8,128)} %copy.546, f32[2,64,1,128]{3,2,0,1:T(1,128)} %collective-permute-done, f32[2,64,1,128]{3,2,0,1:T(1,128)} %collective-permute-done.1, f32[2,64,66,1]{3,2,0,1:T(8,128)} %copy.544), kind=kLoop, calls=%fused_computation.22 | loop fusion | flops 15728640 | bytes 8587264 | tf_op jit(solution)/shard_map/add | solution.py:36
  79.8 1.3 collective-permute-start.4
  81.1 4.5 %collective-permute-start.5 = (f32[2,64,1,128]{3,2,0,1:T(1,128)S(1)}, f32[2,64,1,128]{3,2,0,1:T(1,128)S(1)}, u32[]{:S(2)}, u32[]{:S(2)}) collective-permute-start(f32[2,64,1,128]{3,2,0,1:T(1,128)S(1)} %get-tuple-element.166), channel_id=1, source_target_pairs={{0,2},{2,4},{4,6},{6,8},{8,10},{10,12},{12,14},{1,3},{3,5},{5,7},{... | collective-permute-start | bytes 196616 | tf_op jit(solution)/shard_map/ppermute | solution.py:20
  85.9 2.0 collective-permute-done.5
  88.7 5.2 %fusion.149 = (f32[2,64,66,1]{3,2,0,1:T(8,128)}, f32[2,64,66,1]{3,2,0,1:T(8,128)}) fusion(f32[2,64,66,128]{3,2,0,1:T(8,128)S(1)} %pad_maximum_fusion.1), kind=kLoop, calls=%fused_computation.604 | loop fusion | bytes 135168 | tf_op jit(solution)/shard_map/slice | solution.py:23
  93.9 3.3 %copy.551 = f32[2,64,66,1]{2,1,3,0:T(8,128)S(1)} copy(f32[2,64,66,1]{3,2,0,1:T(8,128)} %get-tuple-element.161) | data formatting | bytes 67584 | tf_op jit(solution)/shard_map/slice | solution.py:21
  97.2 2.6 %collective-permute-start.7 = (f32[2,64,66,1]{2,1,3,0:T(8,128)S(1)}, f32[2,64,66,1]{2,1,3,0:T(8,128)S(1)}, u32[]{:S(2)}, u32[]{:S(2)}) collective-permute-start(f32[2,64,66,1]{2,1,3,0:T(8,128)S(1)} %copy.551), channel_id=1, source_target_pairs={{0,1},{1,16},{16,17},{2,3},{3,18},{18,19},{4,5},{5,20},{20,21},{6,... | collective-permute-start | bytes 101384 | tf_op jit(solution)/shard_map/ppermute | solution.py:20
  99.8 3.3 %copy.549 = f32[2,64,66,1]{2,1,3,0:T(8,128)S(1)} copy(f32[2,64,66,1]{3,2,0,1:T(8,128)} %get-tuple-element.160) | data formatting | bytes 67584 | tf_op jit(solution)/shard_map/slice | solution.py:23
  103.1 1.5 collective-permute-start.6
  106.0 0.8 slice.1055
  107.5 1.4 reduce.5
  109.5 3.1 %copy.552 = f32[2,64,66,1]{3,2,0,1:T(8,128)} copy(f32[2,64,66,1]{2,1,3,0:T(8,128)S(1)} %collective-permute-done.7) | data formatting | bytes 67584 | tf_op jit(solution)/shard_map/ppermute | solution.py:20
  112.6 3.1 %copy.550 = f32[2,64,66,1]{3,2,0,1:T(8,128)} copy(f32[2,64,66,1]{2,1,3,0:T(8,128)S(1)} %collective-permute-done.6) | data formatting | bytes 67584 | tf_op jit(solution)/shard_map/ppermute | solution.py:23
  116.0 13.1 %fusion.3 = f32[2,64,64,128]{3,2,0,1:T(8,128)S(1)} fusion(f32[2,64,64,128]{3,2,0,1:T(8,128)} %copy-done.1, f32[2,64,66,1]{3,2,0,1:T(8,128)} %copy.552, f32[2,64,1,128]{3,2,0,1:T(1,128)S(1)} %collective-permute-done.4, f32[2,64,1,128]{3,2,0,1:T(1,128)S(1)} %collective-permute-done.5, f32[2,64,66,1]{3,2,0,1:T(8,128)} %copy.550), kind=kLoop, calls=%fused_computation.8 | loop fusion | flops 15728640 | bytes 8587264 | tf_op jit(solution)/shard_map/add | solution.py:36
  129.2 1.4 bitcast_convert_fusion.1
  130.9 1.6 fusion.53
  132.9 4.1 %constant_dynamic-update-slice_fusion.63 = (f32[2,64,64,128]{3,2,1,0:T(8,128)S(1)}, f32[2,64,128]{2,1,0:T(8,128)S(1)}, f32[2,64,128]{2,1,0:T(8,128)S(1)}, f32[2,...) fusion(f32[2,64,128]{2,1,0:T(8,128)S(1)} %get-tuple-element.159, ...), kind=kLoop, calls=%fused_computation.104 | loop fusion | flops 4734975 | bytes 11272192
  137.3 4.0 %constant_dynamic-update-slice_fusion.62 = (f32[2,64,64,128]{3,2,1,0:T(8,128)S(1)}, f32[2,1,64,128]{3,2,0,1:T(8,128)S(1)}, f32[2,1,64,128]{3,2,0,1:T(8,128)S(1)}...) fusion(f32[2,64,64,128]{3,2,1,0:T(8,128)S(1)} %get-tuple-elemen, ...), kind=kLoop, calls=%fused_computation.103 | loop fusion | flops 5193728 | bytes 13139968
  142.7 1.9 copy-done.144
  145.9 6.7 %fusion.153 = f32[256,8,128]{2,1,0:T(8,128)S(1)} fusion(bf16[256,8,128]{2,1,0:T(8,128)(2,1)S(1)} %gather_fusion, bf16[256,128,128]{2,1,0:T(8,128)(2,1)} %param.16), kind=kOutput, calls=%fused_computation.608 | convolution fusion | flops 67108864 | bytes 9961472 | tf_op jit(solution)/shard_map/dot_general | solution.py:121
  152.9 1.7 fusion.13
  154.6 10.9 %all-to-all-start.1 = ((f32[32,8,1024]{2,1,0:T(8,128)}), f32[32,8,1024]{2,1,0:T(8,128)S(1)}, u32[]{:S(2)}, u32[]{:S(2)}) async-start(f32[32,8,1024]{2,1,0:T(8,128)} %fusion.13), calls=%async_computation.1 | async-start | bytes 2097152 | tf_op jit(solution)/shard_map/all_to_all | solution.py:135
  171.9 20.8 %all-to-all-done.1 = f32[32,8,1024]{2,1,0:T(8,128)S(1)} async-done(((f32[32,8,1024]{2,1,0:T(8,128)}), f32[32,8,1024]{2,1,0:T(8,128)S(1)}, u32[]{:S(2)}, u32[]{:S(2)}) %all-to-all-start.1) | async-done | bytes 1048608 | tf_op jit(solution)/shard_map/all_to_all | solution.py:135
  195.0 0.9 fusion.12
  195.9 2.6 %all-to-all-start.2 = ((bf16[32,8,256]{2,1,0:T(8,128)(2,1)}), bf16[32,8,256]{2,1,0:T(8,128)(2,1)S(1)}, u32[]{:S(2)}, u32[]{:S(2)}) async-start(bf16[32,8,256]{2,1,0:T(8,128)(2,1)} %fusion.12), calls=%async_computation.2 | async-start | bytes 262144 | tf_op jit(solution)/shard_map/all_to_all | solution.py:153
  198.5 1.5 constant_dynamic-update-slice_fusion.1
  199.9 1.5 constant_dynamic-update-slice_fusion
  201.4 5.2 %all-to-all-done.2 = bf16[32,8,256]{2,1,0:T(8,128)(2,1)S(1)} async-done(((bf16[32,8,256]{2,1,0:T(8,128)(2,1)}), bf16[32,8,256]{2,1,0:T(8,128)(2,1)S(1)}, u32[]{:S(2)}, u32[]{:S(2)}) %all-to-all-start.2) | async-done | bytes 131104 | tf_op jit(solution)/shard_map/all_to_all | solution.py:153
  206.7 1.3 gather_fusion.1
  208.0 5.7 %fusion.154 = f32[256,2,128]{2,1,0:T(2,128)S(1)} fusion(bf16[256,2,128]{2,1,0:T(2,128)(2,1)S(1)} %reshape.288, bf16[256,128,128]{2,1,0:T(8,128)(2,1)} %param.16), kind=kOutput, calls=%fused_computation.609 | convolution fusion | flops 16777216 | bytes 8781824 | tf_op jit(solution)/shard_map/dot_general | solution.py:157
  213.8 0.9 convolution_bitcast_fusion
  (409 shorter events, 30.4 us)
Async XLA Ops:
  0.6 28.7 %copy-start.137 = (s32[256,1]{0,1:T(1,128)S(1)}, s32[256,1]{0,1:T(1,128)}, u32[]{:S(2)}) copy-start(s32[256,1]{0,1:T(1,128)} %param.17) | copy-start | bytes 3076
  0.6 25.5 %copy-start.3 = (f32[63,64,128]{2,1,0:T(8,128)S(1)}, f32[63,64,128]{2,1,0:T(8,128)}, u32[]{:S(2)}) copy-start(f32[63,64,128]{2,1,0:T(8,128)} %param.13) | copy-start | bytes 6193156
  2.8 34.9 %collective-permute-start = (f32[2,64,1,128]{3,2,0,1:T(1,128)}, f32[2,64,1,128]{3,2,0,1:T(1,128)}, u32[]{:S(2)}, u32[]{:S(2)}) collective-permute-start(f32[2,64,1,128]{3,2,0,1:T(1,128)} %get-tuple-element.169), channel_id=1, source_target_pairs={{2,0},{4,2},{6,4},{8,6},{10,8},{12,10},{14,12},{3,1},{5,3},{7,5},{... | collective-permute-start | bytes 196616 | tf_op jit(solution)/shard_map/ppermute | solution.py:23
  4.0 33.7 %collective-permute-start.1 = (f32[2,64,1,128]{3,2,0,1:T(1,128)}, f32[2,64,1,128]{3,2,0,1:T(1,128)}, u32[]{:S(2)}, u32[]{:S(2)}) collective-permute-start(f32[2,64,1,128]{3,2,0,1:T(1,128)} %get-tuple-element.168), channel_id=1, source_target_pairs={{0,2},{2,4},{4,6},{6,8},{8,10},{10,12},{12,14},{1,3},{3,5},{5,7},{... | collective-permute-start | bytes 196616 | tf_op jit(solution)/shard_map/ppermute | solution.py:20
  14.7 92.2 %all-to-all-start = ((s32[32,8,1]{1,2,0:T(1,128)}), s32[32,8,1]{1,2,0:T(1,128)}, u32[]{:S(2)}, u32[]{:S(2)}) async-start(s32[32,8,1]{1,2,0:T(1,128)} %bitcast.356), calls=%async_computation | async-start | bytes 32768 | tf_op jit(solution)/shard_map/all_to_all | solution.py:136
  22.9 107.6 %copy-start.4 = (f32[1,64,128]{2,1,0:T(8,128)}, f32[1,64,128]{2,1,0:T(8,128)S(1)}, u32[]{:S(2)}) copy-start(f32[1,64,128]{2,1,0:T(8,128)S(1)} %get-tuple-element.83) | copy-start | bytes 98308
  23.0 107.6 %copy-start.6 = (f32[1,64,128]{2,1,0:T(8,128)}, f32[1,64,128]{2,1,0:T(8,128)S(1)}, u32[]{:S(2)}) copy-start(f32[1,64,128]{2,1,0:T(8,128)S(1)} %get-tuple-element.119) | copy-start | bytes 98308
  23.0 107.6 %copy-start.15 = (f32[1,64,128]{2,1,0:T(8,128)}, f32[1,64,128]{2,1,0:T(8,128)S(1)}, u32[]{:S(2)}) copy-start(f32[1,64,128]{2,1,0:T(8,128)S(1)} %get-tuple-element.103) | copy-start | bytes 98308
  23.0 107.6 %copy-start.17 = (f32[1,64,128]{2,1,0:T(8,128)}, f32[1,64,128]{2,1,0:T(8,128)S(1)}, u32[]{:S(2)}) copy-start(f32[1,64,128]{2,1,0:T(8,128)S(1)} %get-tuple-element.107) | copy-start | bytes 98308
  23.0 107.6 %copy-start.19 = (f32[1,64,128]{2,1,0:T(8,128)}, f32[1,64,128]{2,1,0:T(8,128)S(1)}, u32[]{:S(2)}) copy-start(f32[1,64,128]{2,1,0:T(8,128)S(1)} %get-tuple-element.111) | copy-start | bytes 98308
  23.0 107.6 %copy-start.21 = (f32[1,64,128]{2,1,0:T(8,128)}, f32[1,64,128]{2,1,0:T(8,128)S(1)}, u32[]{:S(2)}) copy-start(f32[1,64,128]{2,1,0:T(8,128)S(1)} %get-tuple-element.115) | copy-start | bytes 98308
  31.3 99.3 %copy-start.25 = (f32[64,128]{1,0:T(8,128)}, f32[64,128]{1,0:T(8,128)S(1)}, u32[]{:S(2)}) copy-start(f32[64,128]{1,0:T(8,128)S(1)} %get-tuple-element.271) | copy-start | bytes 98308
  31.3 99.3 %copy-start.27 = (f32[64,128]{1,0:T(8,128)}, f32[64,128]{1,0:T(8,128)S(1)}, u32[]{:S(2)}) copy-start(f32[64,128]{1,0:T(8,128)S(1)} %get-tuple-element.273) | copy-start | bytes 98308
  33.7 96.9 %copy-start.8 = (f32[64,128]{1,0:T(8,128)}, f32[64,128]{1,0:T(8,128)S(1)}, u32[]{:S(2)}) copy-start(f32[64,128]{1,0:T(8,128)S(1)} %get-tuple-element.243) | copy-start | bytes 98308
  33.7 97.0 %copy-start.10 = (f32[64,128]{1,0:T(8,128)}, f32[64,128]{1,0:T(8,128)S(1)}, u32[]{:S(2)}) copy-start(f32[64,128]{1,0:T(8,128)S(1)} %get-tuple-element.247) | copy-start | bytes 98308
  33.7 97.0 %copy-start.12 = (f32[64,128]{1,0:T(8,128)}, f32[64,128]{1,0:T(8,128)S(1)}, u32[]{:S(2)}) copy-start(f32[64,128]{1,0:T(8,128)S(1)} %get-tuple-element.249) | copy-start | bytes 98308
  47.9 11.5 %collective-permute-start.3 = (f32[2,64,66,1]{2,1,3,0:T(8,128)S(1)}, f32[2,64,66,1]{2,1,3,0:T(8,128)S(1)}, u32[]{:S(2)}, u32[]{:S(2)}) collective-permute-start(f32[2,64,66,1]{2,1,3,0:T(8,128)S(1)} %copy.545), channel_id=1, source_target_pairs={{0,1},{1,16},{16,17},{2,3},{3,18},{18,19},{4,5},{5,20},{20,21},{6,... | collective-permute-start | bytes 101384 | tf_op jit(solution)/shard_map/ppermute | solution.py:20
  53.2 9.2 %collective-permute-start.2 = (f32[2,64,66,1]{2,1,3,0:T(8,128)S(1)}, f32[2,64,66,1]{2,1,3,0:T(8,128)S(1)}, u32[]{:S(2)}, u32[]{:S(2)}) collective-permute-start(f32[2,64,66,1]{2,1,3,0:T(8,128)S(1)} %copy.543), channel_id=1, source_target_pairs={{1,0},{16,1},{17,16},{3,2},{18,3},{19,18},{5,4},{20,5},{21,20},{7,... | collective-permute-start | bytes 101384 | tf_op jit(solution)/shard_map/ppermute | solution.py:23
  79.8 6.2 %collective-permute-start.4 = (f32[2,64,1,128]{3,2,0,1:T(1,128)S(1)}, f32[2,64,1,128]{3,2,0,1:T(1,128)S(1)}, u32[]{:S(2)}, u32[]{:S(2)}) collective-permute-start(f32[2,64,1,128]{3,2,0,1:T(1,128)S(1)} %get-tuple-element.167), channel_id=1, source_target_pairs={{2,0},{4,2},{6,4},{8,6},{10,8},{12,10},{14,12},{3,1},{5,3},{7,5},{... | collective-permute-start | bytes 196616 | tf_op jit(solution)/shard_map/ppermute | solution.py:23
  81.1 6.8 %collective-permute-start.5 = (f32[2,64,1,128]{3,2,0,1:T(1,128)S(1)}, f32[2,64,1,128]{3,2,0,1:T(1,128)S(1)}, u32[]{:S(2)}, u32[]{:S(2)}) collective-permute-start(f32[2,64,1,128]{3,2,0,1:T(1,128)S(1)} %get-tuple-element.166), channel_id=1, source_target_pairs={{0,2},{2,4},{4,6},{6,8},{8,10},{10,12},{12,14},{1,3},{3,5},{5,7},{... | collective-permute-start | bytes 196616 | tf_op jit(solution)/shard_map/ppermute | solution.py:20
  97.2 12.4 %collective-permute-start.7 = (f32[2,64,66,1]{2,1,3,0:T(8,128)S(1)}, f32[2,64,66,1]{2,1,3,0:T(8,128)S(1)}, u32[]{:S(2)}, u32[]{:S(2)}) collective-permute-start(f32[2,64,66,1]{2,1,3,0:T(8,128)S(1)} %copy.551), channel_id=1, source_target_pairs={{0,1},{1,16},{16,17},{2,3},{3,18},{18,19},{4,5},{5,20},{20,21},{6,... | collective-permute-start | bytes 101384 | tf_op jit(solution)/shard_map/ppermute | solution.py:20
  103.1 9.5 %collective-permute-start.6 = (f32[2,64,66,1]{2,1,3,0:T(8,128)S(1)}, f32[2,64,66,1]{2,1,3,0:T(8,128)S(1)}, u32[]{:S(2)}, u32[]{:S(2)}) collective-permute-start(f32[2,64,66,1]{2,1,3,0:T(8,128)S(1)} %copy.549), channel_id=1, source_target_pairs={{1,0},{16,1},{17,16},{3,2},{18,3},{19,18},{5,4},{20,5},{21,20},{7,... | collective-permute-start | bytes 101384 | tf_op jit(solution)/shard_map/ppermute | solution.py:23
  115.7 15.0 %copy-start.33 = (f32[64,128]{1,0:T(8,128)S(1)}, f32[64,128]{1,0:T(8,128)}, u32[]{:S(2)}) copy-start(f32[64,128]{1,0:T(8,128)} %get-tuple-element.267) | copy-start | bytes 98308
  115.7 15.0 %copy-start.34 = (f32[64,128]{1,0:T(8,128)S(1)}, f32[64,128]{1,0:T(8,128)}, u32[]{:S(2)}) copy-start(f32[64,128]{1,0:T(8,128)} %get-tuple-element.251) | copy-start | bytes 98308
  115.7 15.0 %copy-start.35 = (f32[64,128]{1,0:T(8,128)S(1)}, f32[64,128]{1,0:T(8,128)}, u32[]{:S(2)}) copy-start(f32[64,128]{1,0:T(8,128)} %get-tuple-element.255) | copy-start | bytes 98308
  115.7 15.0 %copy-start.36 = (f32[64,128]{1,0:T(8,128)S(1)}, f32[64,128]{1,0:T(8,128)}, u32[]{:S(2)}) copy-start(f32[64,128]{1,0:T(8,128)} %get-tuple-element.257) | copy-start | bytes 98308
  115.8 15.0 %copy-start.37 = (f32[64,128]{1,0:T(8,128)S(1)}, f32[64,128]{1,0:T(8,128)}, u32[]{:S(2)}) copy-start(f32[64,128]{1,0:T(8,128)} %get-tuple-element.259) | copy-start | bytes 98308
  115.8 15.0 %copy-start.38 = (f32[64,128]{1,0:T(8,128)S(1)}, f32[64,128]{1,0:T(8,128)}, u32[]{:S(2)}) copy-start(f32[64,128]{1,0:T(8,128)} %slice_bitcast_fusion.34) | copy-start | bytes 98308
  115.8 15.0 %copy-start.47 = (f32[1,64,128]{2,1,0:T(8,128)S(1)}, f32[1,64,128]{2,1,0:T(8,128)}, u32[]{:S(2)}) copy-start(f32[1,64,128]{2,1,0:T(8,128)} %copy-done.46) | copy-start | bytes 98308
  115.8 15.0 %copy-start.49 = (f32[1,64,128]{2,1,0:T(8,128)S(1)}, f32[1,64,128]{2,1,0:T(8,128)}, u32[]{:S(2)}) copy-start(f32[1,64,128]{2,1,0:T(8,128)} %copy-done.48) | copy-start | bytes 98308
  115.8 15.0 %copy-start.52 = (f32[64,128]{1,0:T(8,128)S(1)}, f32[64,128]{1,0:T(8,128)}, u32[]{:S(2)}) copy-start(f32[64,128]{1,0:T(8,128)} %get-tuple-element.281) | copy-start | bytes 98308
  115.8 15.0 %copy-start.53 = (f32[64,128]{1,0:T(8,128)S(1)}, f32[64,128]{1,0:T(8,128)}, u32[]{:S(2)}) copy-start(f32[64,128]{1,0:T(8,128)} %get-tuple-element.283) | copy-start | bytes 98308
  115.8 15.0 %copy-start.54 = (f32[64,128]{1,0:T(8,128)S(1)}, f32[64,128]{1,0:T(8,128)}, u32[]{:S(2)}) copy-start(f32[64,128]{1,0:T(8,128)} %get-tuple-element.284) | copy-start | bytes 98308
  115.8 15.0 %copy-start.57 = (f32[64,128]{1,0:T(8,128)S(1)}, f32[64,128]{1,0:T(8,128)}, u32[]{:S(2)}) copy-start(f32[64,128]{1,0:T(8,128)} %get-tuple-element.172) | copy-start | bytes 98308
  152.6 15.5 %copy-start.65 = (f32[64,128]{1,0:T(8,128)S(1)}, f32[64,128]{1,0:T(8,128)}, u32[]{:S(2)}) copy-start(f32[64,128]{1,0:T(8,128)} %get-tuple-element.138) | copy-start | bytes 98308
  152.6 15.5 %copy-start.127 = (f32[2,64,128]{2,1,0:T(8,128)S(1)}, f32[2,64,128]{2,1,0:T(8,128)}, u32[]{:S(2)}) copy-start(f32[2,64,128]{2,1,0:T(8,128)} %get-tuple-element.70) | copy-start | bytes 196612
  152.6 16.7 %copy-start.68 = (f32[64,128]{1,0:T(8,128)S(1)}, f32[64,128]{1,0:T(8,128)}, u32[]{:S(2)}) copy-start(f32[64,128]{1,0:T(8,128)} %get-tuple-element.141) | copy-start | bytes 98308
  152.6 16.7 %copy-start.126 = (f32[2,64,128]{2,1,0:T(8,128)S(1)}, f32[2,64,128]{2,1,0:T(8,128)}, u32[]{:S(2)}) copy-start(f32[2,64,128]{2,1,0:T(8,128)} %get-tuple-element.69) | copy-start | bytes 196612
  152.7 18.0 %copy-start.40 = (f32[64,128]{1,0:T(8,128)S(1)}, f32[64,128]{1,0:T(8,128)}, u32[]{:S(2)}) copy-start(f32[64,128]{1,0:T(8,128)} %get-tuple-element.144) | copy-start | bytes 98308
  152.7 18.0 %copy-start.125 = (f32[2,64,128]{2,1,0:T(8,128)S(1)}, f32[2,64,128]{2,1,0:T(8,128)}, u32[]{:S(2)}) copy-start(f32[2,64,128]{2,1,0:T(8,128)} %get-tuple-element.68) | copy-start | bytes 196612
  152.8 40.2 %copy-start.138 = (s32[256]{0:T(256)S(1)}, s32[256]{0:T(256)}, u32[]{:S(2)}) copy-start(s32[256]{0:T(256)} %eq.107) | copy-start | bytes 3076
  154.5 39.2 %copy-start.131 = (s32[64,128]{1,0:T(8,128)S(1)}, s32[64,128]{1,0:T(8,128)}, u32[]{:S(2)}) copy-start(s32[64,128]{1,0:T(8,128)} %param.20) | copy-start | bytes 98308
  154.5 39.2 %copy-start.134 = (f32[64,128]{1,0:T(8,128)S(1)}, f32[64,128]{1,0:T(8,128)}, u32[]{:S(2)}) copy-start(f32[64,128]{1,0:T(8,128)} %param.21) | copy-start | bytes 98308
  154.5 39.2 %copy-start.135 = (f32[64,128]{1,0:T(8,128)S(1)}, f32[64,128]{1,0:T(8,128)}, u32[]{:S(2)}) copy-start(f32[64,128]{1,0:T(8,128)} %param.23) | copy-start | bytes 98308
  154.6 39.8 %copy-start.136 = (f32[64,128]{1,0:T(8,128)S(1)}, f32[64,128]{1,0:T(8,128)}, u32[]{:S(2)}) copy-start(f32[64,128]{1,0:T(8,128)} %param.22) | copy-start | bytes 98308
  154.6 43.9 %copy-start.115 = (f32[64,128]{1,0:T(8,128)S(1)}, f32[64,128]{1,0:T(8,128)}, u32[]{:S(2)}) copy-start(f32[64,128]{1,0:T(8,128)} %get-tuple-element.218) | copy-start | bytes 98308
  154.6 38.1 %all-to-all-start.1 = ((f32[32,8,1024]{2,1,0:T(8,128)}), f32[32,8,1024]{2,1,0:T(8,128)S(1)}, u32[]{:S(2)}, u32[]{:S(2)}) async-start(f32[32,8,1024]{2,1,0:T(8,128)} %fusion.13), calls=%async_computation.1 | async-start | bytes 2097152 | tf_op jit(solution)/shard_map/all_to_all | solution.py:135
  195.9 10.8 %all-to-all-start.2 = ((bf16[32,8,256]{2,1,0:T(8,128)(2,1)}), bf16[32,8,256]{2,1,0:T(8,128)(2,1)S(1)}, u32[]{:S(2)}, u32[]{:S(2)}) async-start(bf16[32,8,256]{2,1,0:T(8,128)(2,1)} %fusion.12), calls=%async_computation.2 | async-start | bytes 262144 | tf_op jit(solution)/shard_map/all_to_all | solution.py:153
  (108 other events, 753.4 us)
where the time goes:
time: 217 us; the launch traced here: 215 us
  other arithmetic  69.2 us (32%)
  local copies, waits for them, and re-layouts  57.4 us (26%)
  starting transfers between devices  40 us (18%)
  waiting for transfers between devices  28.3 us (13%)
  matrix products  16.7 us (8%)
  between operations  3.25 us (1%)
    add x2, other arithmetic, stencil(): return center + DIFFUSION * (beside_all - 4.0 * center)  27.2 us
    all_to_all x1, waiting for transfers between devices, local(): lax.all_to_all(outgoing, ('comp', 'gx', 'gy'), split_axis=0, concat_axis=...  20.8 us
    slice x4, local copies, waits for them, and re-layouts, with_halo(): lax.slice_in_dim(block, 0, width, axis=dim)  16.9 us
    ppermute x4, starting transfers between devices, with_halo(): lax.ppermute(lax.slice_in_dim(block, block.shape[dim] - width, None, axis...  15.4 us
    unnamed x33, other arithmetic  13.1 us
    mul x12, other arithmetic, column_pass(): solved.append(reduced[level] + coupling[level] / pivots[level] * solved[-1])  11.1 us
    unnamed x324, local copies, waits for them, and re-layouts  11.1 us
    all_to_all x1, starting transfers between devices, local(): lax.all_to_all(outgoing, ('comp', 'gx', 'gy'), split_axis=0, concat_axis=...  10.9 us
  transfers between devices with their start and end apart: 11, of which 4 were waited for; matrix products, arithmetic and copies ran while one was open for 41% of the time, Pallas kernels for 0%

commit v1 on v0

v1 whole, which is shorter than its diff:
```python
import functools

import jax
import jax.numpy as jnp
from jax import lax
from jax.experimental import pallas as pl
from jax.experimental.pallas import tpu as pltpu
from jax.sharding import PartitionSpec as P

F32 = jnp.float32
BF16 = jnp.bfloat16
ALL = ("comp", "gx", "gy")
NF = 8
SENT = 5
SURFACE_STEP = 0.5
MIX = 0.2
MIB = 1 << 20
BIG = 56 * MIB


def swaps(count, first):
    pairs = [(i, i + 1) for i in range(first, count - 1, 2)]
    return pairs + [(b, a) for a, b in pairs]


def grid_place():
    gx, n_gx = lax.axis_index("gx"), lax.axis_size("gx")
    c = lax.axis_index("comp") * lax.axis_size("gy") + lax.axis_index("gy")
    n_c = lax.axis_size("comp") * lax.axis_size("gy")
    there = lambda yes: jnp.where(yes, 1.0, 0.0).astype(F32)
    return gx % 2 == 0, c % 2 == 0, there(gx > 0), there(gx < n_gx - 1), there(c > 0), there(c < n_c - 1)


def rows_kernel(first, last, rows_a, rows_b):
    even_row = grid_place()[0]
    fields, levels, tile, lanes = first.shape
    for field in range(fields):
        at = slice(field * levels, (field + 1) * levels)
        for k in range(2):
            low, high = first[field, :, k, :], last[field, :, tile - 1 - k, :]
            to = slice(k * lanes, (k + 1) * lanes)
            rows_a[at, to] = jnp.where(even_row, high, low).astype(BF16)
            rows_b[at, to] = jnp.where(even_row, low, high).astype(BF16)


def pack_rows(air):
    fields, levels, rows, lanes = air.shape
    tile = 8
    out = jax.ShapeDtypeStruct((fields * levels, 2 * lanes), BF16)
    return pl.pallas_call(
        rows_kernel,
        grid=(1,),
        in_specs=[
            pl.BlockSpec((fields, levels, tile, lanes), lambda i: (0, 0, 0, 0)),
            pl.BlockSpec((fields, levels, tile, lanes), lambda i: (0, 0, rows // tile - 1, 0)),
        ],
        out_specs=[pl.BlockSpec(out.shape, lambda i: (0, 0))] * 2,
        out_shape=[out, out],
        compiler_params=pltpu.CompilerParams(vmem_limit_bytes=BIG),
        name="pack_rows",
    )(air, air)


def cols_kernel(air, own_left, own_right, left, right):
    step = pl.program_id(0)
    fields, chunk, rows, lanes = air.shape
    levels = chunk * pl.num_programs(0)
    pair = lax.broadcasted_iota(jnp.int32, (rows, lanes), 1) >> 1
    for field in range(fields):
        to_left, to_right = left[field], right[field]
        for sub in range(chunk):
            level = step * chunk + sub
            turned = pltpu.roll(air[field, sub], 2 * level, axis=1)
            to_left = jnp.where(pair == level, turned, to_left)
            to_right = jnp.where(pair == (level + levels - 1) % levels, turned, to_right)
        left[field] = to_left
        right[field] = to_right

    @pl.when(step == pl.num_programs(0) - 1)
    def _():
        for field in range(fields):
            own_left[field] = left[field]
            own_right[field] = pltpu.roll(right[field], 2, axis=1)


def pack_cols(air):
    fields, levels, rows, lanes = air.shape
    chunk = 8
    out = jax.ShapeDtypeStruct((fields, rows, lanes), F32)
    return pl.pallas_call(
        cols_kernel,
        grid=(levels // chunk,),
        in_specs=[pl.BlockSpec((fields, chunk, rows, lanes), lambda i: (0, i, 0, 0))],
        out_specs=[pl.BlockSpec(out.shape, lambda i: (0, 0, 0))] * 2,
        out_shape=[out, out],
        scratch_shapes=[pltpu.VMEM(out.shape, F32)] * 2,
        compiler_params=pltpu.CompilerParams(vmem_limit_bytes=BIG),
        cost_estimate=pl.CostEstimate(flops=4 * air.size, bytes_accessed=4 * air.size, transcendentals=0),
        name="pack_cols",
    )(air)


def with_row(strip, row, first):
    rows = strip.shape[0]
    index = lax.broadcasted_iota(jnp.int32, strip.shape, 0)
    if first:
        return jnp.where(index == 0, row, pltpu.roll(strip, 1, axis=0))
    return jnp.where(index == rows - 1, row, pltpu.roll(strip, rows - 1, axis=0))


def strips_kernel(got_a, got_b, own_left, own_right, to_g, to_x):
    even_col = grid_place()[1]
    fields, rows, lanes = own_left.shape
    top, _, low, _ = row_halo(got_a, got_b)
    levels = top.shape[0] // fields
    level = lax.broadcasted_iota(jnp.int32, (levels, lanes), 0)
    pair = lax.broadcasted_iota(jnp.int32, (levels, lanes), 1) >> 1
    spread = jnp.where(level == pair, 1.0, 0.0).astype(BF16)
    odd = (lax.broadcasted_iota(jnp.int32, (rows, lanes), 1) & 1) == 1
    for field in range(fields):
        at = slice(field * levels, (field + 1) * levels)
        above, below = [
            lax.dot_general(h[at].astype(BF16), spread, (((0,), (0,)), ((), ())), preferred_element_type=F32)
            for h in (top, low)
        ]
        left, right = own_left[field], own_right[field]
        edge = pltpu.roll(left, 1, axis=1)
        around = with_row(edge, 2.0 * above[0:1], True) + with_row(edge, 2.0 * below[0:1], False)
        west = jnp.where(odd, MIX * (edge + left + around), left)
        edge = pltpu.roll(right, lanes - 1, axis=1)
        around = with_row(edge, 2.0 * above[lanes - 1 :], True) + with_row(edge, 2.0 * below[lanes - 1 :], False)
        east = jnp.where(odd, right, MIX * (edge + right + around))
        to_g[field] = jnp.where(even_col, east, west).astype(BF16)
        to_x[field] = jnp.where(even_col, west, east).astype(BF16)


def make_strips(got_a, got_b, own_left, own_right):
    vmem = pl.BlockSpec(memory_space=pltpu.VMEM)
    out = jax.ShapeDtypeStruct(own_left.shape, BF16)
    return pl.pallas_call(
        strips_kernel,
        in_specs=[vmem] * 4,
        out_specs=[vmem] * 2,
        out_shape=[out, out],
        compiler_params=pltpu.CompilerParams(vmem_limit_bytes=BIG),
        name="strips",
    )(got_a, got_b, own_left, own_right)


def side_strips(field, got_g, got_x, own_left, own_right):
    _, even_col, _, _, has_left, has_right = grid_place()
    rows, lanes = got_g.shape[1], got_g.shape[2]
    from_g, from_x = got_g[field].astype(F32), got_x[field].astype(F32)
    west = jnp.where(even_col, from_x, from_g)
    east = jnp.where(even_col, from_g, from_x)
    next_west = pltpu.roll(west + MIX * own_left[field], 1, axis=1) * has_left
    next_east = pltpu.roll(east + MIX * own_right[field], lanes - 1, axis=1) * has_right
    odd = (lax.broadcasted_iota(jnp.int32, (rows, lanes), 1) & 1) == 1
    return jnp.where(odd, west, east), jnp.where(odd, next_west, next_east)


def row_halo(got_a, got_b):
    even_row = grid_place()[0]
    from_a, from_b = got_a[...].astype(F32), got_b[...].astype(F32)
    top = jnp.where(even_row, from_b, from_a)
    low = jnp.where(even_row, from_a, from_b)
    lanes = top.shape[1] // 2
    return top[:, :lanes], top[:, lanes:], low[:, :lanes], low[:, lanes:]


def sides_of_row(row):
    lanes = row.shape[1]
    lane = lax.broadcasted_iota(jnp.int32, row.shape, 1)
    from_left = jnp.where(lane == 0, 0.0, pltpu.roll(row, 1, axis=1))
    from_right = jnp.where(lane == lanes - 1, 0.0, pltpu.roll(row, lanes - 1, axis=1))
    return from_left + from_right


def substep(block, above, below, sides):
    lanes = block.shape[1]
    lane = lax.broadcasted_iota(jnp.int32, block.shape, 1)
    from_left = jnp.where(lane == 0, sides, pltpu.roll(block, 1, axis=1))
    from_right = jnp.where(lane == lanes - 1, sides, pltpu.roll(block, lanes - 1, axis=1))
    around = with_row(block, above, True) + with_row(block, below, False)
    return MIX * (block + around + (from_left + from_right))


def mixed_level(block, top1, top2, low1, low2, sides0, sides1):
    rows = block.shape[0]
    first, last = block[0:1], block[rows - 1 : rows]
    _, _, has_top, has_low, _, _ = grid_place()
    next_top = has_top * MIX * (top1 + top2 + first + sides_of_row(top1))
    next_low = has_low * MIX * (low1 + low2 + last + sides_of_row(low1))
    once = substep(block, top1, low1, sides0)
    return substep(once, next_top, next_low, sides1)


def forward_kernel(
    owner, block_row, block_column, air, forcing, surface_temp, got_a, got_b, got_g, got_x,
    own_left, own_right, weight, payload, slots, source,
    flux_rows, found, tags, counts, bound, levels, group,
):
    step = pl.program_id(0)
    blocks = weight.shape[0]
    rows, lanes = surface_temp.shape
    total = payload.shape[0] * payload.shape[1]

    @pl.when(step == 0)
    def _():
        halo = row_halo(got_a, got_b)
        lowest = []
        for field in range(2):
            sides0, sides1 = side_strips(field, got_g, got_x, own_left, own_right)
            at = field * levels
            lowest.append(
                mixed_level(
                    air[field, 0],
                    *[h[at : at + 1] for h in halo],
                    pltpu.roll(sides0, lanes - 1, axis=1),
                    pltpu.roll(sides1, lanes - 1, axis=1),
                )
            )
        u, v = forcing[0], forcing[1]
        ts = surface_temp[...]
        speed = jnp.sqrt(u * u + v * v + 1.0)
        fluxes = [
            speed * (ts - lowest[0]),
            speed * (0.5 * ts - lowest[1]),
            speed * u,
            speed * v,
            forcing[2],
            forcing[3] - 0.3 * ts,
            forcing[4],
            forcing[5],
        ]
        source[0] = fluxes[0]
        source[1] = fluxes[1]
        for field in range(NF):
            flux_rows[pl.ds(field, rows, stride=NF), :] = fluxes[field]
        tags[...] = jnp.full_like(tags, -1.0)
        if total > blocks * pl.num_programs(0):
            found[...] = jnp.zeros_like(found)

        def clear(i, _):
            counts[i] = 0
            return 0

        lax.fori_loop(0, payload.shape[0], clear, 0)

    def some(g, _):
        outs = []
        for k in range(group):
            n = g * group + k
            at = step * blocks + n
            picked = flux_rows[pl.ds(pl.multiple_of(block_column[at] * NF, NF), NF), :]
            out = lax.dot_general(
                picked.astype(BF16), weight[n], (((1,), (1,)), ((), ())), preferred_element_type=F32
            )
            outs.append((at, out))
        for at, out in outs:
            to = owner[at]
            rank = counts[to]
            counts[to] = rank + 1
            slot = to * bound + rank
            slots[at] = slot
            found[pl.ds(pl.multiple_of(slot * NF, NF), NF), :] = out
            tags[pl.ds(slot, 1), :] = jnp.full((1, lanes), block_row[at], jnp.int32).astype(F32)
        return 0

    lax.fori_loop(0, blocks // group, some, 0)

    @pl.when(step == pl.num_programs(0) - 1)
    def _():
        f = [found[pl.ds(k, total, stride=NF), :] for k in range(NF)]
        heat = (f[0] + f[1]) + (f[4] + f[5])
        heat_hi = heat.astype(BF16).astype(F32)
        lane = lax.broadcasted_iota(jnp.int32, (total, lanes), 1)
        heat_lo = jnp.where(lane == 0, tags[...], heat - heat_hi)
        shape = payload.shape[:2] + (lanes,)
        for k, part in enumerate((heat_hi, heat_lo, f[2], f[3], f[6] - f[7])):
            payload[:, :, k * lanes : (k + 1) * lanes] = part.reshape(shape).astype(BF16)


def forward(owner, block_row, block_column, air, forcing, surface_temp, halo, own, weight, devices, bound):
    got_a, got_b, got_g, got_x = halo
    _, levels, rows, lanes = air.shape
    nonzeros = weight.shape[0]
    chunk = 32
    whole = lambda x: pl.BlockSpec(x.shape, lambda i: (0,) * x.ndim)
    smem = pl.BlockSpec(memory_space=pltpu.SMEM)
    args = (forcing, surface_temp, got_a, got_b, got_g, got_x, *own)
    total = devices * bound
    return pl.pallas_call(
        functools.partial(forward_kernel, bound=bound, levels=levels, group=8),
        grid=(nonzeros // chunk,),
        in_specs=[smem, smem, smem]
        + [pl.BlockSpec((2, 1, rows, lanes), lambda i: (0, 0, 0, 0))]
        + [whole(x) for x in args]
        + [pl.BlockSpec((chunk, lanes, lanes), lambda i: (i, 0, 0))],
        out_specs=[
            pl.BlockSpec((devices, bound, SENT * lanes), lambda i: (0, 0, 0)),
            smem,
            pl.BlockSpec((2, rows, lanes), lambda i: (0, 0, 0)),
        ],
        out_shape=[
            jax.ShapeDtypeStruct((devices, bound, SENT * lanes), BF16),
            jax.ShapeDtypeStruct((nonzeros,), jnp.int32),
            jax.ShapeDtypeStruct((2, rows, lanes), F32),
        ],
        scratch_shapes=[
            pltpu.VMEM((rows * NF, lanes), F32),
            pltpu.VMEM((total * NF, lanes), F32),
            pltpu.VMEM((total, lanes), F32),
            pltpu.SMEM((devices,), jnp.int32),
        ],
        compiler_params=pltpu.CompilerParams(vmem_limit_bytes=BIG),
        name="forward_blocks",
    )(owner, block_row, block_column, air, *args, weight)


def column_kernel(
    air, coupling, got_a, got_b, got_g, got_x, own_left, own_right,
    source, air_new, ratio, halo_rows, strips,
):
    _, levels, rows, lanes = air.shape
    for k, h in enumerate(row_halo(got_a, got_b)):
        halo_rows[k] = h
    for field in range(2):
        sides0, sides1 = side_strips(field, got_g, got_x, own_left, own_right)
        strips[field, 0] = sides0
        strips[field, 1] = sides1

    def mixed(field, level):
        at = pl.ds(field * levels + level, 1)
        shift = (2 * lanes - 1 - 2 * level) % lanes
        return mixed_level(
            air[field, level],
            *[halo_rows[k, at, :] for k in range(4)],
            pltpu.roll(strips[field, 0], shift, axis=1),
            pltpu.roll(strips[field, 1], shift, axis=1),
        )

    above = coupling[0]
    inverse = 1.0 / (1.0 + above)
    ratio[0] = above * inverse
    for field in range(2):
        air_new[field, 0] = (mixed(field, 0) + SURFACE_STEP * source[field]) * inverse

    def up(level, carry, top=False):
        below = coupling[level - 1]
        diagonal = 1.0 + below
        if not top:
            above = coupling[level]
            diagonal = diagonal + above
        inverse = 1.0 / (diagonal - below * ratio[level - 1])
        if not top:
            ratio[level] = above * inverse
        for field in range(2):
            air_new[field, level] = (mixed(field, level) + below * air_new[field, level - 1]) * inverse
        return carry

    lax.fori_loop(1, levels - 1, up, 0)
    up(levels - 1, 0, True)

    def down(i, carry):
        level = levels - 2 - i
        for field in range(2):
            air_new[field, level] = air_new[field, level] + ratio[level] * air_new[field, level + 1]
        return carry

    lax.fori_loop(0, levels - 1, down, 0)


def columns(air, coupling, halo, own, source):
    got_a, got_b, got_g, got_x = halo
    fields, levels, rows, lanes = air.shape
    args = (air, coupling, got_a, got_b, got_g, got_x, *own, source)
    vmem = pl.BlockSpec(memory_space=pltpu.VMEM)
    return pl.pallas_call(
        column_kernel,
        in_specs=[vmem] * len(args),
        out_specs=vmem,
        out_shape=jax.ShapeDtypeStruct(air.shape, F32),
        scratch_shapes=[
            pltpu.VMEM((levels - 1, rows, lanes), F32),
            pltpu.VMEM((4, fields * levels, lanes), F32),
            pltpu.VMEM((fields, 2, rows, lanes), F32),
        ],
        compiler_params=pltpu.CompilerParams(vmem_limit_bytes=BIG),
        cost_estimate=pl.CostEstimate(flops=40 * air.size, bytes_accessed=11 * air.size, transcendentals=0),
        name="columns",
    )(*args)


def ocean_kernel(arrived, land_mask, ocean_temp, ocean_ice, layer_depth, temp_new, ice_new, replies):
    blocks, lanes = ocean_temp.shape
    total = arrived.shape[0] * arrived.shape[1]
    parts = [
        arrived[:, :, k * lanes : (k + 1) * lanes].astype(F32).reshape(total, lanes) for k in range(SENT)
    ]
    lane = lax.broadcasted_iota(jnp.int32, (total, lanes), 1)
    tag = parts[1][:, 0:1].astype(jnp.int32)
    parts[1] = jnp.where(lane == 0, 0.0, parts[1])
    slot_of = (tag == lax.broadcasted_iota(jnp.int32, (total, blocks), 1)).astype(F32).astype(BF16)
    sums = [
        lax.dot_general(slot_of, p.astype(BF16), (((0,), (0,)), ((), ())), preferred_element_type=F32)
        for p in parts
    ]
    heat = sums[0] + sums[1]
    stress = sums[2] * sums[2] + sums[3] * sums[3]
    wet = land_mask[...].astype(F32)
    temp = ocean_temp[...]
    temp = temp + wet * (0.3 * heat / layer_depth[...] - 0.01 * stress * temp)
    ice = jnp.clip(ocean_ice[...] - wet * 0.05 * (heat + sums[4]), 0.0, 1.0)
    temp_new[...] = temp
    ice_new[...] = ice
    shape = replies.shape[:2] + (lanes,)
    for k, field in enumerate((temp, ice)):
        answer = jnp.dot(slot_of, field.astype(BF16), preferred_element_type=F32)
        replies[:, :, k * lanes : (k + 1) * lanes] = answer.reshape(shape).astype(BF16)


def ocean(arrived, land_mask, ocean_temp, ocean_ice, layer_depth):
    devices, bound, _ = arrived.shape
    blocks, lanes = ocean_temp.shape
    vmem = pl.BlockSpec(memory_space=pltpu.VMEM)
    return pl.pallas_call(
        ocean_kernel,
        in_specs=[vmem] * 5,
        out_specs=[vmem] * 3,
        out_shape=[
            jax.ShapeDtypeStruct((blocks, lanes), F32),
            jax.ShapeDtypeStruct((blocks, lanes), F32),
            jax.ShapeDtypeStruct((devices, bound, 2 * lanes), BF16),
        ],
        compiler_params=pltpu.CompilerParams(vmem_limit_bytes=BIG),
        name="ocean",
    )(arrived, land_mask, ocean_temp, ocean_ice, layer_depth)


def backward_kernel(slots, block_column, returned, weight, seen, pairs, sums, group):
    step = pl.program_id(0)
    blocks, lanes = weight.shape[0], weight.shape[1]
    total = returned.shape[0] * returned.shape[1]
    rows = seen.shape[1]

    @pl.when(step == 0)
    def _():
        pairs[...] = jnp.zeros_like(pairs)
        sums[...] = jnp.zeros_like(sums)
        for k in range(2):
            part = returned[:, :, k * lanes : (k + 1) * lanes].astype(F32).reshape(total, lanes)
            pairs[pl.ds(k, total, stride=8), :] = part

    def some(g, _):
        outs = []
        for k in range(group):
            n = g * group + k
            at = step * blocks + n
            pair = pairs[pl.ds(pl.multiple_of(slots[at] * 8, 8), 8), :]
            outs.append((at, jnp.dot(pair.astype(BF16), weight[n], preferred_element_type=F32)))
        for at, out in outs:
            place = pl.ds(pl.multiple_of(block_column[at] * 8, 8), 8)
            sums[place, :] += out
        return 0

    lax.fori_loop(0, blocks // group, some, 0)

    @pl.when(step == pl.num_programs(0) - 1)
    def _():
        for k in range(2):
            seen[k] = sums[pl.ds(k, rows, stride=8), :]


def backward(slots, block_column, returned, weight, rows):
    devices, bound, _ = returned.shape
    nonzeros, lanes, _ = weight.shape
    chunk = 32
    smem = pl.BlockSpec(memory_space=pltpu.SMEM)
    return pl.pallas_call(
        functools.partial(backward_kernel, group=8),
        grid=(nonzeros // chunk,),
        in_specs=[
            smem,
            smem,
            pl.BlockSpec((devices, bound, 2 * lanes), lambda i: (0, 0, 0)),
            pl.BlockSpec((chunk, lanes, lanes), lambda i: (i, 0, 0)),
        ],
        out_specs=pl.BlockSpec((2, rows, lanes), lambda i: (0, 0, 0)),
        out_shape=jax.ShapeDtypeStruct((2, rows, lanes), F32),
        scratch_shapes=[
            pltpu.VMEM((devices * bound * 8, lanes), F32),
            pltpu.VMEM((rows * 8, lanes), F32),
        ],
        compiler_params=pltpu.CompilerParams(vmem_limit_bytes=BIG),
        name="backward_blocks",
    )(slots, block_column, returned, weight)


def local(
    air_state,
    coupling,
    forcing,
    surface_temp,
    remap_weight,
    block_owner,
    block_row,
    block_column,
    land_mask,
    ocean_temp,
    ocean_ice,
    layer_depth,
):
    devices = lax.axis_size("comp") * lax.axis_size("gx") * lax.axis_size("gy")
    nonzeros = remap_weight.shape[0]
    bound = max(4, (nonzeros + devices - 1) // devices)
    n_gx = lax.axis_size("gx")
    n_c = lax.axis_size("comp") * lax.axis_size("gy")
    rows_a, rows_b = pack_rows(air_state)
    got_a = lax.ppermute(rows_a, "gx", swaps(n_gx, 0))
    got_b = lax.ppermute(rows_b, "gx", swaps(n_gx, 1))
    own = pack_cols(air_state)
    to_g, to_x = make_strips(got_a, got_b, *own)
    got_x = lax.ppermute(to_x, ("comp", "gy"), swaps(n_c, 1))
    got_g = lax.ppermute(to_g, ("comp", "gy"), swaps(n_c, 0))
    halo = (got_a, got_b, got_g, got_x)
    payload, slots, source = forward(
        block_owner[:, 0], block_row, block_column, air_state, forcing, surface_temp, halo, own,
        remap_weight, devices, bound,
    )
    arrived = lax.all_to_all(payload, ALL, split_axis=0, concat_axis=0, tiled=True)
    air_new = columns(air_state, coupling, halo, own, source)
    ocean_temp_new, ocean_ice_new, replies = ocean(
        arrived, land_mask, ocean_temp, ocean_ice, layer_depth
    )
    returned = lax.all_to_all(replies, ALL, split_axis=0, concat_axis=0, tiled=True)
    surface_seen = backward(slots, block_column, returned, remap_weight, surface_temp.shape[0])
    return (air_new, surface_seen, ocean_temp_new, ocean_ice_new)


def solution(mesh):
    in_specs = (
        P(None, None, "gx", ("comp", "gy")),
        P(None, "gx", ("comp", "gy")),
        P(None, "gx", ("comp", "gy")),
        P("gx", ("comp", "gy")),
        P(ALL, None, None),
        P(ALL, None),
        P(ALL),
        P(ALL),
        P(ALL, None),
        P(ALL, None),
        P(ALL, None),
        P(ALL, None),
    )
    out_specs = (
        P(None, None, "gx", ("comp", "gy")),
        P(None, "gx", ("comp", "gy")),
        P(ALL, None),
        P(ALL, None),
    )
    return jax.shard_map(local, mesh=mesh, in_specs=in_specs, out_specs=out_specs, check_vma=False)
```

time: 217 us -> 88.7 us (0.41)
  other arithmetic: 69.2 us -> 0 us
  local copies, waits for them, and re-layouts: 57.4 us -> 1.91 us
  Pallas kernels: 0 us -> 54.3 us
  starting transfers between devices: 40 us -> 6.82 us
  waiting for transfers between devices: 28.3 us -> 0.77 us
  blocking collectives: 0 us -> 23.4 us
  matrix products: 16.7 us -> 0 us
  between operations: 3.25 us -> 0.68 us
    pallas_call x0 -> x7, Pallas kernels: none -> 54.3 us  [the longest x1 20.5 us: columns(): pl.pallas_call(column_kernel, in_specs=[vmem] * len(args), out_specs=vmem...]
    slice x11 -> x0, local copies, waits for them, and re-layouts: 27.4 us -> none  [the longest x4 16.9 us: with_halo(): lax.slice_in_dim(block, 0, width, axis=dim)]
    add x2 -> x0, other arithmetic: 27.2 us -> none  [stencil(): return center + DIFFUSION * (beside_all - 4.0 * center)]
    all_to_all x3 -> x1, waiting for transfers between devices: 26 us -> 0.01 us  [local(): lax.all_to_all(replies, ALL, split_axis=0, concat_axis=0, tiled=True)]
    all_to_all x0 -> x1, blocking collectives: none -> 23.4 us  [local(): lax.all_to_all(payload, ALL, split_axis=0, concat_axis=0, tiled=True)]
    all_to_all x3 -> x1, starting transfers between devices: 19.3 us -> 2.57 us  [local(): lax.all_to_all(replies, ALL, split_axis=0, concat_axis=0, tiled=True)]
    dot_general x7 -> x0, matrix products: 16.7 us -> none  [the longest x1 6.71 us: local(): lax.dot_general(picked, remap_weight, (((2,), (2,)), ((0,), (0,))), prefe...]
    ppermute x8 -> x4, starting transfers between devices: 20.8 us -> 4.25 us  [the longest x1 2.94 us: local(): got_a = lax.ppermute(rows_a, 'gx', swaps(n_gx, 0))]
  transfers between devices with their start and end apart: 11 -> 5, of which waited for: 4 -> 1; matrix products, arithmetic and copies ran while one was open for 41% -> 0% of each run, Pallas kernels for 0% -> 30%
where the time goes in v1:
time: 88.7 us; the launch traced here: 87.9 us
  Pallas kernels  54.3 us (61%)
  blocking collectives  23.4 us (26%)
  starting transfers between devices  6.82 us (8%)
  local copies, waits for them, and re-layouts  1.91 us (2%)
    all_to_all x1, blocking collectives, local(): lax.all_to_all(payload, ALL, split_axis=0, concat_axis=0, tiled=True)  23.4 us
    pallas_call x1, Pallas kernels, columns(): pl.pallas_call(column_kernel, in_specs=[vmem] * len(args), out_specs=vmem...  20.5 us
    pallas_call x1, Pallas kernels, forward(): pl.pallas_call(functools.partial(forward_kernel, bound=bound, levels=leve...  11.8 us
    pallas_call x1, Pallas kernels, backward(): pl.pallas_call(functools.partial(backward_kernel, group=8), grid=(nonzero...  9.76 us
    pallas_call x1, Pallas kernels, pack_cols(): pl.pallas_call(cols_kernel, grid=(levels // chunk,), in_specs=[pl.BlockSp...  6.11 us
    ppermute x1, starting transfers between devices, local(): got_a = lax.ppermute(rows_a, 'gx', swaps(n_gx, 0))  2.94 us
    all_to_all x1, starting transfers between devices, local(): lax.all_to_all(replies, ALL, split_axis=0, concat_axis=0, tiled=True)  2.57 us
    pallas_call x1, Pallas kernels, pack_rows(): pl.pallas_call(rows_kernel, grid=(1,), in_specs=[pl.BlockSpec((fields, le...  2.19 us
  transfers between devices with their start and end apart: 5, of which 1 were waited for; matrix products, arithmetic and copies ran while one was open for 0% of the time, Pallas kernels for 30%

profile of v1, /device:TPU:0, one launch (start us, length us, event | category | flops | bytes accessed | tf_op | source)
XLA Modules:
  0.0 87.9 jit_solution(10806897530865734497)
XLA Ops:
  0.6 2.2 %pack_rows.1 = (bf16[128,256]{1,0:T(8,128)(2,1)}, bf16[128,256]{1,0:T(8,128)(2,1)}) custom-call(f32[2,64,64,128]{3,2,1,0:T(8,128)} %air.5, f32[2,64,64,128]{3,2,1,0:T(8,128)} %air.5), custom_call_target="tpu_custom_call" | custom-call | tf_op jit(solution)/shard_map/pack_rows/pallas_call | solution.py:50
  2.8 2.9 %collective-permute-start = (bf16[128,256]{1,0:T(8,128)(2,1)}, bf16[128,256]{1,0:T(8,128)(2,1)S(1)}, u32[]{:S(2)}, u32[]{:S(2)}) collective-permute-start(bf16[128,256]{1,0:T(8,128)(2,1)} %get-tuple-element.16), channel_id=1, source_target_pairs={{0,2},{4,6},{8,10},{12,14},{2,0},{6,4},{10,8},{14,12},{1,3},{5,7},... | collective-permute-start | bytes 196616 | tf_op jit(solution)/shard_map/ppermute | solution.py:520
  5.8 0.7 collective-permute-start.1
  6.4 6.1 %pack_cols.1 = (f32[2,64,128]{2,1,0:T(8,128)}, f32[2,64,128]{2,1,0:T(8,128)}) custom-call(f32[2,64,64,128]{3,2,1,0:T(8,128)} %air.5), custom_call_target="tpu_custom_call" | custom-call | flops 4194304 | bytes 4194304 | tf_op jit(solution)/shard_map/pack_cols/pallas_call | solution.py:90
  12.5 0.0 collective-permute-done.got_a
  12.5 0.0 copy-start
  12.5 0.0 collective-permute-done.1.got_b
  12.5 0.0 copy-start.1
  12.6 0.6 copy-done
  13.2 0.0 copy-done.1
  13.2 1.8 %strips.1 = (bf16[2,64,128]{2,1,0:T(8,128)(2,1)}, bf16[2,64,128]{2,1,0:T(8,128)(2,1)}) custom-call(bf16[128,256]{1,0:T(8,128)(2,1)} %copy-done, bf16[128,256]{1,0:T(8,128)(2,1)} %copy-done.1, f32[2,64,128]{2,1,0:T(8,128)} %get-tuple-element.18.own_left, f32[2,64,128]{2,1,0:T(8,128)} %get-tuple-element.19.own_right), custom_call_target="tpu_custom_call" | custom-call | tf_op jit(solution)/shard_map/strips/pallas_call | solution.py:140
  15.0 0.0 collective-permute-start.2
  15.0 0.7 collective-permute-start.3
  15.6 0.8 collective-permute-done.2.got_g
  16.4 0.0 copy-start.3
  16.4 0.0 collective-permute-done.3.got_x
  16.4 0.0 copy-start.4
  16.4 0.6 copy-done.3
  17.0 0.0 copy-done.4
  17.0 11.8 %forward_blocks.1 = (bf16[32,8,640]{2,1,0:T(8,128)(2,1)}, s32[256]{0:T(256)}, f32[2,64,128]{2,1,0:T(8,128)}) custom-call(s32[256]{0:T(256)} %bitcast.1, s32[256]{0:T(256)} %block_row.1, s32[256]{0:T(256)} %block_column.3, f32[2,64,64,128]{3,2,1,0:T(8,128)} %air.5, f32[6,64,128]{2,1,0:T(8,128)} %forcing.1, f32[64,128]{1,0:T(8,128)} %surface_temp.1, ...), custom_call_target="tpu_custom_call" | custom-call | tf_op jit(solution)/shard_map/forward_blocks/pallas_call | solution.py:293
  28.9 23.4 %all_to_all.10.arrived = bf16[32,8,640]{2,1,0:T(8,128)(2,1)} all-to-all(bf16[32,8,640]{2,1,0:T(8,128)(2,1)} %get-tuple-element.24), channel_id=1, replica_groups=mesh['comp'=2,'gx'=8,'gy'=2] {'comp','gx','gy'}, dimensions={0} | all-to-all | bytes 655360 | tf_op jit(solution)/shard_map/all_to_all | solution.py:531
  52.3 2.1 %ocean.1 = (f32[64,128]{1,0:T(8,128)}, f32[64,128]{1,0:T(8,128)}, bf16[32,8,256]{2,1,0:T(8,128)(2,1)}) custom-call(bf16[32,8,640]{2,1,0:T(8,128)(2,1)} %all_to_all.10.arrived, s32[64,128]{1,0:T(8,128)} %land_mask.1, f32[64,128]{1,0:T(8,128)} %ocean_temp.1, f32[64,128]{1,0:T(8,128)} %ocean_ice.1, f32[64,128]{1,0:T(8,128)} %layer_depth.1), custom_call_target="tpu_custom_call" | custom-call | tf_op jit(solution)/shard_map/ocean/pallas_call | solution.py:427
  54.5 2.6 %all-to-all-start.1 = ((bf16[32,8,256]{2,1,0:T(8,128)(2,1)}), bf16[32,8,256]{2,1,0:T(8,128)(2,1)S(1)}, u32[]{:S(2)}, u32[]{:S(2)}) async-start(bf16[32,8,256]{2,1,0:T(8,128)(2,1)} %get-tuple-element.25), calls=%async_computation.1 | async-start | bytes 262144 | tf_op jit(solution)/shard_map/all_to_all | solution.py:536
  57.0 20.5 %columns.1 = f32[2,64,64,128]{3,2,1,0:T(8,128)} custom-call(f32[2,64,64,128]{3,2,1,0:T(8,128)} %air.5, f32[63,64,128]{2,1,0:T(8,128)} %coupling.1, bf16[128,256]{1,0:T(8,128)(2,1)} %copy-done, bf16[128,256]{1,0:T(8,128)(2,1)} %copy-done.1, bf16[2,64,128]{2,1,0:T(8,128)(2,1)} %copy-done.3, bf16[2,64,128]{2,1,0:T(8,128)(2,1)} %copy-done.4, ...), custom_call_target="tpu_custom_call" | custom-call | flops 41943040 | bytes 11534336 | tf_op jit(solution)/shard_map/columns/pallas_call | solution.py:379
  77.5 0.0 all-to-all-done.1.returned
  77.5 0.0 copy-start.2
  77.5 0.7 copy-done.2
  78.2 9.8 %backward_blocks.1 = f32[2,64,128]{2,1,0:T(8,128)} custom-call(s32[256]{0:T(256)} %get-tuple-element.23.slots, s32[256]{0:T(256)} %block_column.3, bf16[32,8,256]{2,1,0:T(8,128)(2,1)} %copy-done.2, bf16[256,128,128]{2,1,0:T(8,128)(2,1)} %weight.3), custom_call_target="tpu_custom_call" | custom-call | tf_op jit(solution)/shard_map/backward_blocks/pallas_call | solution.py:480
Async XLA Ops:
  2.8 9.7 %collective-permute-start = (bf16[128,256]{1,0:T(8,128)(2,1)}, bf16[128,256]{1,0:T(8,128)(2,1)S(1)}, u32[]{:S(2)}, u32[]{:S(2)}) collective-permute-start(bf16[128,256]{1,0:T(8,128)(2,1)} %get-tuple-element.16), channel_id=1, source_target_pairs={{0,2},{4,6},{8,10},{12,14},{2,0},{6,4},{10,8},{14,12},{1,3},{5,7},... | collective-permute-start | bytes 196616 | tf_op jit(solution)/shard_map/ppermute | solution.py:520
  5.8 6.8 %collective-permute-start.1 = (bf16[128,256]{1,0:T(8,128)(2,1)}, bf16[128,256]{1,0:T(8,128)(2,1)S(1)}, u32[]{:S(2)}, u32[]{:S(2)}) collective-permute-start(bf16[128,256]{1,0:T(8,128)(2,1)} %get-tuple-element.17), channel_id=1, source_target_pairs={{2,4},{6,8},{10,12},{4,2},{8,6},{12,10},{3,5},{7,9},{11,13},{5,3},... | collective-permute-start | bytes 196616 | tf_op jit(solution)/shard_map/ppermute | solution.py:521
  12.5 0.6 copy-start
  12.5 0.6 copy-start.1
  15.0 1.4 %collective-permute-start.2 = (bf16[2,64,128]{2,1,0:T(8,128)(2,1)}, bf16[2,64,128]{2,1,0:T(8,128)(2,1)S(1)}, u32[]{:S(2)}, u32[]{:S(2)}) collective-permute-start(bf16[2,64,128]{2,1,0:T(8,128)(2,1)} %get-tuple-element.20), channel_id=1, source_target_pairs={{0,1},{16,17},{1,0},{17,16},{2,3},{18,19},{3,2},{19,18},{4,5},{20,... | collective-permute-start | bytes 98312 | tf_op jit(solution)/shard_map/ppermute | solution.py:525
  15.0 1.4 %collective-permute-start.3 = (bf16[2,64,128]{2,1,0:T(8,128)(2,1)}, bf16[2,64,128]{2,1,0:T(8,128)(2,1)S(1)}, u32[]{:S(2)}, u32[]{:S(2)}) collective-permute-start(bf16[2,64,128]{2,1,0:T(8,128)(2,1)} %get-tuple-element.21), channel_id=1, source_target_pairs={{1,16},{16,1},{3,18},{18,3},{5,20},{20,5},{7,22},{22,7},{9,24},{24... | collective-permute-start | bytes 98312 | tf_op jit(solution)/shard_map/ppermute | solution.py:524
  16.4 0.6 copy-start.3
  16.4 0.6 copy-start.4
  54.5 23.0 %all-to-all-start.1 = ((bf16[32,8,256]{2,1,0:T(8,128)(2,1)}), bf16[32,8,256]{2,1,0:T(8,128)(2,1)S(1)}, u32[]{:S(2)}, u32[]{:S(2)}) async-start(bf16[32,8,256]{2,1,0:T(8,128)(2,1)} %get-tuple-element.25), calls=%async_computation.1 | async-start | bytes 262144 | tf_op jit(solution)/shard_map/all_to_all | solution.py:536
  77.5 0.7 copy-start.2

commit v2 on v1

v2 whole, which is shorter than its diff:
```python
import functools

import jax
import jax.numpy as jnp
from jax import lax
from jax.experimental import pallas as pl
from jax.experimental.pallas import tpu as pltpu
from jax.sharding import PartitionSpec as P

F32 = jnp.float32
BF16 = jnp.bfloat16
ALL = ("comp", "gx", "gy")
NF = 8
SENT = 5
SURFACE_STEP = 0.5
MIX = 0.2
MIB = 1 << 20
BIG = 56 * MIB
PARTS = 8
STEP = 8
GROUP = 4


def row_swaps(first):
    n_gx, n_gy = lax.axis_size("gx"), lax.axis_size("gy")
    pairs = []
    for comp in range(lax.axis_size("comp")):
        for gx in range(n_gx):
            for gy in range(n_gy):
                other = gx + 1 if (gx - first) % 2 == 0 else gx - 1
                to, core = (other, gy) if 0 <= other < n_gx else (gx, gy ^ 1)
                pairs.append(((comp * n_gx + gx) * n_gy + gy, (comp * n_gx + to) * n_gy + core))
    return pairs


def col_swaps(first):
    count = lax.axis_size("comp") * lax.axis_size("gy")
    return [(i, (i + 1 if (i - first) % 2 == 0 else i - 1) % count) for i in range(count)]


def grid_place():
    gx, n_gx = lax.axis_index("gx"), lax.axis_size("gx")
    c = lax.axis_index("comp") * lax.axis_size("gy") + lax.axis_index("gy")
    n_c = lax.axis_size("comp") * lax.axis_size("gy")
    there = lambda yes: jnp.where(yes, 1.0, 0.0).astype(F32)
    return gx % 2 == 0, c % 2 == 0, there(gx > 0), there(gx < n_gx - 1), there(c > 0), there(c < n_c - 1)


def rows_kernel(air, rows_a, rows_b, first, last, sem):
    even_row = grid_place()[0]
    count, tile, lanes = first.shape
    rows = air.shape[1]
    copies = [
        pltpu.make_async_copy(air.at[:, pl.ds(0, tile)], first, sem.at[0]),
        pltpu.make_async_copy(air.at[:, pl.ds(rows - tile, tile)], last, sem.at[1]),
    ]
    for c in copies:
        c.start()
    for c in copies:
        c.wait()
    first, last = [x.reshape(count * tile, lanes) for x in (first, last)]
    for k in range(2):
        low, high = first[pl.ds(k, count, stride=tile), :], last[pl.ds(tile - 1 - k, count, stride=tile), :]
        to = slice(k * lanes, (k + 1) * lanes)
        rows_a[:, to] = jnp.where(even_row, high, low).astype(BF16)
        rows_b[:, to] = jnp.where(even_row, low, high).astype(BF16)


def pack_rows(air):
    fields, levels, rows, lanes = air.shape
    out = jax.ShapeDtypeStruct((fields * levels, 2 * lanes), BF16)
    edge = pltpu.VMEM((fields * levels, 8, lanes), F32)
    return pl.pallas_call(
        rows_kernel,
        in_specs=[pl.BlockSpec(memory_space=pl.ANY)],
        out_specs=[pl.BlockSpec(memory_space=pltpu.VMEM)] * 2,
        out_shape=[out, out],
        scratch_shapes=[edge, edge, pltpu.SemaphoreType.DMA((2,))],
        compiler_params=pltpu.CompilerParams(vmem_limit_bytes=BIG),
        name="pack_rows",
    )(air.reshape(fields * levels, rows, lanes))


def cols_kernel(air, own_left, own_right, held, sem, chunk):
    fields, levels, rows, lanes = air.shape
    copies = []
    for i in range(levels // chunk):
        part = pl.ds(i * chunk, chunk)
        copies.append(pltpu.make_async_copy(air.at[:, part], held.at[:, part], sem.at[i]))
        copies[i].start()
    pair = lax.broadcasted_iota(jnp.int32, (rows, lanes), 1) >> 1
    for i in range(levels // chunk):
        copies[i].wait()

        def some(g, carry):
            out = []
            for field in range(fields):
                left, right = carry[2 * field : 2 * field + 2]
                for k in range(4):
                    level = i * chunk + g * 4 + k
                    turned = pltpu.roll(held[field, level], 2 * level, axis=1)
                    left = jnp.where(pair == level, turned, left)
                    right = jnp.where(pair == (level + levels - 1) % levels, turned, right)
                out += [left, right]
            return tuple(out)

        if i == 0:
            carry = (jnp.zeros((rows, lanes), F32),) * (2 * fields)
        carry = lax.fori_loop(0, chunk // 4, some, carry)
    for field in range(fields):
        own_left[field] = carry[2 * field]
        own_right[field] = pltpu.roll(carry[2 * field + 1], 2, axis=1)


def pack_cols(air):
    fields, levels, rows, lanes = air.shape
    chunk = 8
    out = jax.ShapeDtypeStruct((fields, rows, lanes), F32)
    return pl.pallas_call(
        functools.partial(cols_kernel, chunk=chunk),
        in_specs=[pl.BlockSpec(memory_space=pl.ANY)],
        out_specs=[pl.BlockSpec(memory_space=pltpu.VMEM)] * 2,
        out_shape=[out, out],
        scratch_shapes=[pltpu.VMEM(air.shape, F32), pltpu.SemaphoreType.DMA((levels // chunk,))],
        compiler_params=pltpu.CompilerParams(vmem_limit_bytes=BIG),
        cost_estimate=pl.CostEstimate(flops=4 * air.size, bytes_accessed=4 * air.size, transcendentals=0),
        name="pack_cols",
    )(air)


def with_row(strip, row, first):
    rows = strip.shape[0]
    index = lax.broadcasted_iota(jnp.int32, strip.shape, 0)
    if first:
        return jnp.where(index == 0, row, pltpu.roll(strip, 1, axis=0))
    return jnp.where(index == rows - 1, row, pltpu.roll(strip, rows - 1, axis=0))


def strips_kernel(got_a, got_b, own_left, own_right, to_g, to_x):
    even_col = grid_place()[1]
    fields, rows, lanes = own_left.shape
    top, _, low, _ = row_halo(got_a, got_b)
    levels = top.shape[0] // fields
    level = lax.broadcasted_iota(jnp.int32, (levels, lanes), 0)
    pair = lax.broadcasted_iota(jnp.int32, (levels, lanes), 1) >> 1
    spread = jnp.where(level == pair, 1.0, 0.0).astype(BF16)
    odd = (lax.broadcasted_iota(jnp.int32, (rows, lanes), 1) & 1) == 1
    for field in range(fields):
        at = slice(field * levels, (field + 1) * levels)
        above, below = [
            lax.dot_general(h[at].astype(BF16), spread, (((0,), (0,)), ((), ())), preferred_element_type=F32)
            for h in (top, low)
        ]
        left, right = own_left[field], own_right[field]
        edge = pltpu.roll(left, 1, axis=1)
        around = with_row(edge, 2.0 * above[0:1], True) + with_row(edge, 2.0 * below[0:1], False)
        west = jnp.where(odd, MIX * (edge + left + around), left)
        edge = pltpu.roll(right, lanes - 1, axis=1)
        around = with_row(edge, 2.0 * above[lanes - 1 :], True) + with_row(edge, 2.0 * below[lanes - 1 :], False)
        east = jnp.where(odd, right, MIX * (edge + right + around))
        to_g[field] = jnp.where(even_col, east, west).astype(BF16)
        to_x[field] = jnp.where(even_col, west, east).astype(BF16)


def make_strips(got_a, got_b, own_left, own_right):
    vmem = pl.BlockSpec(memory_space=pltpu.VMEM)
    out = jax.ShapeDtypeStruct(own_left.shape, BF16)
    return pl.pallas_call(
        strips_kernel,
        in_specs=[vmem] * 4,
        out_specs=[vmem] * 2,
        out_shape=[out, out],
        compiler_params=pltpu.CompilerParams(vmem_limit_bytes=BIG),
        name="strips",
    )(got_a, got_b, own_left, own_right)


def side_strips(field, got_g, got_x, own_left, own_right):
    _, even_col, _, _, has_left, has_right = grid_place()
    rows, lanes = got_g.shape[1], got_g.shape[2]
    from_g, from_x = got_g[field].astype(F32), got_x[field].astype(F32)
    west = jnp.where(even_col, from_x, from_g) * has_left
    east = jnp.where(even_col, from_g, from_x) * has_right
    next_west = pltpu.roll(west + MIX * own_left[field], 1, axis=1) * has_left
    next_east = pltpu.roll(east + MIX * own_right[field], lanes - 1, axis=1) * has_right
    odd = (lax.broadcasted_iota(jnp.int32, (rows, lanes), 1) & 1) == 1
    return jnp.where(odd, west, east), jnp.where(odd, next_west, next_east)


def row_halo(got_a, got_b):
    even_row, _, has_top, has_low, _, _ = grid_place()
    from_a, from_b = got_a[...].astype(F32), got_b[...].astype(F32)
    top = jnp.where(even_row, from_b, from_a) * has_top
    low = jnp.where(even_row, from_a, from_b) * has_low
    lanes = top.shape[1] // 2
    return top[:, :lanes], top[:, lanes:], low[:, :lanes], low[:, lanes:]


def sides_of_row(row):
    lanes = row.shape[1]
    lane = lax.broadcasted_iota(jnp.int32, row.shape, 1)
    from_left = jnp.where(lane == 0, 0.0, pltpu.roll(row, 1, axis=1))
    from_right = jnp.where(lane == lanes - 1, 0.0, pltpu.roll(row, lanes - 1, axis=1))
    return from_left + from_right


def substep(block, above, below, sides):
    lanes = block.shape[1]
    lane = lax.broadcasted_iota(jnp.int32, block.shape, 1)
    from_left = jnp.where(lane == 0, sides, pltpu.roll(block, 1, axis=1))
    from_right = jnp.where(lane == lanes - 1, sides, pltpu.roll(block, lanes - 1, axis=1))
    around = with_row(block, above, True) + with_row(block, below, False)
    return MIX * (block + around + (from_left + from_right))


def next_rows(top1, top2, low1, low2):
    return MIX * (top1 + top2 + sides_of_row(top1)), MIX * (low1 + low2 + sides_of_row(low1))


def mixed_level(block, top, next_top, low, next_low, sides0, sides1):
    rows = block.shape[0]
    _, _, has_top, has_low, _, _ = grid_place()
    once = substep(block, top, low, sides0)
    next_top = next_top + has_top * MIX * block[0:1]
    next_low = next_low + has_low * MIX * block[rows - 1 : rows]
    return substep(once, next_top, next_low, sides1)


def forward_kernel(
    owner, block_row, block_column, air, forcing, surface_temp, got_a, got_b, got_g, got_x,
    own_left, own_right, weight, payload, slots, source, held, sem, flux_rows, found, tags, counts,
    bound, levels, group,
):
    blocks = weight.shape[0]
    rows, lanes = surface_temp.shape
    devices = payload.shape[0]
    total = devices * bound
    copies = fetch(weight, held, sem)
    top1, top2, low1, low2 = [jnp.concatenate([h[0:1], h[levels : levels + 1]]) for h in row_halo(got_a, got_b)]
    next_top, next_low = next_rows(top1, top2, low1, low2)
    lowest = []
    for field in range(2):
        sides0, sides1 = side_strips(field, got_g, got_x, own_left, own_right)
        lowest.append(
            mixed_level(
                air[field, 0],
                *[h[field : field + 1] for h in (top1, next_top, low1, next_low)],
                pltpu.roll(sides0, lanes - 1, axis=1),
                pltpu.roll(sides1, lanes - 1, axis=1),
            )
        )
    u, v = forcing[0], forcing[1]
    ts = surface_temp[...]
    speed = jnp.sqrt(u * u + v * v + 1.0)
    fluxes = [
        speed * (ts - lowest[0]),
        speed * (0.5 * ts - lowest[1]),
        speed * u,
        speed * v,
        forcing[2],
        forcing[3] - 0.3 * ts,
        forcing[4],
        forcing[5],
    ]
    source[0] = fluxes[0]
    source[1] = fluxes[1]
    for field in range(NF):
        flux_rows[pl.ds(field, rows, stride=NF), :] = fluxes[field]
    if total > blocks:
        tags[...] = jnp.full_like(tags, -1.0)
        found[...] = jnp.zeros_like(found)

    def clear(i, _):
        counts[i] = 0
        return 0

    lax.fori_loop(0, devices, clear, 0)

    def some(first):
        outs = []
        for k in range(0, group, 2):
            at = first + k
            picked = [
                flux_rows[pl.ds(pl.multiple_of(block_column[n] * NF, NF), NF), :] for n in (at, at + 1)
            ]
            out = lax.dot_general(
                jnp.concatenate(picked).astype(BF16),
                held[pl.ds(at, 2)].reshape(2 * lanes, lanes),
                (((1,), (1,)), ((), ())),
                preferred_element_type=F32,
            )
            outs += [out[:NF, :lanes], out[NF:, lanes:]]
        for k, out in enumerate(outs):
            at = first + k
            to = owner[at]
            rank = counts[to]
            counts[to] = rank + 1
            slot = to * bound + rank
            slots[at] = slot
            found[pl.ds(pl.multiple_of(slot * NF, NF), NF), :] = out
            tags[pl.ds(slot, 1), :] = jnp.full((1, lanes), block_row[at], jnp.int32).astype(F32)

    per_chunk(copies, blocks, group, some)
    f = [found[pl.ds(k, total, stride=NF), :] for k in range(NF)]
    heat = (f[0] + f[1]) + (f[4] + f[5])
    heat_hi = heat.astype(BF16).astype(F32)
    lane = lax.broadcasted_iota(jnp.int32, (total, lanes), 1)
    heat_lo = jnp.where(lane == 0, tags[...], heat - heat_hi)
    shape = payload.shape[:2] + (lanes,)
    for k, part in enumerate((heat_hi, heat_lo, f[2], f[3], f[6] - f[7])):
        payload[:, :, k * lanes : (k + 1) * lanes] = part.reshape(shape).astype(BF16)


def fetch(source, held, sem):
    parts = sem.shape[0]
    size = source.shape[0] // parts
    copies = []
    for i in range(parts):
        at = pl.ds(i * size, size)
        copies.append(pltpu.make_async_copy(source.at[at], held.at[at], sem.at[i]))
        copies[i].start()
    return copies


def per_chunk(copies, blocks, group, some):
    size = blocks // len(copies)
    for i, copy in enumerate(copies):
        copy.wait()

        def body(g, carry, start=i * size):
            some(start + g * group)
            return carry

        lax.fori_loop(0, size // group, body, 0)


def forward(owner, block_row, block_column, air, forcing, surface_temp, halo, own, weight, devices, bound):
    _, levels, rows, lanes = air.shape
    nonzeros = weight.shape[0]
    smem = pl.BlockSpec(memory_space=pltpu.SMEM)
    vmem = pl.BlockSpec(memory_space=pltpu.VMEM)
    args = (forcing, surface_temp, *halo, *own)
    total = devices * bound
    return pl.pallas_call(
        functools.partial(forward_kernel, bound=bound, levels=levels, group=32),
        grid=(1,),
        in_specs=[smem, smem, smem]
        + [pl.BlockSpec((2, 1, rows, lanes), lambda i: (0, 0, 0, 0))]
        + [vmem for x in args]
        + [pl.BlockSpec(memory_space=pl.ANY)],
        out_specs=[vmem, smem, vmem],
        out_shape=[
            jax.ShapeDtypeStruct((devices, bound, SENT * lanes), BF16),
            jax.ShapeDtypeStruct((nonzeros,), jnp.int32),
            jax.ShapeDtypeStruct((2, rows, lanes), F32),
        ],
        scratch_shapes=[
            pltpu.VMEM(weight.shape, BF16),
            pltpu.SemaphoreType.DMA((PARTS,)),
            pltpu.VMEM((rows * NF, lanes), F32),
            pltpu.VMEM((total * NF, lanes), F32),
            pltpu.VMEM((total, lanes), F32),
            pltpu.SMEM((devices,), jnp.int32),
        ],
        compiler_params=pltpu.CompilerParams(vmem_limit_bytes=BIG),
        name="forward_blocks",
    )(owner, block_row, block_column, air, *args, weight)


def pivot_kernel(coupling, inverse, held, sem):
    levels = inverse.shape[0]
    copies = fetch_levels([(coupling, held)], sem, levels - 1)

    def one(level, ratio, last=False):
        below = held[level - 1]
        diagonal = 1.0 + below
        if not last:
            diagonal = diagonal + held[level]
        inv = 1.0 / (diagonal - below * ratio)
        inverse[level] = inv
        return inv if last else held[level] * inv

    for i, part in enumerate(copies):
        for c in part:
            c.wait()
        if i == 0:
            inv = 1.0 / (1.0 + held[0])
            inverse[0] = inv
            ratio = held[0] * inv
        start = max(1, i * STEP)
        stop = min((i + 1) * STEP, levels - 1)
        ratio = lax.fori_loop(start, stop, one, ratio)
    one(levels - 1, ratio, True)


def fetch_levels(pairs, sem, levels, order=1):
    copies = []
    starts = list(range(0, levels, STEP))[::order]
    for i, start in enumerate(starts):
        part = []
        for k, (source, held) in enumerate(pairs):
            at = pl.ds(start, min(STEP, source.shape[-3] - start))
            if len(source.shape) == 4:
                part.append(pltpu.make_async_copy(source.at[:, at], held.at[:, at], sem.at[k * len(starts) + i]))
            else:
                part.append(pltpu.make_async_copy(source.at[at], held.at[at], sem.at[k * len(starts) + i]))
        for c in part:
            c.start()
        copies.append(part)
    return copies


def pivots(coupling):
    levels, rows, lanes = coupling.shape
    shape = (levels + 1, rows, lanes)
    return pl.pallas_call(
        pivot_kernel,
        in_specs=[pl.BlockSpec(memory_space=pl.ANY)],
        out_specs=pl.BlockSpec(memory_space=pltpu.VMEM),
        out_shape=jax.ShapeDtypeStruct(shape, F32),
        scratch_shapes=[pltpu.VMEM(coupling.shape, F32), pltpu.SemaphoreType.DMA(((levels + STEP) // STEP,))],
        compiler_params=pltpu.CompilerParams(vmem_limit_bytes=BIG),
        cost_estimate=pl.CostEstimate(flops=8 * coupling.size, bytes_accessed=8 * coupling.size, transcendentals=0),
        name="pivots",
    )(coupling)


def beside(block, shifts):
    high = block.astype(BF16)
    low = (block - high.astype(F32)).astype(BF16)
    return jnp.dot(jnp.concatenate([high, low], axis=1), shifts, preferred_element_type=F32)


def stepped(block, above, below, inside, sides, edge):
    around = with_row(block, above, True) + with_row(block, below, False)
    return MIX * (block + around + (inside + jnp.where(edge, sides, 0.0)))


def up_kernel(
    air, coupling, inverse, got_a, got_b, got_g, got_x, own_left, own_right, source, reduced,
    held, held_c, held_i, done, halo_rows, strips, shifts, inside, once, sem, out_sem,
):
    fields, levels, rows, lanes = air.shape
    copies = fetch_levels([(air, held), (inverse, held_i), (coupling, held_c)], sem, levels)
    _, _, has_top, has_low, _, _ = grid_place()
    halo = row_halo(got_a, got_b)
    for k, h in enumerate((halo[0], halo[2], *next_rows(*halo))):
        halo_rows[k] = h
    for field in range(fields):
        sides0, sides1 = side_strips(field, got_g, got_x, own_left, own_right)
        strips[field, 0] = sides0
        strips[field, 1] = sides1
    row = lax.broadcasted_iota(jnp.int32, (2 * lanes, lanes), 0) % lanes
    column = lax.broadcasted_iota(jnp.int32, (2 * lanes, lanes), 1)
    shifts[...] = jnp.where(jnp.abs(row - column) == 1, 1.0, 0.0).astype(BF16)
    lane = lax.broadcasted_iota(jnp.int32, (rows, lanes), 1)
    edge = (lane == 0) | (lane == lanes - 1)
    groups = levels // GROUP
    members = [(field, k) for k in range(GROUP) for field in range(fields)]

    def place(k, field):
        return slice((k * fields + field) * rows, (k * fields + field + 1) * rows)

    def first_inside(g):
        block = jnp.concatenate([held[field, g * GROUP + k] for field, k in members])
        inside[0, g % 2] = beside(block, shifts[...])

    def first_step(g):
        for field, k in members:
            level = g * GROUP + k
            at = field * levels + level
            sides = pltpu.roll(strips[field, 0], (2 * lanes - 1 - 2 * level) % lanes, axis=1)
            once[g % 2, place(k, field)] = stepped(
                held[field, level], halo_rows[0, at : at + 1], halo_rows[1, at : at + 1],
                inside[0, g % 2, place(k, field)], sides, edge,
            )
        inside[1, g % 2] = beside(once[g % 2], shifts[...])

    def second_step(g):
        for field, k in members:
            level = g * GROUP + k
            at = field * levels + level
            sides = pltpu.roll(strips[field, 1], (2 * lanes - 1 - 2 * level) % lanes, axis=1)
            top = halo_rows[2, at : at + 1] + has_top * MIX * held[field, level, 0:1]
            low = halo_rows[3, at : at + 1] + has_low * MIX * held[field, level, rows - 1 : rows]
            right = stepped(
                once[g % 2, place(k, field)], top, low, inside[1, g % 2, place(k, field)], sides, edge
            )
            if level == 0:
                right = right + SURFACE_STEP * source[field]
            else:
                right = right + held_c[level - 1] * done[field, level - 1]
            done[field, level] = right * held_i[level]

    outs = []
    for g in range(groups + 2):
        if g < groups:
            if g * GROUP % STEP == 0:
                for c in copies[g * GROUP // STEP]:
                    c.wait()
            first_inside(g)
        if 0 <= g - 1 < groups:
            first_step(g - 1)
        if g >= 2:
            second_step(g - 2)
            end = (g - 1) * GROUP
            if end % STEP == 0:
                at = pl.ds(end - STEP, STEP)
                outs.append(pltpu.make_async_copy(done.at[:, at], reduced.at[:, at], out_sem.at[end // STEP - 1]))
                outs[-1].start()
    for c in outs:
        c.wait()


def columns_up(air, coupling, inverse, halo, own, source):
    fields, levels, rows, lanes = air.shape
    args = (air, coupling, inverse, *halo, *own, source)
    hbm = pl.BlockSpec(memory_space=pl.ANY)
    parts = levels // STEP
    return pl.pallas_call(
        up_kernel,
        in_specs=[hbm] * 3 + [pl.BlockSpec(memory_space=pltpu.VMEM)] * (len(args) - 3),
        out_specs=hbm,
        out_shape=jax.ShapeDtypeStruct(air.shape, F32),
        scratch_shapes=[
            pltpu.VMEM(air.shape, F32),
            pltpu.VMEM(coupling.shape, F32),
            pltpu.VMEM(inverse.shape, F32),
            pltpu.VMEM(air.shape, F32),
            pltpu.VMEM((4, fields * levels, lanes), F32),
            pltpu.VMEM((fields, 2, rows, lanes), F32),
            pltpu.VMEM((2 * lanes, lanes), BF16),
            pltpu.VMEM((2, 2, GROUP * fields * rows, lanes), F32),
            pltpu.VMEM((2, GROUP * fields * rows, lanes), F32),
            pltpu.SemaphoreType.DMA((3 * parts,)),
            pltpu.SemaphoreType.DMA((parts,)),
        ],
        compiler_params=pltpu.CompilerParams(vmem_limit_bytes=BIG),
        cost_estimate=pl.CostEstimate(flops=40 * air.size, bytes_accessed=12 * air.size, transcendentals=0),
        name="columns_up",
    )(*args)


def down_kernel(reduced, coupling, inverse, air_new, held, held_c, held_i, sem, out_sem):
    _, levels, rows, lanes = reduced.shape
    copies = fetch_levels([(reduced, held), (inverse, held_i), (coupling, held_c)], sem, levels, -1)
    outs = []
    for i, part in enumerate(copies):
        for c in part:
            c.wait()
        top = levels - 1 - i * STEP

        def one(k, _, top=top):
            level = top - k
            ratio = held_c[level] * held_i[level]
            for field in range(2):
                held[field, level] = held[field, level] + ratio * held[field, level + 1]
            return 0

        lax.fori_loop(1 if i == 0 else 0, STEP, one, 0)
        at = pl.ds(levels - (i + 1) * STEP, STEP)
        outs.append(pltpu.make_async_copy(held.at[:, at], air_new.at[:, at], out_sem.at[i]))
        outs[i].start()
    for c in outs:
        c.wait()


def columns_down(reduced, coupling, inverse):
    levels = reduced.shape[1]
    hbm = pl.BlockSpec(memory_space=pl.ANY)
    parts = levels // STEP
    return pl.pallas_call(
        down_kernel,
        in_specs=[hbm] * 3,
        out_specs=hbm,
        out_shape=jax.ShapeDtypeStruct(reduced.shape, F32),
        scratch_shapes=[
            pltpu.VMEM(reduced.shape, F32),
            pltpu.VMEM(coupling.shape, F32),
            pltpu.VMEM(inverse.shape, F32),
            pltpu.SemaphoreType.DMA((3 * parts,)),
            pltpu.SemaphoreType.DMA((parts,)),
        ],
        compiler_params=pltpu.CompilerParams(vmem_limit_bytes=BIG),
        cost_estimate=pl.CostEstimate(flops=8 * reduced.size, bytes_accessed=12 * reduced.size, transcendentals=0),
        name="columns_down",
    )(reduced, coupling, inverse)


def ocean_kernel(arrived, land_mask, ocean_temp, ocean_ice, layer_depth, temp_new, ice_new, replies):
    blocks, lanes = ocean_temp.shape
    total = arrived.shape[0] * arrived.shape[1]
    wide = arrived.shape[2]
    block = arrived[...].astype(F32).reshape(total, wide)
    lane = lax.broadcasted_iota(jnp.int32, (total, wide), 1)
    tag = block[:, lanes : lanes + 1].astype(jnp.int32)
    block = jnp.where(lane == lanes, 0.0, block).astype(BF16)
    slot_of = (tag == lax.broadcasted_iota(jnp.int32, (total, blocks), 1)).astype(F32).astype(BF16)
    sums = lax.dot_general(slot_of, block, (((0,), (0,)), ((), ())), preferred_element_type=F32)
    sums = [sums[:, k * lanes : (k + 1) * lanes] for k in range(SENT)]
    heat = sums[0] + sums[1]
    stress = sums[2] * sums[2] + sums[3] * sums[3]
    wet = land_mask[...].astype(F32)
    temp = ocean_temp[...]
    temp = temp + wet * (0.3 * heat / layer_depth[...] - 0.01 * stress * temp)
    ice = jnp.clip(ocean_ice[...] - wet * 0.05 * (heat + sums[4]), 0.0, 1.0)
    temp_new[...] = temp
    ice_new[...] = ice
    pair = jnp.concatenate([temp, ice], axis=1).astype(BF16)
    answer = jnp.dot(slot_of, pair, preferred_element_type=F32)
    replies[...] = answer.reshape(replies.shape).astype(BF16)


def ocean(arrived, land_mask, ocean_temp, ocean_ice, layer_depth):
    devices, bound, _ = arrived.shape
    blocks, lanes = ocean_temp.shape
    vmem = pl.BlockSpec(memory_space=pltpu.VMEM)
    return pl.pallas_call(
        ocean_kernel,
        in_specs=[vmem] * 5,
        out_specs=[vmem] * 3,
        out_shape=[
            jax.ShapeDtypeStruct((blocks, lanes), F32),
            jax.ShapeDtypeStruct((blocks, lanes), F32),
            jax.ShapeDtypeStruct((devices, bound, 2 * lanes), BF16),
        ],
        compiler_params=pltpu.CompilerParams(vmem_limit_bytes=BIG),
        name="ocean",
    )(arrived, land_mask, ocean_temp, ocean_ice, layer_depth)


def backward_kernel(slots, block_column, returned, weight, seen, held, sem, pairs, sums, group):
    blocks, lanes = weight.shape[0], weight.shape[1]
    total = returned.shape[0] * returned.shape[1]
    rows = seen.shape[1]
    copies = fetch(weight, held, sem)
    pairs[...] = jnp.zeros_like(pairs)
    sums[...] = jnp.zeros_like(sums)
    for k in range(2):
        part = returned[:, :, k * lanes : (k + 1) * lanes].astype(F32).reshape(total, lanes)
        pairs[pl.ds(k, total, stride=8), :] = part

    def some(first):
        outs = []
        for k in range(0, group, 2):
            at = first + k
            picked = [pairs[pl.ds(pl.multiple_of(slots[n] * 8, 8), 8), :] for n in (at, at + 1)]
            out = jnp.dot(
                jnp.concatenate(picked).astype(BF16),
                jnp.concatenate([held[at], held[at + 1]], axis=1),
                preferred_element_type=F32,
            )
            outs += [out[:8, :lanes], out[8:, lanes:]]
        for k, out in enumerate(outs):
            place = pl.ds(pl.multiple_of(block_column[first + k] * 8, 8), 8)
            sums[place, :] += out

    per_chunk(copies, blocks, group, some)
    for k in range(2):
        seen[k] = sums[pl.ds(k, rows, stride=8), :]


def backward(slots, block_column, returned, weight, rows):
    devices, bound, _ = returned.shape
    nonzeros, lanes, _ = weight.shape
    smem = pl.BlockSpec(memory_space=pltpu.SMEM)
    vmem = pl.BlockSpec(memory_space=pltpu.VMEM)
    return pl.pallas_call(
        functools.partial(backward_kernel, group=32),
        in_specs=[smem, smem, vmem, pl.BlockSpec(memory_space=pl.ANY)],
        out_specs=vmem,
        out_shape=jax.ShapeDtypeStruct((2, rows, lanes), F32),
        scratch_shapes=[
            pltpu.VMEM(weight.shape, BF16),
            pltpu.SemaphoreType.DMA((PARTS,)),
            pltpu.VMEM((devices * bound * 8, lanes), F32),
            pltpu.VMEM((rows * 8, lanes), F32),
        ],
        compiler_params=pltpu.CompilerParams(vmem_limit_bytes=BIG),
        name="backward_blocks",
    )(slots, block_column, returned, weight)


def local(
    air_state,
    coupling,
    forcing,
    surface_temp,
    remap_weight,
    block_owner,
    block_row,
    block_column,
    land_mask,
    ocean_temp,
    ocean_ice,
    layer_depth,
):
    devices = lax.axis_size("comp") * lax.axis_size("gx") * lax.axis_size("gy")
    nonzeros = remap_weight.shape[0]
    bound = max(4, (nonzeros + devices - 1) // devices)
    rows_a, rows_b = pack_rows(air_state)
    got_a = lax.ppermute(rows_a, ALL, row_swaps(0))
    got_b = lax.ppermute(rows_b, ALL, row_swaps(1))
    own = pack_cols(air_state)
    to_g, to_x = make_strips(got_a, got_b, *own)
    got_x = lax.ppermute(to_x, ("comp", "gy"), col_swaps(1))
    got_g = lax.ppermute(to_g, ("comp", "gy"), col_swaps(0))
    halo = (got_a, got_b, got_g, got_x)
    inverse = pivots(coupling)
    halo, inverse = lax.optimization_barrier((halo, inverse))
    payload, slots, source = forward(
        block_owner[:, 0], block_row, block_column, air_state, forcing, surface_temp, halo, own,
        remap_weight, devices, bound,
    )
    arrived = lax.all_to_all(payload, ALL, split_axis=0, concat_axis=0, tiled=True)
    reduced = columns_up(air_state, coupling, inverse, halo, own, source)
    arrived, reduced = lax.optimization_barrier((arrived, reduced))
    ocean_temp_new, ocean_ice_new, replies = ocean(
        arrived, land_mask, ocean_temp, ocean_ice, layer_depth
    )
    returned = lax.all_to_all(replies, ALL, split_axis=0, concat_axis=0, tiled=True)
    air_new = columns_down(reduced, coupling, inverse)
    returned, air_new = lax.optimization_barrier((returned, air_new))
    surface_seen = backward(slots, block_column, returned, remap_weight, surface_temp.shape[0])
    return (air_new, surface_seen, ocean_temp_new, ocean_ice_new)


def solution(mesh):
    in_specs = (
        P(None, None, "gx", ("comp", "gy")),
        P(None, "gx", ("comp", "gy")),
        P(None, "gx", ("comp", "gy")),
        P("gx", ("comp", "gy")),
        P(ALL, None, None),
        P(ALL, None),
        P(ALL),
        P(ALL),
        P(ALL, None),
        P(ALL, None),
        P(ALL, None),
        P(ALL, None),
    )
    out_specs = (
        P(None, None, "gx", ("comp", "gy")),
        P(None, "gx", ("comp", "gy")),
        P(ALL, None),
        P(ALL, None),
    )
    return jax.shard_map(local, mesh=mesh, in_specs=in_specs, out_specs=out_specs, check_vma=False)
```

time: 88.7 us -> 62.4 us (0.70)
  blocking collectives: 23.4 us -> 0 us
  Pallas kernels: 54.3 us -> 39.9 us
  starting transfers between devices: 6.82 us -> 13.4 us
  waiting for transfers between devices: 0.77 us -> 5.21 us
    all_to_all x1 -> x0, blocking collectives: 23.4 us -> none  [local(): lax.all_to_all(payload, ALL, split_axis=0, concat_axis=0, tiled=True)]
    pallas_call x4 -> x6, Pallas kernels: 38.5 us -> 29.4 us  [the longest x1 9.23 us: columns_up(): pl.pallas_call(up_kernel, in_specs=[hbm] * 3 + [pl.BlockSpec(memory_space...]
    all_to_all x0 -> x1, starting transfers between devices: none -> 5.43 us  [local(): lax.all_to_all(payload, ALL, split_axis=0, concat_axis=0, tiled=True)]
    pallas_call x1, Pallas kernels: 11.8 us -> 6.54 us  [forward(): pl.pallas_call(functools.partial(forward_kernel, bound=bound, levels=leve...]
    all_to_all x1, waiting for transfers between devices: 0.01 us -> 2.74 us  [local(): lax.all_to_all(replies, ALL, split_axis=0, concat_axis=0, tiled=True)]
    all_to_all x0 -> x1, waiting for transfers between devices: none -> 2.46 us  [local(): lax.all_to_all(payload, ALL, split_axis=0, concat_axis=0, tiled=True)]
    unnamed x10 -> x12, local copies, waits for them, and re-layouts: 1.91 us -> 2.62 us
  transfers between devices with their start and end apart: 5 -> 6, of which waited for: 1 -> 2; matrix products, arithmetic and copies ran while one was open for 0% -> 0% of each run, Pallas kernels for 30% -> 36%
where the time goes in v2:
time: 62.4 us; the launch traced here: 61.9 us
  Pallas kernels  39.9 us (64%)
  starting transfers between devices  13.4 us (21%)
  waiting for transfers between devices  5.21 us (8%)
  local copies, waits for them, and re-layouts  2.62 us (4%)
  between operations  0.76 us (1%)
    pallas_call x1, Pallas kernels, columns_up(): pl.pallas_call(up_kernel, in_specs=[hbm] * 3 + [pl.BlockSpec(memory_space...  9.23 us
    pallas_call x1, Pallas kernels, forward(): pl.pallas_call(functools.partial(forward_kernel, bound=bound, levels=leve...  6.54 us
    pallas_call x1, Pallas kernels, columns_down(): pl.pallas_call(down_kernel, in_specs=[hbm] * 3, out_specs=hbm, out_shape=...  5.48 us
    all_to_all x1, starting transfers between devices, local(): lax.all_to_all(payload, ALL, split_axis=0, concat_axis=0, tiled=True)  5.43 us
    pallas_call x1, Pallas kernels, backward(): pl.pallas_call(functools.partial(backward_kernel, group=32), in_specs=[sm...  5.31 us
    pallas_call x1, Pallas kernels, pack_cols(): pl.pallas_call(functools.partial(cols_kernel, chunk=chunk), in_specs=[pl....  4.08 us
    all_to_all x1, starting transfers between devices, local(): lax.all_to_all(replies, ALL, split_axis=0, concat_axis=0, tiled=True)  3.38 us
    pallas_call x1, Pallas kernels, pivots(): pl.pallas_call(pivot_kernel, in_specs=[pl.BlockSpec(memory_space=pl.ANY)]...  3.36 us
  transfers between devices with their start and end apart: 6, of which 2 were waited for; matrix products, arithmetic and copies ran while one was open for 0% of the time, Pallas kernels for 36%

profile of v2, /device:TPU:0, one launch (start us, length us, event | category | flops | bytes accessed | tf_op | source)
XLA Modules:
  0.0 61.9 jit_solution(8725107605578286261)
XLA Ops:
  0.6 1.9 %pack_rows.1 = (bf16[128,256]{1,0:T(8,128)(2,1)}, bf16[128,256]{1,0:T(8,128)(2,1)}) custom-call(f32[128,64,128]{2,1,0:T(8,128)} %bitcast.2), custom_call_target="tpu_custom_call" | custom-call | tf_op jit(solution)/shard_map/pack_rows/pallas_call | solution.py:73
  2.6 3.0 %collective-permute-start = (bf16[128,256]{1,0:T(8,128)(2,1)}, bf16[128,256]{1,0:T(8,128)(2,1)S(1)}, u32[]{:S(2)}, u32[]{:S(2)}) collective-permute-start(bf16[128,256]{1,0:T(8,128)(2,1)} %get-tuple-element.25), channel_id=1, source_target_pairs={{0,2},{1,3},{2,0},{3,1},{4,6},{5,7},{6,4},{7,5},{8,10},{9,11},{10,... | collective-permute-start | bytes 196616 | tf_op jit(solution)/shard_map/ppermute | solution.py:702
  5.6 0.0 collective-permute-start.1
  5.6 4.1 %pack_cols.1 = (f32[2,64,128]{2,1,0:T(8,128)}, f32[2,64,128]{2,1,0:T(8,128)}) custom-call(f32[2,64,64,128]{3,2,1,0:T(8,128)} %air.5), custom_call_target="tpu_custom_call" | custom-call | flops 4194304 | bytes 4194304 | tf_op jit(solution)/shard_map/pack_cols/pallas_call | solution.py:119
  9.7 0.0 collective-permute-done.got_a
  9.7 0.0 copy-start.1
  9.7 0.0 collective-permute-done.1.got_b
  9.7 0.0 copy-start.2
  9.7 0.6 copy-done.1
  10.3 0.0 copy-done.2
  10.3 1.8 %strips.1 = (bf16[2,64,128]{2,1,0:T(8,128)(2,1)}, bf16[2,64,128]{2,1,0:T(8,128)(2,1)}) custom-call(bf16[128,256]{1,0:T(8,128)(2,1)} %copy-done.1, bf16[128,256]{1,0:T(8,128)(2,1)} %copy-done.2, f32[2,64,128]{2,1,0:T(8,128)} %get-tuple-element.27.own_left, f32[2,64,128]{2,1,0:T(8,128)} %get-tuple-element.28.own_right), custom_call_target="tpu_custom_call" | custom-call | tf_op jit(solution)/shard_map/strips/pallas_call | solution.py:168
  12.1 0.5 collective-permute-start.2
  12.6 1.1 %collective-permute-start.3 = (bf16[2,64,128]{2,1,0:T(8,128)(2,1)}, bf16[2,64,128]{2,1,0:T(8,128)(2,1)S(1)}, u32[]{:S(2)}, u32[]{:S(2)}) collective-permute-start(bf16[2,64,128]{2,1,0:T(8,128)(2,1)} %get-tuple-element.30), channel_id=1, source_target_pairs={{0,17},{1,16},{16,1},{17,0},{2,19},{3,18},{18,3},{19,2},{4,21},{5,... | collective-permute-start | bytes 98312 | tf_op jit(solution)/shard_map/ppermute | solution.py:706
  13.8 3.4 %pivots.1.inverse = f32[64,64,128]{2,1,0:T(8,128)} custom-call(f32[63,64,128]{2,1,0:T(8,128)} %coupling.5), custom_call_target="tpu_custom_call" | custom-call | flops 4128768 | bytes 4128768 | tf_op jit(solution)/shard_map/pivots/pallas_call | solution.py:416
  17.1 0.0 collective-permute-done.2.got_g
  17.1 0.0 copy-start.4
  17.1 0.0 collective-permute-done.3.got_x
  17.2 0.0 copy-start.5
  17.2 0.6 copy-done.4
  17.8 0.0 copy-done.5
  17.8 6.5 %forward_blocks.1 = (bf16[32,8,640]{2,1,0:T(8,128)(2,1)}, s32[256]{0:T(256)}, f32[2,64,128]{2,1,0:T(8,128)}) custom-call(s32[256]{0:T(256)} %bitcast.3, s32[256]{0:T(256)} %block_row.1, s32[256]{0:T(256)} %block_column.3, f32[2,64,64,128]{3,2,1,0:T(8,128)} %air.5, f32[6,64,128]{2,1,0:T(8,128)} %forcing.1, f32[64,128]{1,0:T(8,128)} %surface_temp.1, ...), custom_call_target="tpu_custom_call" | custom-call | tf_op jit(solution)/shard_map/forward_blocks/pallas_call | solution.py:344
  24.3 5.4 %all-to-all-start = ((bf16[32,8,640]{2,1,0:T(8,128)(2,1)}), bf16[32,8,640]{2,1,0:T(8,128)(2,1)S(1)}, u32[]{:S(2)}, u32[]{:S(2)}) async-start(bf16[32,8,640]{2,1,0:T(8,128)(2,1)} %get-tuple-element.35), calls=%async_computation | async-start | bytes 655360 | tf_op jit(solution)/shard_map/all_to_all | solution.py:715
  29.8 9.2 %columns_up.1.reduced = f32[2,64,64,128]{3,2,1,0:T(8,128)} custom-call(f32[2,64,64,128]{3,2,1,0:T(8,128)} %air.5, f32[63,64,128]{2,1,0:T(8,128)} %coupling.5, f32[64,64,128]{2,1,0:T(8,128)} %pivots.1.inverse, bf16[128,256]{1,0:T(8,128)(2,1)} %copy-done.1, bf16[128,256]{1,0:T(8,128)(2,1)} %copy-done.2, bf16[2,64,128]{2,1,0:T(8,128)(2,1)} %copy-done.4, ...), custom_call_target="tpu_custom_call" | custom-call | flops 41943040 | bytes 12582912 | tf_op jit(solution)/shard_map/columns_up/pallas_call | solution.py:520
  39.0 2.5 %all-to-all-done.arrived = bf16[32,8,640]{2,1,0:T(8,128)(2,1)S(1)} async-done(((bf16[32,8,640]{2,1,0:T(8,128)(2,1)}), bf16[32,8,640]{2,1,0:T(8,128)(2,1)S(1)}, u32[]{:S(2)}, u32[]{:S(2)}) %all-to-all-start) | async-done | bytes 327712 | tf_op jit(solution)/shard_map/all_to_all | solution.py:715
  41.5 0.0 copy-start
  41.5 0.7 %copy-done = bf16[32,8,640]{2,1,0:T(8,128)(2,1)} copy-done((bf16[32,8,640]{2,1,0:T(8,128)(2,1)}, bf16[32,8,640]{2,1,0:T(8,128)(2,1)S(1)}, u32[]{:S(2)}) %copy-start) | copy-done | bytes 327704
  42.2 2.1 %ocean.1 = (f32[64,128]{1,0:T(8,128)}, f32[64,128]{1,0:T(8,128)}, bf16[32,8,256]{2,1,0:T(8,128)(2,1)}) custom-call(bf16[32,8,640]{2,1,0:T(8,128)(2,1)} %copy-done, s32[64,128]{1,0:T(8,128)} %land_mask.1, f32[64,128]{1,0:T(8,128)} %ocean_temp.1, f32[64,128]{1,0:T(8,128)} %ocean_ice.1, f32[64,128]{1,0:T(8,128)} %layer_depth.1), custom_call_target="tpu_custom_call" | custom-call | tf_op jit(solution)/shard_map/ocean/pallas_call | solution.py:618
  44.3 3.4 %all-to-all-start.1 = ((bf16[32,8,256]{2,1,0:T(8,128)(2,1)}), bf16[32,8,256]{2,1,0:T(8,128)(2,1)S(1)}, u32[]{:S(2)}, u32[]{:S(2)}) async-start(bf16[32,8,256]{2,1,0:T(8,128)(2,1)} %get-tuple-element.39), calls=%async_computation.1 | async-start | bytes 262144 | tf_op jit(solution)/shard_map/all_to_all | solution.py:721
  47.7 5.5 %columns_down.1 = f32[2,64,64,128]{3,2,1,0:T(8,128)} custom-call(f32[2,64,64,128]{3,2,1,0:T(8,128)} %columns_up.1.reduced, f32[63,64,128]{2,1,0:T(8,128)} %coupling.5, f32[64,64,128]{2,1,0:T(8,128)} %pivots.1.inverse), custom_call_target="tpu_custom_call" | custom-call | flops 8388608 | bytes 12582912 | tf_op jit(solution)/shard_map/columns_down/pallas_call | solution.py:572
  53.2 2.7 %all-to-all-done.1.returned = bf16[32,8,256]{2,1,0:T(8,128)(2,1)S(1)} async-done(((bf16[32,8,256]{2,1,0:T(8,128)(2,1)}), bf16[32,8,256]{2,1,0:T(8,128)(2,1)S(1)}, u32[]{:S(2)}, u32[]{:S(2)}) %all-to-all-start.1) | async-done | bytes 131104 | tf_op jit(solution)/shard_map/all_to_all | solution.py:721
  55.9 0.0 copy-start.3
  56.0 0.7 %copy-done.3 = bf16[32,8,256]{2,1,0:T(8,128)(2,1)} copy-done((bf16[32,8,256]{2,1,0:T(8,128)(2,1)}, bf16[32,8,256]{2,1,0:T(8,128)(2,1)S(1)}, u32[]{:S(2)}) %copy-start.3) | copy-done | bytes 131096
  56.6 5.3 %backward_blocks.1 = f32[2,64,128]{2,1,0:T(8,128)} custom-call(s32[256]{0:T(256)} %get-tuple-element.42.slots, s32[256]{0:T(256)} %block_column.3, bf16[32,8,256]{2,1,0:T(8,128)(2,1)} %copy-done.3, bf16[256,128,128]{2,1,0:T(8,128)(2,1)} %weight.3), custom_call_target="tpu_custom_call" | custom-call | tf_op jit(solution)/shard_map/backward_blocks/pallas_call | solution.py:668
Async XLA Ops:
  2.6 7.1 %collective-permute-start = (bf16[128,256]{1,0:T(8,128)(2,1)}, bf16[128,256]{1,0:T(8,128)(2,1)S(1)}, u32[]{:S(2)}, u32[]{:S(2)}) collective-permute-start(bf16[128,256]{1,0:T(8,128)(2,1)} %get-tuple-element.25), channel_id=1, source_target_pairs={{0,2},{1,3},{2,0},{3,1},{4,6},{5,7},{6,4},{7,5},{8,10},{9,11},{10,... | collective-permute-start | bytes 196616 | tf_op jit(solution)/shard_map/ppermute | solution.py:702
  5.6 4.1 %collective-permute-start.1 = (bf16[128,256]{1,0:T(8,128)(2,1)}, bf16[128,256]{1,0:T(8,128)(2,1)S(1)}, u32[]{:S(2)}, u32[]{:S(2)}) collective-permute-start(bf16[128,256]{1,0:T(8,128)(2,1)} %get-tuple-element.26), channel_id=1, source_target_pairs={{0,1},{1,0},{2,4},{3,5},{4,2},{5,3},{6,8},{7,9},{8,6},{9,7},{10,12... | collective-permute-start | bytes 196616 | tf_op jit(solution)/shard_map/ppermute | solution.py:703
  9.7 0.6 %copy-start.1 = (bf16[128,256]{1,0:T(8,128)(2,1)}, bf16[128,256]{1,0:T(8,128)(2,1)S(1)}, u32[]{:S(2)}) copy-start(bf16[128,256]{1,0:T(8,128)(2,1)S(1)} %collective-permute-done.got_a) | copy-start | bytes 196612
  9.7 0.6 %copy-start.2 = (bf16[128,256]{1,0:T(8,128)(2,1)}, bf16[128,256]{1,0:T(8,128)(2,1)S(1)}, u32[]{:S(2)}) copy-start(bf16[128,256]{1,0:T(8,128)(2,1)S(1)} %collective-permute-done.1.got_b) | copy-start | bytes 196612
  12.1 5.0 %collective-permute-start.2 = (bf16[2,64,128]{2,1,0:T(8,128)(2,1)}, bf16[2,64,128]{2,1,0:T(8,128)(2,1)S(1)}, u32[]{:S(2)}, u32[]{:S(2)}) collective-permute-start(bf16[2,64,128]{2,1,0:T(8,128)(2,1)} %get-tuple-element.29), channel_id=1, source_target_pairs={{0,1},{1,0},{16,17},{17,16},{2,3},{3,2},{18,19},{19,18},{4,5},{5,4... | collective-permute-start | bytes 98312 | tf_op jit(solution)/shard_map/ppermute | solution.py:707
  12.6 4.5 %collective-permute-start.3 = (bf16[2,64,128]{2,1,0:T(8,128)(2,1)}, bf16[2,64,128]{2,1,0:T(8,128)(2,1)S(1)}, u32[]{:S(2)}, u32[]{:S(2)}) collective-permute-start(bf16[2,64,128]{2,1,0:T(8,128)(2,1)} %get-tuple-element.30), channel_id=1, source_target_pairs={{0,17},{1,16},{16,1},{17,0},{2,19},{3,18},{18,3},{19,2},{4,21},{5,... | collective-permute-start | bytes 98312 | tf_op jit(solution)/shard_map/ppermute | solution.py:706
  17.1 0.6 copy-start.4
  17.2 0.6 copy-start.5
  24.3 17.1 %all-to-all-start = ((bf16[32,8,640]{2,1,0:T(8,128)(2,1)}), bf16[32,8,640]{2,1,0:T(8,128)(2,1)S(1)}, u32[]{:S(2)}, u32[]{:S(2)}) async-start(bf16[32,8,640]{2,1,0:T(8,128)(2,1)} %get-tuple-element.35), calls=%async_computation | async-start | bytes 655360 | tf_op jit(solution)/shard_map/all_to_all | solution.py:715
  41.5 0.7 %copy-start = (bf16[32,8,640]{2,1,0:T(8,128)(2,1)}, bf16[32,8,640]{2,1,0:T(8,128)(2,1)S(1)}, u32[]{:S(2)}) copy-start(bf16[32,8,640]{2,1,0:T(8,128)(2,1)S(1)} %all-to-all-done.arrived) | copy-start | bytes 983044
  44.3 11.6 %all-to-all-start.1 = ((bf16[32,8,256]{2,1,0:T(8,128)(2,1)}), bf16[32,8,256]{2,1,0:T(8,128)(2,1)S(1)}, u32[]{:S(2)}, u32[]{:S(2)}) async-start(bf16[32,8,256]{2,1,0:T(8,128)(2,1)} %get-tuple-element.39), calls=%async_computation.1 | async-start | bytes 262144 | tf_op jit(solution)/shard_map/all_to_all | solution.py:721
  55.9 0.7 %copy-start.3 = (bf16[32,8,256]{2,1,0:T(8,128)(2,1)}, bf16[32,8,256]{2,1,0:T(8,128)(2,1)S(1)}, u32[]{:S(2)}) copy-start(bf16[32,8,256]{2,1,0:T(8,128)(2,1)S(1)} %all-to-all-done.1.returned) | copy-start | bytes 393220

commit v3 on v2

--- a/solution.py
+++ b/solution.py
@@ -15,10 +15,17 @@
 SURFACE_STEP = 0.5
 MIX = 0.2
 MIB = 1 << 20
-BIG = 56 * MIB
 PARTS = 8
 STEP = 8
 GROUP = 4
+
+
+def in_vmem(*arrays):
+    return [pltpu.with_memory_space_constraint(x, pltpu.VMEM) for x in arrays]
+
+
+def in_hbm(*arrays):
+    return [pltpu.with_memory_space_constraint(x, pltpu.HBM) for x in arrays]
 
 
 def row_swaps(first):
@@ -72,60 +79,60 @@
     edge = pltpu.VMEM((fields * levels, 8, lanes), F32)
     return pl.pallas_call(
         rows_kernel,
-        in_specs=[pl.BlockSpec(memory_space=pl.ANY)],
+        in_specs=[pl.BlockSpec(memory_space=pltpu.HBM)],
         out_specs=[pl.BlockSpec(memory_space=pltpu.VMEM)] * 2,
         out_shape=[out, out],
         scratch_shapes=[edge, edge, pltpu.SemaphoreType.DMA((2,))],
-        compiler_params=pltpu.CompilerParams(vmem_limit_bytes=BIG),
+        compiler_params=pltpu.CompilerParams(vmem_limit_bytes=8 * MIB),
         name="pack_rows",
-    )(air.reshape(fields * levels, rows, lanes))
-
-
-def cols_kernel(air, own_left, own_right, held, sem, chunk):
+    )(*in_hbm(air.reshape(fields * levels, rows, lanes)))
+
+
+def cols_kernel(air, weight, own_left, own_right, lowest, first_half, held, sem, sem_w, chunk):
     fields, levels, rows, lanes = air.shape
     copies = []
     for i in range(levels // chunk):
         part = pl.ds(i * chunk, chunk)
         copies.append(pltpu.make_async_copy(air.at[:, part], held.at[:, part], sem.at[i]))
         copies[i].start()
+    weights = fetch(weight.at[pl.ds(0, first_half.shape[0])], first_half, sem_w)
     pair = lax.broadcasted_iota(jnp.int32, (rows, lanes), 1) >> 1
+    left, right = [[jnp.zeros((rows, lanes), F32)] * fields for _ in range(2)]
     for i in range(levels // chunk):
         copies[i].wait()
-
-        def some(g, carry):
-            out = []
+        if i == 0:
+            lowest[...] = held[:, 0]
+        for level in range(i * chunk, (i + 1) * chunk):
             for field in range(fields):
-                left, right = carry[2 * field : 2 * field + 2]
-                for k in range(4):
-                    level = i * chunk + g * 4 + k
-                    turned = pltpu.roll(held[field, level], 2 * level, axis=1)
-                    left = jnp.where(pair == level, turned, left)
-                    right = jnp.where(pair == (level + levels - 1) % levels, turned, right)
-                out += [left, right]
-            return tuple(out)
-
-        if i == 0:
-            carry = (jnp.zeros((rows, lanes), F32),) * (2 * fields)
-        carry = lax.fori_loop(0, chunk // 4, some, carry)
+                turned = pltpu.roll(held[field, level], 2 * level % lanes, axis=1)
+                left[field] = jnp.where(pair == level, turned, left[field])
+                right[field] = jnp.where(pair == (level - 1) % levels, turned, right[field])
     for field in range(fields):
-        own_left[field] = carry[2 * field]
-        own_right[field] = pltpu.roll(carry[2 * field + 1], 2, axis=1)
-
-
-def pack_cols(air):
+        own_left[field] = left[field]
+        own_right[field] = pltpu.roll(right[field], 2, axis=1)
+    for c in weights:
+        c.wait()
+
+
+def pack_cols(air, weight):
     fields, levels, rows, lanes = air.shape
     chunk = 8
+    vmem = pl.BlockSpec(memory_space=pltpu.VMEM)
     out = jax.ShapeDtypeStruct((fields, rows, lanes), F32)
     return pl.pallas_call(
         functools.partial(cols_kernel, chunk=chunk),
-        in_specs=[pl.BlockSpec(memory_space=pl.ANY)],
-        out_specs=[pl.BlockSpec(memory_space=pltpu.VMEM)] * 2,
-        out_shape=[out, out],
-        scratch_shapes=[pltpu.VMEM(air.shape, F32), pltpu.SemaphoreType.DMA((levels // chunk,))],
-        compiler_params=pltpu.CompilerParams(vmem_limit_bytes=BIG),
+        in_specs=[pl.BlockSpec(memory_space=pltpu.HBM)] * 2,
+        out_specs=[vmem] * 4,
+        out_shape=[out, out, out, pltpu.VMEM((weight.shape[0] // 2, lanes, lanes), BF16)],
+        scratch_shapes=[
+            pltpu.VMEM(air.shape, F32),
+            pltpu.SemaphoreType.DMA((levels // chunk,)),
+            pltpu.SemaphoreType.DMA((PARTS,)),
+        ],
+        compiler_params=pltpu.CompilerParams(vmem_limit_bytes=12 * MIB),
         cost_estimate=pl.CostEstimate(flops=4 * air.size, bytes_accessed=4 * air.size, transcendentals=0),
         name="pack_cols",
-    )(air)
+    )(*in_hbm(air, weight))
 
 
 def with_row(strip, row, first):
@@ -170,7 +177,7 @@
         in_specs=[vmem] * 4,
         out_specs=[vmem] * 2,
         out_shape=[out, out],
-        compiler_params=pltpu.CompilerParams(vmem_limit_bytes=BIG),
+        compiler_params=pltpu.CompilerParams(vmem_limit_bytes=8 * MIB),
         name="strips",
     )(got_a, got_b, own_left, own_right)
 
@@ -228,14 +235,16 @@
 
 def forward_kernel(
     owner, block_row, block_column, air, forcing, surface_temp, got_a, got_b, got_g, got_x,
-    own_left, own_right, weight, payload, slots, source, held, sem, flux_rows, found, tags, counts,
+    own_left, own_right, first_half, weight, payload, slots, source, held, sem, flux_rows, found, tags,
+    counts,
     bound, levels, group,
 ):
     blocks = weight.shape[0]
     rows, lanes = surface_temp.shape
     devices = payload.shape[0]
     total = devices * bound
-    copies = fetch(weight, held, sem)
+    half = held.shape[0]
+    copies = fetch(weight.at[pl.ds(half, half)], held, sem)
     top1, top2, low1, low2 = [jnp.concatenate([h[0:1], h[levels : levels + 1]]) for h in row_halo(got_a, got_b)]
     next_top, next_low = next_rows(top1, top2, low1, low2)
     lowest = []
@@ -243,7 +252,7 @@
         sides0, sides1 = side_strips(field, got_g, got_x, own_left, own_right)
         lowest.append(
             mixed_level(
-                air[field, 0],
+                air[field],
                 *[h[field : field + 1] for h in (top1, next_top, low1, next_low)],
                 pltpu.roll(sides0, lanes - 1, axis=1),
                 pltpu.roll(sides1, lanes - 1, axis=1),
@@ -276,22 +285,22 @@
 
     lax.fori_loop(0, devices, clear, 0)
 
-    def some(first):
+    def some(first, start, half):
         outs = []
         for k in range(0, group, 2):
-            at = first + k
+            at = start + first + k
             picked = [
                 flux_rows[pl.ds(pl.multiple_of(block_column[n] * NF, NF), NF), :] for n in (at, at + 1)
             ]
             out = lax.dot_general(
                 jnp.concatenate(picked).astype(BF16),
-                held[pl.ds(at, 2)].reshape(2 * lanes, lanes),
+                half[pl.ds(first + k, 2)].reshape(2 * lanes, lanes),
                 (((1,), (1,)), ((), ())),
                 preferred_element_type=F32,
             )
             outs += [out[:NF, :lanes], out[NF:, lanes:]]
         for k, out in enumerate(outs):
-            at = first + k
+            at = start + first + k
             to = owner[at]
             rank = counts[to]
             counts[to] = rank + 1
@@ -300,7 +309,10 @@
             found[pl.ds(pl.multiple_of(slot * NF, NF), NF), :] = out
             tags[pl.ds(slot, 1), :] = jnp.full((1, lanes), block_row[at], jnp.int32).astype(F32)
 
-    per_chunk(copies, blocks, group, some)
+    all_of(first_half, 0, group, some)
+    for c in copies:
+        c.wait()
+    all_of(held, half, group, some)
     f = [found[pl.ds(k, total, stride=NF), :] for k in range(NF)]
     heat = (f[0] + f[1]) + (f[4] + f[5])
     heat_hi = heat.astype(BF16).astype(F32)
@@ -322,20 +334,19 @@
     return copies
 
 
-def per_chunk(copies, blocks, group, some):
-    size = blocks // len(copies)
-    for i, copy in enumerate(copies):
-        copy.wait()
-
-        def body(g, carry, start=i * size):
-            some(start + g * group)
-            return carry
-
-        lax.fori_loop(0, size // group, body, 0)
-
-
-def forward(owner, block_row, block_column, air, forcing, surface_temp, halo, own, weight, devices, bound):
-    _, levels, rows, lanes = air.shape
+def all_of(weight, start, group, some):
+    def body(g, carry):
+        some(g * group, start, weight)
+        return carry
+
+    lax.fori_loop(0, weight.shape[0] // group, body, 0)
+
+
+def forward(
+    owner, block_row, block_column, lowest, forcing, surface_temp, halo, own, first_half, weight, levels,
+    devices, bound,
+):
+    _, rows, lanes = lowest.shape
     nonzeros = weight.shape[0]
     smem = pl.BlockSpec(memory_space=pltpu.SMEM)
     vmem = pl.BlockSpec(memory_space=pltpu.VMEM)
@@ -343,11 +354,9 @@
     total = devices * bound
     return pl.pallas_call(
         functools.partial(forward_kernel, bound=bound, levels=levels, group=32),
-        grid=(1,),
         in_specs=[smem, smem, smem]
-        + [pl.BlockSpec((2, 1, rows, lanes), lambda i: (0, 0, 0, 0))]
-        + [vmem for x in args]
-        + [pl.BlockSpec(memory_space=pl.ANY)],
+        + [vmem] * (len(args) + 2)
+        + [pl.BlockSpec(memory_space=pltpu.HBM)],
         out_specs=[vmem, smem, vmem],
         out_shape=[
             jax.ShapeDtypeStruct((devices, bound, SENT * lanes), BF16),
@@ -355,19 +364,19 @@
             jax.ShapeDtypeStruct((2, rows, lanes), F32),
         ],
         scratch_shapes=[
-            pltpu.VMEM(weight.shape, BF16),
+            pltpu.VMEM(first_half.shape, BF16),
             pltpu.SemaphoreType.DMA((PARTS,)),
             pltpu.VMEM((rows * NF, lanes), F32),
             pltpu.VMEM((total * NF, lanes), F32),
             pltpu.VMEM((total, lanes), F32),
             pltpu.SMEM((devices,), jnp.int32),
         ],
-        compiler_params=pltpu.CompilerParams(vmem_limit_bytes=BIG),
+        compiler_params=pltpu.CompilerParams(vmem_limit_bytes=20 * MIB),
         name="forward_blocks",
-    )(owner, block_row, block_column, air, *args, weight)
-
-
-def pivot_kernel(coupling, inverse, held, sem):
+    )(owner, block_row, block_column, lowest, *args, *in_vmem(first_half), *in_hbm(weight))
+
+
+def pivot_kernel(coupling, out, held, inverse, sem, out_sem):
     levels = inverse.shape[0]
     copies = fetch_levels([(coupling, held)], sem, levels - 1)
 
@@ -380,6 +389,7 @@
         inverse[level] = inv
         return inv if last else held[level] * inv
 
+    outs = []
     for i, part in enumerate(copies):
         for c in part:
             c.wait()
@@ -390,7 +400,13 @@
         start = max(1, i * STEP)
         stop = min((i + 1) * STEP, levels - 1)
         ratio = lax.fori_loop(start, stop, one, ratio)
-    one(levels - 1, ratio, True)
+        if stop == levels - 1:
+            one(levels - 1, ratio, True)
+        at = pl.ds(i * STEP, STEP)
+        outs.append(pltpu.make_async_copy(inverse.at[at], out.at[at], out_sem.at[i]))
+        outs[i].start()
+    for c in outs:
+        c.wait()
 
 
 def fetch_levels(pairs, sem, levels, order=1):
@@ -415,14 +431,19 @@
     shape = (levels + 1, rows, lanes)
     return pl.pallas_call(
         pivot_kernel,
-        in_specs=[pl.BlockSpec(memory_space=pl.ANY)],
-        out_specs=pl.BlockSpec(memory_space=pltpu.VMEM),
-        out_shape=jax.ShapeDtypeStruct(shape, F32),
-        scratch_shapes=[pltpu.VMEM(coupling.shape, F32), pltpu.SemaphoreType.DMA(((levels + STEP) // STEP,))],
-        compiler_params=pltpu.CompilerParams(vmem_limit_bytes=BIG),
+        in_specs=[pl.BlockSpec(memory_space=pltpu.HBM)],
+        out_specs=pl.BlockSpec(memory_space=pltpu.HBM),
+        out_shape=pltpu.HBM(shape, F32),
+        scratch_shapes=[
+            pltpu.VMEM(coupling.shape, F32),
+            pltpu.VMEM(shape, F32),
+            pltpu.SemaphoreType.DMA(((levels + STEP) // STEP,)),
+            pltpu.SemaphoreType.DMA(((levels + STEP) // STEP,)),
+        ],
+        compiler_params=pltpu.CompilerParams(vmem_limit_bytes=12 * MIB),
         cost_estimate=pl.CostEstimate(flops=8 * coupling.size, bytes_accessed=8 * coupling.size, transcendentals=0),
         name="pivots",
-    )(coupling)
+    )(*in_hbm(coupling))
 
 
 def beside(block, shifts):
@@ -515,13 +536,13 @@
 def columns_up(air, coupling, inverse, halo, own, source):
     fields, levels, rows, lanes = air.shape
     args = (air, coupling, inverse, *halo, *own, source)
-    hbm = pl.BlockSpec(memory_space=pl.ANY)
+    hbm = pl.BlockSpec(memory_space=pltpu.HBM)
     parts = levels // STEP
     return pl.pallas_call(
         up_kernel,
         in_specs=[hbm] * 3 + [pl.BlockSpec(memory_space=pltpu.VMEM)] * (len(args) - 3),
         out_specs=hbm,
-        out_shape=jax.ShapeDtypeStruct(air.shape, F32),
+        out_shape=pltpu.HBM(air.shape, F32),
         scratch_shapes=[
             pltpu.VMEM(air.shape, F32),
             pltpu.VMEM(coupling.shape, F32),
@@ -535,10 +556,10 @@
             pltpu.SemaphoreType.DMA((3 * parts,)),
             pltpu.SemaphoreType.DMA((parts,)),
         ],
-        compiler_params=pltpu.CompilerParams(vmem_limit_bytes=BIG),
+        compiler_params=pltpu.CompilerParams(vmem_limit_bytes=24 * MIB),
         cost_estimate=pl.CostEstimate(flops=40 * air.size, bytes_accessed=12 * air.size, transcendentals=0),
         name="columns_up",
-    )(*args)
+    )(*in_hbm(*args[:3]), *args[3:])
 
 
 def down_kernel(reduced, coupling, inverse, air_new, held, held_c, held_i, sem, out_sem):
@@ -567,13 +588,13 @@
 
 def columns_down(reduced, coupling, inverse):
     levels = reduced.shape[1]
-    hbm = pl.BlockSpec(memory_space=pl.ANY)
+    hbm = pl.BlockSpec(memory_space=pltpu.HBM)
     parts = levels // STEP
     return pl.pallas_call(
         down_kernel,
         in_specs=[hbm] * 3,
         out_specs=hbm,
-        out_shape=jax.ShapeDtypeStruct(reduced.shape, F32),
+        out_shape=pltpu.HBM(reduced.shape, F32),
         scratch_shapes=[
             pltpu.VMEM(reduced.shape, F32),
             pltpu.VMEM(coupling.shape, F32),
@@ -581,10 +602,10 @@
             pltpu.SemaphoreType.DMA((3 * parts,)),
             pltpu.SemaphoreType.DMA((parts,)),
         ],
-        compiler_params=pltpu.CompilerParams(vmem_limit_bytes=BIG),
+        compiler_params=pltpu.CompilerParams(vmem_limit_bytes=16 * MIB),
         cost_estimate=pl.CostEstimate(flops=8 * reduced.size, bytes_accessed=12 * reduced.size, transcendentals=0),
         name="columns_down",
-    )(reduced, coupling, inverse)
+    )(*in_hbm(reduced, coupling, inverse))
 
 
 def ocean_kernel(arrived, land_mask, ocean_temp, ocean_ice, layer_depth, temp_new, ice_new, replies):
@@ -624,13 +645,13 @@
             jax.ShapeDtypeStruct((blocks, lanes), F32),
             jax.ShapeDtypeStruct((devices, bound, 2 * lanes), BF16),
         ],
-        compiler_params=pltpu.CompilerParams(vmem_limit_bytes=BIG),
+        compiler_params=pltpu.CompilerParams(vmem_limit_bytes=16 * MIB),
         name="ocean",
     )(arrived, land_mask, ocean_temp, ocean_ice, layer_depth)
 
 
 def backward_kernel(slots, block_column, returned, weight, seen, held, sem, pairs, sums, group):
-    blocks, lanes = weight.shape[0], weight.shape[1]
+    lanes = weight.shape[1]
     total = returned.shape[0] * returned.shape[1]
     rows = seen.shape[1]
     copies = fetch(weight, held, sem)
@@ -655,7 +676,15 @@
             place = pl.ds(pl.multiple_of(block_column[first + k] * 8, 8), 8)
             sums[place, :] += out
 
-    per_chunk(copies, blocks, group, some)
+    size = weight.shape[0] // PARTS
+    for i, copy in enumerate(copies):
+        copy.wait()
+
+        def body(g, carry, start=i * size):
+            some(start + g * group)
+            return carry
+
+        lax.fori_loop(0, size // group, body, 0)
     for k in range(2):
         seen[k] = sums[pl.ds(k, rows, stride=8), :]
 
@@ -667,7 +696,7 @@
     vmem = pl.BlockSpec(memory_space=pltpu.VMEM)
     return pl.pallas_call(
         functools.partial(backward_kernel, group=32),
-        in_specs=[smem, smem, vmem, pl.BlockSpec(memory_space=pl.ANY)],
+        in_specs=[smem, smem, vmem, pl.BlockSpec(memory_space=pltpu.HBM)],
         out_specs=vmem,
         out_shape=jax.ShapeDtypeStruct((2, rows, lanes), F32),
         scratch_shapes=[
@@ -676,9 +705,9 @@
             pltpu.VMEM((devices * bound * 8, lanes), F32),
             pltpu.VMEM((rows * 8, lanes), F32),
         ],
-        compiler_params=pltpu.CompilerParams(vmem_limit_bytes=BIG),
+        compiler_params=pltpu.CompilerParams(vmem_limit_bytes=16 * MIB),
         name="backward_blocks",
-    )(slots, block_column, returned, weight)
+    )(slots, block_column, returned, *in_hbm(weight))
 
 
 def local(
@@ -701,7 +730,7 @@
     rows_a, rows_b = pack_rows(air_state)
     got_a = lax.ppermute(rows_a, ALL, row_swaps(0))
     got_b = lax.ppermute(rows_b, ALL, row_swaps(1))
-    own = pack_cols(air_state)
+    *own, lowest, first_half = pack_cols(air_state, remap_weight)
     to_g, to_x = make_strips(got_a, got_b, *own)
     got_x = lax.ppermute(to_x, ("comp", "gy"), col_swaps(1))
     got_g = lax.ppermute(to_g, ("comp", "gy"), col_swaps(0))
@@ -709,8 +738,8 @@
     inverse = pivots(coupling)
     halo, inverse = lax.optimization_barrier((halo, inverse))
     payload, slots, source = forward(
-        block_owner[:, 0], block_row, block_column, air_state, forcing, surface_temp, halo, own,
-        remap_weight, devices, bound,
+        block_owner[:, 0], block_row, block_column, lowest, forcing, surface_temp, halo, own,
+        first_half, remap_weight, air_state.shape[1], devices, bound,
     )
     arrived = lax.all_to_all(payload, ALL, split_axis=0, concat_axis=0, tiled=True)
     reduced = columns_up(air_state, coupling, inverse, halo, own, source)

time: 62.4 us -> 53.2 us (0.85)
  Pallas kernels: 39.9 us -> 33.2 us
  local copies, waits for them, and re-layouts: 2.62 us -> 0.06 us
  waiting for transfers between devices: 5.21 us -> 6.1 us
  starting transfers between devices: 13.4 us -> 12.7 us
    unnamed x12 -> x18, local copies, waits for them, and re-layouts: 2.62 us -> 0.06 us
    pallas_call x1, Pallas kernels: 1.8 us -> 0.24 us  [make_strips(): pl.pallas_call(strips_kernel, in_specs=[vmem] * 4, out_specs=[vmem] * 2,...]
    pallas_call x2, Pallas kernels: 5.29 us -> 4.06 us  [the longest x1 2.78 us: pivots(): pl.pallas_call(pivot_kernel, in_specs=[pl.BlockSpec(memory_space=pltpu.HB...]
    pallas_call x1, Pallas kernels: 6.54 us -> 5.37 us  [forward(): pl.pallas_call(functools.partial(forward_kernel, bound=bound, levels=leve...]
    pallas_call x1, Pallas kernels: 2.15 us -> 1.12 us  [ocean(): pl.pallas_call(ocean_kernel, in_specs=[vmem] * 5, out_specs=[vmem] * 3, o...]
    pallas_call x1, Pallas kernels: 9.23 us -> 8.3 us  [columns_up(): pl.pallas_call(up_kernel, in_specs=[hbm] * 3 + [pl.BlockSpec(memory_space...]
    all_to_all x1, waiting for transfers between devices: 2.46 us -> 3.35 us  [local(): lax.all_to_all(payload, ALL, split_axis=0, concat_axis=0, tiled=True)]
    all_to_all x1, starting transfers between devices: 3.38 us -> 2.57 us  [local(): lax.all_to_all(replies, ALL, split_axis=0, concat_axis=0, tiled=True)]
  transfers between devices with their start and end apart: 6 -> 6, of which waited for: 2 -> 2; matrix products, arithmetic and copies ran while one was open for 0% -> 0% of each run, Pallas kernels for 36% -> 38%
where the time goes in v3:
time: 53.2 us; the launch traced here: 52.9 us
  Pallas kernels  33.2 us (62%)
  starting transfers between devices  12.7 us (24%)
  waiting for transfers between devices  6.1 us (11%)
  between operations  0.85 us (2%)
    pallas_call x1, Pallas kernels, columns_up(): pl.pallas_call(up_kernel, in_specs=[hbm] * 3 + [pl.BlockSpec(memory_space...  8.3 us
    pallas_call x1, Pallas kernels, columns_down(): pl.pallas_call(down_kernel, in_specs=[hbm] * 3, out_specs=hbm, out_shape=...  5.48 us
    all_to_all x1, starting transfers between devices, local(): lax.all_to_all(payload, ALL, split_axis=0, concat_axis=0, tiled=True)  5.37 us
    pallas_call x1, Pallas kernels, forward(): pl.pallas_call(functools.partial(forward_kernel, bound=bound, levels=leve...  5.37 us
    pallas_call x1, Pallas kernels, backward(): pl.pallas_call(functools.partial(backward_kernel, group=32), in_specs=[sm...  4.95 us
    pallas_call x1, Pallas kernels, pack_cols(): pl.pallas_call(functools.partial(cols_kernel, chunk=chunk), in_specs=[pl....  3.64 us
    all_to_all x1, waiting for transfers between devices, local(): lax.all_to_all(payload, ALL, split_axis=0, concat_axis=0, tiled=True)  3.35 us
    ppermute x1, starting transfers between devices, local(): got_a = lax.ppermute(rows_a, ALL, row_swaps(0))  3 us
  transfers between devices with their start and end apart: 6, of which 2 were waited for; matrix products, arithmetic and copies ran while one was open for 0% of the time, Pallas kernels for 38%

profile of v3, /device:TPU:0, one launch (start us, length us, event | category | flops | bytes accessed | tf_op | source)
XLA Modules:
  0.0 52.9 jit_solution(8890487718759417049)
XLA Ops:
  0.6 1.3 %pack_rows.1 = (bf16[128,256]{1,0:T(8,128)(2,1)S(1)}, bf16[128,256]{1,0:T(8,128)(2,1)S(1)}) custom-call(f32[128,64,128]{2,1,0:T(8,128)} %bitcast.3), custom_call_target="tpu_custom_call" | custom-call | tf_op jit(solution)/shard_map/pack_rows/pallas_call | solution.py:80
  1.9 3.0 %collective-permute-start = (bf16[128,256]{1,0:T(8,128)(2,1)S(1)}, bf16[128,256]{1,0:T(8,128)(2,1)S(1)}, u32[]{:S(2)}, u32[]{:S(2)}) collective-permute-start(bf16[128,256]{1,0:T(8,128)(2,1)S(1)} %get-tuple-element.28), channel_id=1, source_target_pairs={{0,2},{1,3},{2,0},{3,1},{4,6},{5,7},{6,4},{7,5},{8,10},{9,11},{10,... | collective-permute-start | bytes 196616 | tf_op jit(solution)/shard_map/ppermute | solution.py:731
  4.9 0.0 collective-permute-start.1
  4.9 3.6 %pack_cols.1 = (f32[2,64,128]{2,1,0:T(8,128)S(1)}, f32[2,64,128]{2,1,0:T(8,128)S(1)}, f32[2,64,128]{2,1,0:T(8,128)S(1)}, bf16[128,128,128]{2,1,0:T(8,128)(2,1)S(1)}) custom-call(f32[2,64,64,128]{3,2,1,0:T(8,128)} %air.3, bf16[256,128,128]{2,1,0:T(8,128)(2,1)} %weight.5), custom_call_target="tpu_custom_call" | custom-call | flops 4194304 | bytes 4194304 | tf_op jit(solution)/shard_map/pack_cols/pallas_call | solution.py:122
  8.6 0.0 copy-start
  8.6 0.0 copy-start.1
  8.6 0.0 copy-start.6
  8.6 0.0 copy-start.7
  8.6 0.0 copy-start.8
  8.6 0.0 collective-permute-done.got_a
  8.6 0.0 collective-permute-done.1.got_b
  8.7 0.2 strips.1
  8.9 0.6 %collective-permute-start.2 = (bf16[2,64,128]{2,1,0:T(8,128)(2,1)S(1)}, bf16[2,64,128]{2,1,0:T(8,128)(2,1)S(1)}, u32[]{:S(2)}, u32[]{:S(2)}) collective-permute-start(bf16[2,64,128]{2,1,0:T(8,128)(2,1)S(1)} %get-tuple-element.32), channel_id=1, source_target_pairs={{0,1},{1,0},{16,17},{17,16},{2,3},{3,2},{18,19},{19,18},{4,5},{5,4... | collective-permute-start | bytes 98312 | tf_op jit(solution)/shard_map/ppermute | solution.py:736
  9.5 1.2 %collective-permute-start.3 = (bf16[2,64,128]{2,1,0:T(8,128)(2,1)S(1)}, bf16[2,64,128]{2,1,0:T(8,128)(2,1)S(1)}, u32[]{:S(2)}, u32[]{:S(2)}) collective-permute-start(bf16[2,64,128]{2,1,0:T(8,128)(2,1)S(1)} %get-tuple-element.33), channel_id=1, source_target_pairs={{0,17},{1,16},{16,1},{17,0},{2,19},{3,18},{18,3},{19,2},{4,21},{5,... | collective-permute-start | bytes 98312 | tf_op jit(solution)/shard_map/ppermute | solution.py:735
  10.7 2.8 %pivots.1.inverse = f32[64,64,128]{2,1,0:T(8,128)} custom-call(f32[63,64,128]{2,1,0:T(8,128)} %coupling.5), custom_call_target="tpu_custom_call" | custom-call | flops 4128768 | bytes 4128768 | tf_op jit(solution)/shard_map/pivots/pallas_call | solution.py:432
  13.5 0.0 collective-permute-done.2.got_g
  13.5 0.0 collective-permute-done.3.got_x
  13.5 0.0 copy-done
  13.5 0.0 copy-done.1
  13.5 0.0 copy-done.6
  13.5 0.0 copy-done.7
  13.5 0.0 copy-done.8
  13.5 5.4 %forward_blocks.1 = (bf16[32,8,640]{2,1,0:T(8,128)(2,1)}, s32[256]{0:T(256)S(1)}, f32[2,64,128]{2,1,0:T(8,128)S(1)}) custom-call(s32[256]{0:T(256)S(1)} %bitcast.2, s32[256]{0:T(256)S(1)} %copy-done.8, s32[256]{0:T(256)S(1)} %copy-done.6, f32[2,64,128]{2,1,0:T(8,128)S(1)} %get-tuple-element.27.air, f32[6,64,128]{2,1,0:T(8,128)S(1)} %copy-done, ...), custom_call_target="tpu_custom_call" | custom-call | tf_op jit(solution)/shard_map/forward_blocks/pallas_call | solution.py:355
  18.9 5.4 %all-to-all-start = ((bf16[32,8,640]{2,1,0:T(8,128)(2,1)}), bf16[32,8,640]{2,1,0:T(8,128)(2,1)S(1)}, u32[]{:S(2)}, u32[]{:S(2)}) async-start(bf16[32,8,640]{2,1,0:T(8,128)(2,1)} %get-tuple-element.39), calls=%async_computation | async-start | bytes 655360 | tf_op jit(solution)/shard_map/all_to_all | solution.py:744
  24.3 0.0 copy-start.2
  24.3 0.0 copy-start.3
  24.3 0.0 copy-start.4
  24.3 0.0 copy-start.5
  24.3 8.3 %columns_up.1.reduced = f32[2,64,64,128]{3,2,1,0:T(8,128)} custom-call(f32[2,64,64,128]{3,2,1,0:T(8,128)} %air.3, f32[63,64,128]{2,1,0:T(8,128)} %coupling.5, f32[64,64,128]{2,1,0:T(8,128)} %pivots.1.inverse, bf16[128,256]{1,0:T(8,128)(2,1)S(1)} %collective-permute-done.got_a, bf16[128,256]{1,0:T(8,128)(2,1)S(1)} %collective-permute-done.1.got_b, ...), custom_call_target="tpu_custom_call" | custom-call | flops 41943040 | bytes 12582912 | tf_op jit(solution)/shard_map/columns_up/pallas_call | solution.py:541
  32.6 3.3 %all-to-all-done.arrived = bf16[32,8,640]{2,1,0:T(8,128)(2,1)S(1)} async-done(((bf16[32,8,640]{2,1,0:T(8,128)(2,1)}), bf16[32,8,640]{2,1,0:T(8,128)(2,1)S(1)}, u32[]{:S(2)}, u32[]{:S(2)}) %all-to-all-start) | async-done | bytes 327712 | tf_op jit(solution)/shard_map/all_to_all | solution.py:744
  36.0 0.0 copy-done.2
  36.0 0.0 copy-done.3
  36.0 0.0 copy-done.4
  36.0 0.0 copy-done.5
  36.0 1.1 %ocean.1 = (f32[64,128]{1,0:T(8,128)}, f32[64,128]{1,0:T(8,128)}, bf16[32,8,256]{2,1,0:T(8,128)(2,1)}) custom-call(bf16[32,8,640]{2,1,0:T(8,128)(2,1)S(1)} %all-to-all-done.arrived, s32[64,128]{1,0:T(8,128)S(1)} %copy-done.2, f32[64,128]{1,0:T(8,128)S(1)} %copy-done.3, f32[64,128]{1,0:T(8,128)S(1)} %copy-done.4, f32[64,128]{1,0:T(8,128)S(1)} %copy-done.5), custom_call_target="tpu_custom_call" | custom-call | tf_op jit(solution)/shard_map/ocean/pallas_call | solution.py:639
  37.1 2.6 %all-to-all-start.1 = ((bf16[32,8,256]{2,1,0:T(8,128)(2,1)}), bf16[32,8,256]{2,1,0:T(8,128)(2,1)S(1)}, u32[]{:S(2)}, u32[]{:S(2)}) async-start(bf16[32,8,256]{2,1,0:T(8,128)(2,1)} %get-tuple-element.43), calls=%async_computation.1 | async-start | bytes 262144 | tf_op jit(solution)/shard_map/all_to_all | solution.py:750
  39.7 5.5 %columns_down.1 = f32[2,64,64,128]{3,2,1,0:T(8,128)} custom-call(f32[2,64,64,128]{3,2,1,0:T(8,128)} %columns_up.1.reduced, f32[63,64,128]{2,1,0:T(8,128)} %coupling.5, f32[64,64,128]{2,1,0:T(8,128)} %pivots.1.inverse), custom_call_target="tpu_custom_call" | custom-call | flops 8388608 | bytes 12582912 | tf_op jit(solution)/shard_map/columns_down/pallas_call | solution.py:593
  45.2 2.7 %all-to-all-done.1.returned = bf16[32,8,256]{2,1,0:T(8,128)(2,1)S(1)} async-done(((bf16[32,8,256]{2,1,0:T(8,128)(2,1)}), bf16[32,8,256]{2,1,0:T(8,128)(2,1)S(1)}, u32[]{:S(2)}, u32[]{:S(2)}) %all-to-all-start.1) | async-done | bytes 131104 | tf_op jit(solution)/shard_map/all_to_all | solution.py:750
  47.9 5.0 %backward_blocks.1 = f32[2,64,128]{2,1,0:T(8,128)} custom-call(s32[256]{0:T(256)S(1)} %get-tuple-element.46.slots, s32[256]{0:T(256)S(1)} %copy-done.6, bf16[32,8,256]{2,1,0:T(8,128)(2,1)S(1)} %all-to-all-done.1.returned, bf16[256,128,128]{2,1,0:T(8,128)(2,1)} %weight.5), custom_call_target="tpu_custom_call" | custom-call | tf_op jit(solution)/shard_map/backward_blocks/pallas_call | solution.py:697
Async XLA Ops:
  1.9 6.7 %collective-permute-start = (bf16[128,256]{1,0:T(8,128)(2,1)S(1)}, bf16[128,256]{1,0:T(8,128)(2,1)S(1)}, u32[]{:S(2)}, u32[]{:S(2)}) collective-permute-start(bf16[128,256]{1,0:T(8,128)(2,1)S(1)} %get-tuple-element.28), channel_id=1, source_target_pairs={{0,2},{1,3},{2,0},{3,1},{4,6},{5,7},{6,4},{7,5},{8,10},{9,11},{10,... | collective-permute-start | bytes 196616 | tf_op jit(solution)/shard_map/ppermute | solution.py:731
  4.9 3.7 %collective-permute-start.1 = (bf16[128,256]{1,0:T(8,128)(2,1)S(1)}, bf16[128,256]{1,0:T(8,128)(2,1)S(1)}, u32[]{:S(2)}, u32[]{:S(2)}) collective-permute-start(bf16[128,256]{1,0:T(8,128)(2,1)S(1)} %get-tuple-element.29), channel_id=1, source_target_pairs={{0,1},{1,0},{2,4},{3,5},{4,2},{5,3},{6,8},{7,9},{8,6},{9,7},{10,12... | collective-permute-start | bytes 196616 | tf_op jit(solution)/shard_map/ppermute | solution.py:732
  8.6 4.9 %copy-start = (f32[6,64,128]{2,1,0:T(8,128)S(1)}, f32[6,64,128]{2,1,0:T(8,128)}, u32[]{:S(2)}) copy-start(f32[6,64,128]{2,1,0:T(8,128)} %forcing.1) | copy-start | bytes 589828
  8.6 4.9 %copy-start.1 = (f32[64,128]{1,0:T(8,128)S(1)}, f32[64,128]{1,0:T(8,128)}, u32[]{:S(2)}) copy-start(f32[64,128]{1,0:T(8,128)} %surface_temp.1) | copy-start | bytes 98308
  8.6 4.9 %copy-start.6 = (s32[256]{0:T(256)S(1)}, s32[256]{0:T(256)}, u32[]{:S(2)}) copy-start(s32[256]{0:T(256)} %block_column.3) | copy-start | bytes 3076
  8.6 4.9 %copy-start.7 = (s32[256,1]{0,1:T(1,128)S(1)}, s32[256,1]{0,1:T(1,128)}, u32[]{:S(2)}) copy-start(s32[256,1]{0,1:T(1,128)} %param.17) | copy-start | bytes 3076
  8.6 4.9 %copy-start.8 = (s32[256]{0:T(256)S(1)}, s32[256]{0:T(256)}, u32[]{:S(2)}) copy-start(s32[256]{0:T(256)} %block_row.1) | copy-start | bytes 3076
  8.9 4.6 %collective-permute-start.2 = (bf16[2,64,128]{2,1,0:T(8,128)(2,1)S(1)}, bf16[2,64,128]{2,1,0:T(8,128)(2,1)S(1)}, u32[]{:S(2)}, u32[]{:S(2)}) collective-permute-start(bf16[2,64,128]{2,1,0:T(8,128)(2,1)S(1)} %get-tuple-element.32), channel_id=1, source_target_pairs={{0,1},{1,0},{16,17},{17,16},{2,3},{3,2},{18,19},{19,18},{4,5},{5,4... | collective-permute-start | bytes 98312 | tf_op jit(solution)/shard_map/ppermute | solution.py:736
  9.5 4.0 %collective-permute-start.3 = (bf16[2,64,128]{2,1,0:T(8,128)(2,1)S(1)}, bf16[2,64,128]{2,1,0:T(8,128)(2,1)S(1)}, u32[]{:S(2)}, u32[]{:S(2)}) collective-permute-start(bf16[2,64,128]{2,1,0:T(8,128)(2,1)S(1)} %get-tuple-element.33), channel_id=1, source_target_pairs={{0,17},{1,16},{16,1},{17,0},{2,19},{3,18},{18,3},{19,2},{4,21},{5,... | collective-permute-start | bytes 98312 | tf_op jit(solution)/shard_map/ppermute | solution.py:735
  18.9 17.1 %all-to-all-start = ((bf16[32,8,640]{2,1,0:T(8,128)(2,1)}), bf16[32,8,640]{2,1,0:T(8,128)(2,1)S(1)}, u32[]{:S(2)}, u32[]{:S(2)}) async-start(bf16[32,8,640]{2,1,0:T(8,128)(2,1)} %get-tuple-element.39), calls=%async_computation | async-start | bytes 655360 | tf_op jit(solution)/shard_map/all_to_all | solution.py:744
  24.3 11.7 %copy-start.2 = (s32[64,128]{1,0:T(8,128)S(1)}, s32[64,128]{1,0:T(8,128)}, u32[]{:S(2)}) copy-start(s32[64,128]{1,0:T(8,128)} %land_mask.1) | copy-start | bytes 98308
  24.3 11.7 %copy-start.3 = (f32[64,128]{1,0:T(8,128)S(1)}, f32[64,128]{1,0:T(8,128)}, u32[]{:S(2)}) copy-start(f32[64,128]{1,0:T(8,128)} %ocean_temp.1) | copy-start | bytes 98308
  24.3 11.7 %copy-start.4 = (f32[64,128]{1,0:T(8,128)S(1)}, f32[64,128]{1,0:T(8,128)}, u32[]{:S(2)}) copy-start(f32[64,128]{1,0:T(8,128)} %ocean_ice.1) | copy-start | bytes 98308
  24.3 11.7 %copy-start.5 = (f32[64,128]{1,0:T(8,128)S(1)}, f32[64,128]{1,0:T(8,128)}, u32[]{:S(2)}) copy-start(f32[64,128]{1,0:T(8,128)} %layer_depth.1) | copy-start | bytes 98308
  37.1 10.8 %all-to-all-start.1 = ((bf16[32,8,256]{2,1,0:T(8,128)(2,1)}), bf16[32,8,256]{2,1,0:T(8,128)(2,1)S(1)}, u32[]{:S(2)}, u32[]{:S(2)}) async-start(bf16[32,8,256]{2,1,0:T(8,128)(2,1)} %get-tuple-element.43), calls=%async_computation.1 | async-start | bytes 262144 | tf_op jit(solution)/shard_map/all_to_all | solution.py:750

commit v4 on v3

--- a/solution.py
+++ b/solution.py
@@ -18,6 +18,7 @@
 PARTS = 8
 STEP = 8
 GROUP = 4
+LAG = 8
 
 
 def in_vmem(*arrays):
@@ -234,9 +235,9 @@
 
 
 def forward_kernel(
-    owner, block_row, block_column, air, forcing, surface_temp, got_a, got_b, got_g, got_x,
-    own_left, own_right, first_half, weight, payload, slots, source, held, sem, flux_rows, found, tags,
-    counts,
+    owner_far, row_far, column_far, air, forcing, surface_temp, got_a, got_b, got_g, got_x,
+    own_left, own_right, first_half, weight, payload, slots_far, source, held, sem, flux_rows, found, tags,
+    counts, owner, block_row, block_column, slots, sem_i,
     bound, levels, group,
 ):
     blocks = weight.shape[0]
@@ -245,6 +246,7 @@
     total = devices * bound
     half = held.shape[0]
     copies = fetch(weight.at[pl.ds(half, half)], held, sem)
+    indices = fetch_indices((owner_far, row_far, column_far), (owner, block_row, block_column), sem_i)
     top1, top2, low1, low2 = [jnp.concatenate([h[0:1], h[levels : levels + 1]]) for h in row_halo(got_a, got_b)]
     next_top, next_low = next_rows(top1, top2, low1, low2)
     lowest = []
@@ -284,9 +286,21 @@
         return 0
 
     lax.fori_loop(0, devices, clear, 0)
+    for c in indices:
+        c.wait()
+
+    def place(pair):
+        for at, out in pair:
+            to = owner[at]
+            rank = counts[to]
+            counts[to] = rank + 1
+            slot = to * bound + rank
+            slots[at] = slot
+            found[pl.ds(pl.multiple_of(slot * NF, NF), NF), :] = out
+            tags[pl.ds(slot, 1), :] = jnp.full((1, lanes), block_row[at], jnp.int32).astype(F32)
 
     def some(first, start, half):
-        outs = []
+        waiting = []
         for k in range(0, group, 2):
             at = start + first + k
             picked = [
@@ -298,21 +312,17 @@
                 (((1,), (1,)), ((), ())),
                 preferred_element_type=F32,
             )
-            outs += [out[:NF, :lanes], out[NF:, lanes:]]
-        for k, out in enumerate(outs):
-            at = start + first + k
-            to = owner[at]
-            rank = counts[to]
-            counts[to] = rank + 1
-            slot = to * bound + rank
-            slots[at] = slot
-            found[pl.ds(pl.multiple_of(slot * NF, NF), NF), :] = out
-            tags[pl.ds(slot, 1), :] = jnp.full((1, lanes), block_row[at], jnp.int32).astype(F32)
+            waiting.append(((at, out[:NF, :lanes]), (at + 1, out[NF:, lanes:])))
+            if len(waiting) > LAG:
+                place(waiting.pop(0))
+        for pair in waiting:
+            place(pair)
 
     all_of(first_half, 0, group, some)
     for c in copies:
         c.wait()
     all_of(held, half, group, some)
+    (kept,) = fetch_indices((slots,), (slots_far,), sem_i)
     f = [found[pl.ds(k, total, stride=NF), :] for k in range(NF)]
     heat = (f[0] + f[1]) + (f[4] + f[5])
     heat_hi = heat.astype(BF16).astype(F32)
@@ -321,6 +331,7 @@
     shape = payload.shape[:2] + (lanes,)
     for k, part in enumerate((heat_hi, heat_lo, f[2], f[3], f[6] - f[7])):
         payload[:, :, k * lanes : (k + 1) * lanes] = part.reshape(shape).astype(BF16)
+    kept.wait()
 
 
 def fetch(source, held, sem):
@@ -334,6 +345,13 @@
     return copies
 
 
+def fetch_indices(sources, targets, sem):
+    copies = [pltpu.make_async_copy(a, b, sem.at[i]) for i, (a, b) in enumerate(zip(sources, targets))]
+    for c in copies:
+        c.start()
+    return copies
+
+
 def all_of(weight, start, group, some):
     def body(g, carry):
         some(g * group, start, weight)
@@ -348,19 +366,19 @@
 ):
     _, rows, lanes = lowest.shape
     nonzeros = weight.shape[0]
-    smem = pl.BlockSpec(memory_space=pltpu.SMEM)
+    hbm = pl.BlockSpec(memory_space=pltpu.HBM)
     vmem = pl.BlockSpec(memory_space=pltpu.VMEM)
     args = (forcing, surface_temp, *halo, *own)
     total = devices * bound
     return pl.pallas_call(
-        functools.partial(forward_kernel, bound=bound, levels=levels, group=32),
-        in_specs=[smem, smem, smem]
+        functools.partial(forward_kernel, bound=bound, levels=levels, group=128),
+        in_specs=[hbm, hbm, hbm]
         + [vmem] * (len(args) + 2)
         + [pl.BlockSpec(memory_space=pltpu.HBM)],
-        out_specs=[vmem, smem, vmem],
+        out_specs=[vmem, hbm, vmem],
         out_shape=[
             jax.ShapeDtypeStruct((devices, bound, SENT * lanes), BF16),
-            jax.ShapeDtypeStruct((nonzeros,), jnp.int32),
+            pltpu.HBM((nonzeros,), jnp.int32),
             jax.ShapeDtypeStruct((2, rows, lanes), F32),
         ],
         scratch_shapes=[
@@ -370,10 +388,15 @@
             pltpu.VMEM((total * NF, lanes), F32),
             pltpu.VMEM((total, lanes), F32),
             pltpu.SMEM((devices,), jnp.int32),
+            pltpu.SMEM((nonzeros,), jnp.int32),
+            pltpu.SMEM((nonzeros,), jnp.int32),
+            pltpu.SMEM((nonzeros,), jnp.int32),
+            pltpu.SMEM((nonzeros,), jnp.int32),
+            pltpu.SemaphoreType.DMA((3,)),
         ],
         compiler_params=pltpu.CompilerParams(vmem_limit_bytes=20 * MIB),
         name="forward_blocks",
-    )(owner, block_row, block_column, lowest, *args, *in_vmem(first_half), *in_hbm(weight))
+    )(*in_hbm(owner, block_row, block_column), lowest, *args, *in_vmem(first_half), *in_hbm(weight))
 
 
 def pivot_kernel(coupling, out, held, inverse, sem, out_sem):
@@ -650,41 +673,42 @@
     )(arrived, land_mask, ocean_temp, ocean_ice, layer_depth)
 
 
-def backward_kernel(slots, block_column, returned, weight, seen, held, sem, pairs, sums, group):
+def backward_kernel(
+    slots_far, column_far, returned, weight, seen, held, sem, pairs, sums, slots, block_column, sem_i
+):
     lanes = weight.shape[1]
     total = returned.shape[0] * returned.shape[1]
     rows = seen.shape[1]
     copies = fetch(weight, held, sem)
+    indices = fetch_indices((slots_far, column_far), (slots, block_column), sem_i)
     pairs[...] = jnp.zeros_like(pairs)
     sums[...] = jnp.zeros_like(sums)
     for k in range(2):
         part = returned[:, :, k * lanes : (k + 1) * lanes].astype(F32).reshape(total, lanes)
         pairs[pl.ds(k, total, stride=8), :] = part
 
-    def some(first):
-        outs = []
-        for k in range(0, group, 2):
-            at = first + k
-            picked = [pairs[pl.ds(pl.multiple_of(slots[n] * 8, 8), 8), :] for n in (at, at + 1)]
-            out = jnp.dot(
-                jnp.concatenate(picked).astype(BF16),
-                jnp.concatenate([held[at], held[at + 1]], axis=1),
-                preferred_element_type=F32,
-            )
-            outs += [out[:8, :lanes], out[8:, lanes:]]
-        for k, out in enumerate(outs):
-            place = pl.ds(pl.multiple_of(block_column[first + k] * 8, 8), 8)
-            sums[place, :] += out
+    def place(pair):
+        for at, out in pair:
+            sums[pl.ds(pl.multiple_of(block_column[at] * 8, 8), 8), :] += out
 
     size = weight.shape[0] // PARTS
-    for i, copy in enumerate(copies):
-        copy.wait()
-
-        def body(g, carry, start=i * size):
-            some(start + g * group)
-            return carry
-
-        lax.fori_loop(0, size // group, body, 0)
+    for c in indices:
+        c.wait()
+    waiting = []
+    for at in range(0, weight.shape[0], 2):
+        if at % size == 0:
+            copies[at // size].wait()
+        picked = [pairs[pl.ds(pl.multiple_of(slots[n] * 8, 8), 8), :] for n in (at, at + 1)]
+        out = jnp.dot(
+            jnp.concatenate(picked).astype(BF16),
+            jnp.concatenate([held[at], held[at + 1]], axis=1),
+            preferred_element_type=F32,
+        )
+        waiting.append(((at, out[:8, :lanes]), (at + 1, out[8:, lanes:])))
+        if len(waiting) > LAG:
+            place(waiting.pop(0))
+    for pair in waiting:
+        place(pair)
     for k in range(2):
         seen[k] = sums[pl.ds(k, rows, stride=8), :]
 
@@ -692,11 +716,11 @@
 def backward(slots, block_column, returned, weight, rows):
     devices, bound, _ = returned.shape
     nonzeros, lanes, _ = weight.shape
-    smem = pl.BlockSpec(memory_space=pltpu.SMEM)
+    hbm = pl.BlockSpec(memory_space=pltpu.HBM)
     vmem = pl.BlockSpec(memory_space=pltpu.VMEM)
     return pl.pallas_call(
-        functools.partial(backward_kernel, group=32),
-        in_specs=[smem, smem, vmem, pl.BlockSpec(memory_space=pltpu.HBM)],
+        backward_kernel,
+        in_specs=[hbm, hbm, vmem, hbm],
         out_specs=vmem,
         out_shape=jax.ShapeDtypeStruct((2, rows, lanes), F32),
         scratch_shapes=[
@@ -704,10 +728,13 @@
             pltpu.SemaphoreType.DMA((PARTS,)),
             pltpu.VMEM((devices * bound * 8, lanes), F32),
             pltpu.VMEM((rows * 8, lanes), F32),
+            pltpu.SMEM(slots.shape, jnp.int32),
+            pltpu.SMEM(slots.shape, jnp.int32),
+            pltpu.SemaphoreType.DMA((2,)),
         ],
         compiler_params=pltpu.CompilerParams(vmem_limit_bytes=16 * MIB),
         name="backward_blocks",
-    )(slots, block_column, returned, *in_hbm(weight))
+    )(*in_hbm(slots, block_column), returned, *in_hbm(weight))
 
 
 def local(
@@ -728,8 +755,8 @@
     nonzeros = remap_weight.shape[0]
     bound = max(4, (nonzeros + devices - 1) // devices)
     rows_a, rows_b = pack_rows(air_state)
+    got_b = lax.ppermute(rows_b, ALL, row_swaps(1))
     got_a = lax.ppermute(rows_a, ALL, row_swaps(0))
-    got_b = lax.ppermute(rows_b, ALL, row_swaps(1))
     *own, lowest, first_half = pack_cols(air_state, remap_weight)
     to_g, to_x = make_strips(got_a, got_b, *own)
     got_x = lax.ppermute(to_x, ("comp", "gy"), col_swaps(1))

time: 53.2 us -> 52.2 us (0.981)
  Pallas kernels: 33.2 us -> 32.3 us
  transfers between devices with their start and end apart: 6 -> 6, of which waited for: 2 -> 2; matrix products, arithmetic and copies ran while one was open for 0% -> 0% of each run, Pallas kernels for 38% -> 39%
where the time goes in v4:
time: 52.2 us; the launch traced here: 51.9 us
  Pallas kernels  32.3 us (62%)
  starting transfers between devices  12.7 us (24%)
  waiting for transfers between devices  6.09 us (12%)
  between operations  0.81 us (2%)
    pallas_call x1, Pallas kernels, columns_up(): pl.pallas_call(up_kernel, in_specs=[hbm] * 3 + [pl.BlockSpec(memory_space...  8.3 us
    pallas_call x1, Pallas kernels, columns_down(): pl.pallas_call(down_kernel, in_specs=[hbm] * 3, out_specs=hbm, out_shape=...  5.48 us
    all_to_all x1, starting transfers between devices, local(): lax.all_to_all(payload, ALL, split_axis=0, concat_axis=0, tiled=True)  5.37 us
    pallas_call x1, Pallas kernels, forward(): pl.pallas_call(functools.partial(forward_kernel, bound=bound, levels=leve...  4.96 us
    pallas_call x1, Pallas kernels, backward(): pl.pallas_call(backward_kernel, in_specs=[hbm, hbm, vmem, hbm], out_specs...  4.46 us
    pallas_call x1, Pallas kernels, pack_cols(): pl.pallas_call(functools.partial(cols_kernel, chunk=chunk), in_specs=[pl....  3.64 us
    all_to_all x1, waiting for transfers between devices, local(): lax.all_to_all(payload, ALL, split_axis=0, concat_axis=0, tiled=True)  3.34 us
    ppermute x1, starting transfers between devices, local(): got_a = lax.ppermute(rows_a, ALL, row_swaps(0))  3 us
  transfers between devices with their start and end apart: 6, of which 2 were waited for; matrix products, arithmetic and copies ran while one was open for 0% of the time, Pallas kernels for 39%

profile of v4, /device:TPU:0, one launch (start us, length us, event | category | flops | bytes accessed | tf_op | source)
XLA Modules:
  0.0 51.9 jit_solution(15575260286233452083)
XLA Ops:
  0.6 1.3 %pack_rows.1 = (bf16[128,256]{1,0:T(8,128)(2,1)S(1)}, bf16[128,256]{1,0:T(8,128)(2,1)S(1)}) custom-call(f32[128,64,128]{2,1,0:T(8,128)} %bitcast.2), custom_call_target="tpu_custom_call" | custom-call | tf_op jit(solution)/shard_map/pack_rows/pallas_call | solution.py:81
  1.9 3.0 %collective-permute-start = (bf16[128,256]{1,0:T(8,128)(2,1)S(1)}, bf16[128,256]{1,0:T(8,128)(2,1)S(1)}, u32[]{:S(2)}, u32[]{:S(2)}) collective-permute-start(bf16[128,256]{1,0:T(8,128)(2,1)S(1)} %get-tuple-element.28), channel_id=1, source_target_pairs={{0,2},{1,3},{2,0},{3,1},{4,6},{5,7},{6,4},{7,5},{8,10},{9,11},{10,... | collective-permute-start | bytes 196616 | tf_op jit(solution)/shard_map/ppermute | solution.py:759
  4.9 0.0 collective-permute-start.1
  4.9 3.6 %pack_cols.1 = (f32[2,64,128]{2,1,0:T(8,128)S(1)}, f32[2,64,128]{2,1,0:T(8,128)S(1)}, f32[2,64,128]{2,1,0:T(8,128)S(1)}, bf16[128,128,128]{2,1,0:T(8,128)(2,1)S(1)}) custom-call(f32[2,64,64,128]{3,2,1,0:T(8,128)} %air.3, bf16[256,128,128]{2,1,0:T(8,128)(2,1)} %weight.5), custom_call_target="tpu_custom_call" | custom-call | flops 4194304 | bytes 4194304 | tf_op jit(solution)/shard_map/pack_cols/pallas_call | solution.py:123
  8.6 0.0 copy-start
  8.6 0.0 copy-start.1
  8.6 0.0 collective-permute-done.got_a
  8.6 0.0 collective-permute-done.1.got_b
  8.6 0.2 strips.1
  8.9 0.6 %collective-permute-start.2 = (bf16[2,64,128]{2,1,0:T(8,128)(2,1)S(1)}, bf16[2,64,128]{2,1,0:T(8,128)(2,1)S(1)}, u32[]{:S(2)}, u32[]{:S(2)}) collective-permute-start(bf16[2,64,128]{2,1,0:T(8,128)(2,1)S(1)} %get-tuple-element.32), channel_id=1, source_target_pairs={{0,1},{1,0},{16,17},{17,16},{2,3},{3,2},{18,19},{19,18},{4,5},{5,4... | collective-permute-start | bytes 98312 | tf_op jit(solution)/shard_map/ppermute | solution.py:763
  9.4 1.2 %collective-permute-start.3 = (bf16[2,64,128]{2,1,0:T(8,128)(2,1)S(1)}, bf16[2,64,128]{2,1,0:T(8,128)(2,1)S(1)}, u32[]{:S(2)}, u32[]{:S(2)}) collective-permute-start(bf16[2,64,128]{2,1,0:T(8,128)(2,1)S(1)} %get-tuple-element.33), channel_id=1, source_target_pairs={{0,17},{1,16},{16,1},{17,0},{2,19},{3,18},{18,3},{19,2},{4,21},{5,... | collective-permute-start | bytes 98312 | tf_op jit(solution)/shard_map/ppermute | solution.py:762
  10.6 2.8 %pivots.1.inverse = f32[64,64,128]{2,1,0:T(8,128)} custom-call(f32[63,64,128]{2,1,0:T(8,128)} %coupling.5), custom_call_target="tpu_custom_call" | custom-call | flops 4128768 | bytes 4128768 | tf_op jit(solution)/shard_map/pivots/pallas_call | solution.py:455
  13.5 0.0 collective-permute-done.2.got_g
  13.5 0.0 collective-permute-done.3.got_x
  13.5 0.0 copy-done
  13.5 0.0 copy-done.1
  13.5 5.0 %forward_blocks.1 = (bf16[32,8,640]{2,1,0:T(8,128)(2,1)}, s32[256]{0:T(256)}, f32[2,64,128]{2,1,0:T(8,128)S(1)}) custom-call(s32[256]{0:T(256)} %bitcast.3, s32[256]{0:T(256)} %row_far.1, s32[256]{0:T(256)} %column_far.3, f32[2,64,128]{2,1,0:T(8,128)S(1)} %get-tuple-element.27.air, f32[6,64,128]{2,1,0:T(8,128)S(1)} %copy-done, f32[64,128]{1,0:T(8,128)S(1)} %copy-done.1, ...), custom_call_target="tpu_custom_call" | custom-call | tf_op jit(solution)/shard_map/forward_blocks/pallas_call | solution.py:373
  18.5 5.4 %all-to-all-start = ((bf16[32,8,640]{2,1,0:T(8,128)(2,1)}), bf16[32,8,640]{2,1,0:T(8,128)(2,1)S(1)}, u32[]{:S(2)}, u32[]{:S(2)}) async-start(bf16[32,8,640]{2,1,0:T(8,128)(2,1)} %get-tuple-element.39), calls=%async_computation | async-start | bytes 655360 | tf_op jit(solution)/shard_map/all_to_all | solution.py:771
  23.8 0.0 copy-start.2
  23.9 0.0 copy-start.3
  23.9 0.0 copy-start.4
  23.9 0.0 copy-start.5
  23.9 8.3 %columns_up.1.reduced = f32[2,64,64,128]{3,2,1,0:T(8,128)} custom-call(f32[2,64,64,128]{3,2,1,0:T(8,128)} %air.3, f32[63,64,128]{2,1,0:T(8,128)} %coupling.5, f32[64,64,128]{2,1,0:T(8,128)} %pivots.1.inverse, bf16[128,256]{1,0:T(8,128)(2,1)S(1)} %collective-permute-done.got_a, bf16[128,256]{1,0:T(8,128)(2,1)S(1)} %collective-permute-done.1.got_b, ...), custom_call_target="tpu_custom_call" | custom-call | flops 41943040 | bytes 12582912 | tf_op jit(solution)/shard_map/columns_up/pallas_call | solution.py:564
  32.2 3.3 %all-to-all-done.arrived = bf16[32,8,640]{2,1,0:T(8,128)(2,1)S(1)} async-done(((bf16[32,8,640]{2,1,0:T(8,128)(2,1)}), bf16[32,8,640]{2,1,0:T(8,128)(2,1)S(1)}, u32[]{:S(2)}, u32[]{:S(2)}) %all-to-all-start) | async-done | bytes 327712 | tf_op jit(solution)/shard_map/all_to_all | solution.py:771
  35.5 0.0 copy-done.2
  35.5 0.0 copy-done.3
  35.5 0.0 copy-done.4
  35.6 0.0 copy-done.5
  35.6 1.1 %ocean.1 = (f32[64,128]{1,0:T(8,128)}, f32[64,128]{1,0:T(8,128)}, bf16[32,8,256]{2,1,0:T(8,128)(2,1)}) custom-call(bf16[32,8,640]{2,1,0:T(8,128)(2,1)S(1)} %all-to-all-done.arrived, s32[64,128]{1,0:T(8,128)S(1)} %copy-done.2, f32[64,128]{1,0:T(8,128)S(1)} %copy-done.3, f32[64,128]{1,0:T(8,128)S(1)} %copy-done.4, f32[64,128]{1,0:T(8,128)S(1)} %copy-done.5), custom_call_target="tpu_custom_call" | custom-call | tf_op jit(solution)/shard_map/ocean/pallas_call | solution.py:662
  36.7 2.6 %all-to-all-start.1 = ((bf16[32,8,256]{2,1,0:T(8,128)(2,1)}), bf16[32,8,256]{2,1,0:T(8,128)(2,1)S(1)}, u32[]{:S(2)}, u32[]{:S(2)}) async-start(bf16[32,8,256]{2,1,0:T(8,128)(2,1)} %get-tuple-element.43), calls=%async_computation.1 | async-start | bytes 262144 | tf_op jit(solution)/shard_map/all_to_all | solution.py:777
  39.2 5.5 %columns_down.1 = f32[2,64,64,128]{3,2,1,0:T(8,128)} custom-call(f32[2,64,64,128]{3,2,1,0:T(8,128)} %columns_up.1.reduced, f32[63,64,128]{2,1,0:T(8,128)} %coupling.5, f32[64,64,128]{2,1,0:T(8,128)} %pivots.1.inverse), custom_call_target="tpu_custom_call" | custom-call | flops 8388608 | bytes 12582912 | tf_op jit(solution)/shard_map/columns_down/pallas_call | solution.py:616
  44.7 2.7 %all-to-all-done.1.returned = bf16[32,8,256]{2,1,0:T(8,128)(2,1)S(1)} async-done(((bf16[32,8,256]{2,1,0:T(8,128)(2,1)}), bf16[32,8,256]{2,1,0:T(8,128)(2,1)S(1)}, u32[]{:S(2)}, u32[]{:S(2)}) %all-to-all-start.1) | async-done | bytes 131104 | tf_op jit(solution)/shard_map/all_to_all | solution.py:777
  47.5 4.5 %backward_blocks.1 = f32[2,64,128]{2,1,0:T(8,128)} custom-call(s32[256]{0:T(256)} %get-tuple-element.46.slots_far, s32[256]{0:T(256)} %column_far.3, bf16[32,8,256]{2,1,0:T(8,128)(2,1)S(1)} %all-to-all-done.1.returned, bf16[256,128,128]{2,1,0:T(8,128)(2,1)} %weight.5), custom_call_target="tpu_custom_call" | custom-call | tf_op jit(solution)/shard_map/backward_blocks/pallas_call | solution.py:721
Async XLA Ops:
  1.9 6.7 %collective-permute-start = (bf16[128,256]{1,0:T(8,128)(2,1)S(1)}, bf16[128,256]{1,0:T(8,128)(2,1)S(1)}, u32[]{:S(2)}, u32[]{:S(2)}) collective-permute-start(bf16[128,256]{1,0:T(8,128)(2,1)S(1)} %get-tuple-element.28), channel_id=1, source_target_pairs={{0,2},{1,3},{2,0},{3,1},{4,6},{5,7},{6,4},{7,5},{8,10},{9,11},{10,... | collective-permute-start | bytes 196616 | tf_op jit(solution)/shard_map/ppermute | solution.py:759
  4.9 3.7 %collective-permute-start.1 = (bf16[128,256]{1,0:T(8,128)(2,1)S(1)}, bf16[128,256]{1,0:T(8,128)(2,1)S(1)}, u32[]{:S(2)}, u32[]{:S(2)}) collective-permute-start(bf16[128,256]{1,0:T(8,128)(2,1)S(1)} %get-tuple-element.29), channel_id=1, source_target_pairs={{0,1},{1,0},{2,4},{3,5},{4,2},{5,3},{6,8},{7,9},{8,6},{9,7},{10,12... | collective-permute-start | bytes 196616 | tf_op jit(solution)/shard_map/ppermute | solution.py:758
  8.6 4.9 %copy-start = (f32[6,64,128]{2,1,0:T(8,128)S(1)}, f32[6,64,128]{2,1,0:T(8,128)}, u32[]{:S(2)}) copy-start(f32[6,64,128]{2,1,0:T(8,128)} %forcing.1) | copy-start | bytes 589828
  8.6 4.9 %copy-start.1 = (f32[64,128]{1,0:T(8,128)S(1)}, f32[64,128]{1,0:T(8,128)}, u32[]{:S(2)}) copy-start(f32[64,128]{1,0:T(8,128)} %surface_temp.1) | copy-start | bytes 98308
  8.9 4.6 %collective-permute-start.2 = (bf16[2,64,128]{2,1,0:T(8,128)(2,1)S(1)}, bf16[2,64,128]{2,1,0:T(8,128)(2,1)S(1)}, u32[]{:S(2)}, u32[]{:S(2)}) collective-permute-start(bf16[2,64,128]{2,1,0:T(8,128)(2,1)S(1)} %get-tuple-element.32), channel_id=1, source_target_pairs={{0,1},{1,0},{16,17},{17,16},{2,3},{3,2},{18,19},{19,18},{4,5},{5,4... | collective-permute-start | bytes 98312 | tf_op jit(solution)/shard_map/ppermute | solution.py:763
  9.4 4.0 %collective-permute-start.3 = (bf16[2,64,128]{2,1,0:T(8,128)(2,1)S(1)}, bf16[2,64,128]{2,1,0:T(8,128)(2,1)S(1)}, u32[]{:S(2)}, u32[]{:S(2)}) collective-permute-start(bf16[2,64,128]{2,1,0:T(8,128)(2,1)S(1)} %get-tuple-element.33), channel_id=1, source_target_pairs={{0,17},{1,16},{16,1},{17,0},{2,19},{3,18},{18,3},{19,2},{4,21},{5,... | collective-permute-start | bytes 98312 | tf_op jit(solution)/shard_map/ppermute | solution.py:762
  18.5 17.1 %all-to-all-start = ((bf16[32,8,640]{2,1,0:T(8,128)(2,1)}), bf16[32,8,640]{2,1,0:T(8,128)(2,1)S(1)}, u32[]{:S(2)}, u32[]{:S(2)}) async-start(bf16[32,8,640]{2,1,0:T(8,128)(2,1)} %get-tuple-element.39), calls=%async_computation | async-start | bytes 655360 | tf_op jit(solution)/shard_map/all_to_all | solution.py:771
  23.8 11.7 %copy-start.2 = (s32[64,128]{1,0:T(8,128)S(1)}, s32[64,128]{1,0:T(8,128)}, u32[]{:S(2)}) copy-start(s32[64,128]{1,0:T(8,128)} %land_mask.1) | copy-start | bytes 98308
  23.9 11.7 %copy-start.3 = (f32[64,128]{1,0:T(8,128)S(1)}, f32[64,128]{1,0:T(8,128)}, u32[]{:S(2)}) copy-start(f32[64,128]{1,0:T(8,128)} %ocean_temp.1) | copy-start | bytes 98308
  23.9 11.7 %copy-start.4 = (f32[64,128]{1,0:T(8,128)S(1)}, f32[64,128]{1,0:T(8,128)}, u32[]{:S(2)}) copy-start(f32[64,128]{1,0:T(8,128)} %ocean_ice.1) | copy-start | bytes 98308
  23.9 11.7 %copy-start.5 = (f32[64,128]{1,0:T(8,128)S(1)}, f32[64,128]{1,0:T(8,128)}, u32[]{:S(2)}) copy-start(f32[64,128]{1,0:T(8,128)} %layer_depth.1) | copy-start | bytes 98308
  36.7 10.8 %all-to-all-start.1 = ((bf16[32,8,256]{2,1,0:T(8,128)(2,1)}), bf16[32,8,256]{2,1,0:T(8,128)(2,1)S(1)}, u32[]{:S(2)}, u32[]{:S(2)}) async-start(bf16[32,8,256]{2,1,0:T(8,128)(2,1)} %get-tuple-element.43), calls=%async_computation.1 | async-start | bytes 262144 | tf_op jit(solution)/shard_map/all_to_all | solution.py:777

commit v5 on v4

--- a/solution.py
+++ b/solution.py
@@ -19,6 +19,7 @@
 STEP = 8
 GROUP = 4
 LAG = 8
+NEAR = 64
 
 
 def in_vmem(*arrays):
@@ -585,9 +586,12 @@
     )(*in_hbm(*args[:3]), *args[3:])
 
 
-def down_kernel(reduced, coupling, inverse, air_new, held, held_c, held_i, sem, out_sem):
+def down_kernel(
+    reduced, coupling, inverse, weight, air_new, near, held, held_c, held_i, sem, out_sem, sem_w
+):
     _, levels, rows, lanes = reduced.shape
     copies = fetch_levels([(reduced, held), (inverse, held_i), (coupling, held_c)], sem, levels, -1)
+    weights = fetch(weight.at[pl.ds(0, near.shape[0])], near, sem_w)
     outs = []
     for i, part in enumerate(copies):
         for c in part:
@@ -605,30 +609,31 @@
         at = pl.ds(levels - (i + 1) * STEP, STEP)
         outs.append(pltpu.make_async_copy(held.at[:, at], air_new.at[:, at], out_sem.at[i]))
         outs[i].start()
-    for c in outs:
+    for c in outs + weights:
         c.wait()
 
 
-def columns_down(reduced, coupling, inverse):
+def columns_down(reduced, coupling, inverse, weight):
     levels = reduced.shape[1]
     hbm = pl.BlockSpec(memory_space=pltpu.HBM)
     parts = levels // STEP
     return pl.pallas_call(
         down_kernel,
-        in_specs=[hbm] * 3,
-        out_specs=hbm,
-        out_shape=pltpu.HBM(reduced.shape, F32),
+        in_specs=[hbm] * 4,
+        out_specs=[hbm, pl.BlockSpec(memory_space=pltpu.VMEM)],
+        out_shape=[pltpu.HBM(reduced.shape, F32), pltpu.VMEM((NEAR,) + weight.shape[1:], BF16)],
         scratch_shapes=[
             pltpu.VMEM(reduced.shape, F32),
             pltpu.VMEM(coupling.shape, F32),
             pltpu.VMEM(inverse.shape, F32),
             pltpu.SemaphoreType.DMA((3 * parts,)),
             pltpu.SemaphoreType.DMA((parts,)),
+            pltpu.SemaphoreType.DMA((4,)),
         ],
         compiler_params=pltpu.CompilerParams(vmem_limit_bytes=16 * MIB),
         cost_estimate=pl.CostEstimate(flops=8 * reduced.size, bytes_accessed=12 * reduced.size, transcendentals=0),
         name="columns_down",
-    )(*in_hbm(reduced, coupling, inverse))
+    )(*in_hbm(reduced, coupling, inverse, weight))
 
 
 def ocean_kernel(arrived, land_mask, ocean_temp, ocean_ice, layer_depth, temp_new, ice_new, replies):
@@ -674,12 +679,13 @@
 
 
 def backward_kernel(
-    slots_far, column_far, returned, weight, seen, held, sem, pairs, sums, slots, block_column, sem_i
+    slots_far, column_far, returned, near, weight, seen, held, sem, pairs, sums, slots, block_column, sem_i
 ):
     lanes = weight.shape[1]
     total = returned.shape[0] * returned.shape[1]
     rows = seen.shape[1]
-    copies = fetch(weight, held, sem)
+    first, blocks = near.shape[0], weight.shape[0]
+    copies = fetch(weight.at[pl.ds(first, blocks - first)], held, sem)
     indices = fetch_indices((slots_far, column_far), (slots, block_column), sem_i)
     pairs[...] = jnp.zeros_like(pairs)
     sums[...] = jnp.zeros_like(sums)
@@ -691,17 +697,18 @@
         for at, out in pair:
             sums[pl.ds(pl.multiple_of(block_column[at] * 8, 8), 8), :] += out
 
-    size = weight.shape[0] // PARTS
+    size = held.shape[0] // PARTS
     for c in indices:
         c.wait()
     waiting = []
-    for at in range(0, weight.shape[0], 2):
-        if at % size == 0:
-            copies[at // size].wait()
+    for at in range(0, blocks, 2):
+        if at >= first and (at - first) % size == 0:
+            copies[(at - first) // size].wait()
+        block, k = (near, at) if at < first else (held, at - first)
         picked = [pairs[pl.ds(pl.multiple_of(slots[n] * 8, 8), 8), :] for n in (at, at + 1)]
         out = jnp.dot(
             jnp.concatenate(picked).astype(BF16),
-            jnp.concatenate([held[at], held[at + 1]], axis=1),
+            jnp.concatenate([block[k], block[k + 1]], axis=1),
             preferred_element_type=F32,
         )
         waiting.append(((at, out[:8, :lanes]), (at + 1, out[8:, lanes:])))
@@ -713,18 +720,18 @@
         seen[k] = sums[pl.ds(k, rows, stride=8), :]
 
 
-def backward(slots, block_column, returned, weight, rows):
+def backward(slots, block_column, returned, near, weight, rows):
     devices, bound, _ = returned.shape
     nonzeros, lanes, _ = weight.shape
     hbm = pl.BlockSpec(memory_space=pltpu.HBM)
     vmem = pl.BlockSpec(memory_space=pltpu.VMEM)
     return pl.pallas_call(
         backward_kernel,
-        in_specs=[hbm, hbm, vmem, hbm],
+        in_specs=[hbm, hbm, vmem, vmem, hbm],
         out_specs=vmem,
         out_shape=jax.ShapeDtypeStruct((2, rows, lanes), F32),
         scratch_shapes=[
-            pltpu.VMEM(weight.shape, BF16),
+            pltpu.VMEM((nonzeros - NEAR, lanes, lanes), BF16),
             pltpu.SemaphoreType.DMA((PARTS,)),
             pltpu.VMEM((devices * bound * 8, lanes), F32),
             pltpu.VMEM((rows * 8, lanes), F32),
@@ -734,7 +741,7 @@
         ],
         compiler_params=pltpu.CompilerParams(vmem_limit_bytes=16 * MIB),
         name="backward_blocks",
-    )(*in_hbm(slots, block_column), returned, *in_hbm(weight))
+    )(*in_hbm(slots, block_column), returned, *in_vmem(near), *in_hbm(weight))
 
 
 def local(
@@ -775,9 +782,9 @@
         arrived, land_mask, ocean_temp, ocean_ice, layer_depth
     )
     returned = lax.all_to_all(replies, ALL, split_axis=0, concat_axis=0, tiled=True)
-    air_new = columns_down(reduced, coupling, inverse)
+    air_new, near = columns_down(reduced, coupling, inverse, remap_weight)
     returned, air_new = lax.optimization_barrier((returned, air_new))
-    surface_seen = backward(slots, block_column, returned, remap_weight, surface_temp.shape[0])
+    surface_seen = backward(slots, block_column, returned, near, remap_weight, surface_temp.shape[0])
     return (air_new, surface_seen, ocean_temp_new, ocean_ice_new)
 
 

time: 52.2 us -> 51.7 us (level)
  waiting for transfers between devices: 6.09 us -> 5.23 us
    all_to_all x1, waiting for transfers between devices: 2.74 us -> 1.87 us  [local(): lax.all_to_all(replies, ALL, split_axis=0, concat_axis=0, tiled=True)]
  transfers between devices with their start and end apart: 6 -> 6, of which waited for: 2 -> 2; matrix products, arithmetic and copies ran while one was open for 0% -> 0% of each run, Pallas kernels for 39% -> 41%
where the time goes in v5:
time: 51.7 us; the launch traced here: 51.4 us
  Pallas kernels  32.6 us (63%)
  starting transfers between devices  12.7 us (25%)
  waiting for transfers between devices  5.23 us (10%)
  between operations  0.81 us (2%)
    pallas_call x1, Pallas kernels, columns_up(): pl.pallas_call(up_kernel, in_specs=[hbm] * 3 + [pl.BlockSpec(memory_space...  8.3 us
    pallas_call x1, Pallas kernels, columns_down(): pl.pallas_call(down_kernel, in_specs=[hbm] * 4, out_specs=[hbm, pl.BlockS...  6.35 us
    all_to_all x1, starting transfers between devices, local(): lax.all_to_all(payload, ALL, split_axis=0, concat_axis=0, tiled=True)  5.37 us
    pallas_call x1, Pallas kernels, forward(): pl.pallas_call(functools.partial(forward_kernel, bound=bound, levels=leve...  4.96 us
    pallas_call x1, Pallas kernels, backward(): pl.pallas_call(backward_kernel, in_specs=[hbm, hbm, vmem, vmem, hbm], out...  3.91 us
    pallas_call x1, Pallas kernels, pack_cols(): pl.pallas_call(functools.partial(cols_kernel, chunk=chunk), in_specs=[pl....  3.64 us
    all_to_all x1, waiting for transfers between devices, local(): lax.all_to_all(payload, ALL, split_axis=0, concat_axis=0, tiled=True)  3.34 us
    ppermute x1, starting transfers between devices, local(): got_a = lax.ppermute(rows_a, ALL, row_swaps(0))  3 us
  transfers between devices with their start and end apart: 6, of which 2 were waited for; matrix products, arithmetic and copies ran while one was open for 0% of the time, Pallas kernels for 41%

profile of v5, /device:TPU:0, one launch (start us, length us, event | category | flops | bytes accessed | tf_op | source)
XLA Modules:
  0.0 51.4 jit_solution(1661085891020073274)
XLA Ops:
  0.6 1.3 %pack_rows.1 = (bf16[128,256]{1,0:T(8,128)(2,1)S(1)}, bf16[128,256]{1,0:T(8,128)(2,1)S(1)}) custom-call(f32[128,64,128]{2,1,0:T(8,128)} %bitcast.2), custom_call_target="tpu_custom_call" | custom-call | tf_op jit(solution)/shard_map/pack_rows/pallas_call | solution.py:82
  1.9 3.0 %collective-permute-start = (bf16[128,256]{1,0:T(8,128)(2,1)S(1)}, bf16[128,256]{1,0:T(8,128)(2,1)S(1)}, u32[]{:S(2)}, u32[]{:S(2)}) collective-permute-start(bf16[128,256]{1,0:T(8,128)(2,1)S(1)} %get-tuple-element.30), channel_id=1, source_target_pairs={{0,2},{1,3},{2,0},{3,1},{4,6},{5,7},{6,4},{7,5},{8,10},{9,11},{10,... | collective-permute-start | bytes 196616 | tf_op jit(solution)/shard_map/ppermute | solution.py:766
  4.9 0.0 collective-permute-start.1
  4.9 3.6 %pack_cols.1 = (f32[2,64,128]{2,1,0:T(8,128)S(1)}, f32[2,64,128]{2,1,0:T(8,128)S(1)}, f32[2,64,128]{2,1,0:T(8,128)S(1)}, bf16[128,128,128]{2,1,0:T(8,128)(2,1)S(1)}) custom-call(f32[2,64,64,128]{3,2,1,0:T(8,128)} %air.3, bf16[256,128,128]{2,1,0:T(8,128)(2,1)} %weight.7), custom_call_target="tpu_custom_call" | custom-call | flops 4194304 | bytes 4194304 | tf_op jit(solution)/shard_map/pack_cols/pallas_call | solution.py:124
  8.6 0.0 copy-start
  8.6 0.0 copy-start.1
  8.6 0.0 collective-permute-done.got_a
  8.6 0.0 collective-permute-done.1.got_b
  8.6 0.2 strips.1
  8.9 0.6 %collective-permute-start.2 = (bf16[2,64,128]{2,1,0:T(8,128)(2,1)S(1)}, bf16[2,64,128]{2,1,0:T(8,128)(2,1)S(1)}, u32[]{:S(2)}, u32[]{:S(2)}) collective-permute-start(bf16[2,64,128]{2,1,0:T(8,128)(2,1)S(1)} %get-tuple-element.34), channel_id=1, source_target_pairs={{0,1},{1,0},{16,17},{17,16},{2,3},{3,2},{18,19},{19,18},{4,5},{5,4... | collective-permute-start | bytes 98312 | tf_op jit(solution)/shard_map/ppermute | solution.py:770
  9.4 1.2 %collective-permute-start.3 = (bf16[2,64,128]{2,1,0:T(8,128)(2,1)S(1)}, bf16[2,64,128]{2,1,0:T(8,128)(2,1)S(1)}, u32[]{:S(2)}, u32[]{:S(2)}) collective-permute-start(bf16[2,64,128]{2,1,0:T(8,128)(2,1)S(1)} %get-tuple-element.35), channel_id=1, source_target_pairs={{0,17},{1,16},{16,1},{17,0},{2,19},{3,18},{18,3},{19,2},{4,21},{5,... | collective-permute-start | bytes 98312 | tf_op jit(solution)/shard_map/ppermute | solution.py:769
  10.6 2.8 %pivots.1.inverse = f32[64,64,128]{2,1,0:T(8,128)} custom-call(f32[63,64,128]{2,1,0:T(8,128)} %coupling.5), custom_call_target="tpu_custom_call" | custom-call | flops 4128768 | bytes 4128768 | tf_op jit(solution)/shard_map/pivots/pallas_call | solution.py:456
  13.4 0.0 collective-permute-done.2.got_g
  13.5 0.0 collective-permute-done.3.got_x
  13.5 0.0 copy-done
  13.5 0.0 copy-done.1
  13.5 5.0 %forward_blocks.1 = (bf16[32,8,640]{2,1,0:T(8,128)(2,1)}, s32[256]{0:T(256)}, f32[2,64,128]{2,1,0:T(8,128)S(1)}) custom-call(s32[256]{0:T(256)} %bitcast.3, s32[256]{0:T(256)} %row_far.1, s32[256]{0:T(256)} %column_far.3, f32[2,64,128]{2,1,0:T(8,128)S(1)} %get-tuple-element.29.air, f32[6,64,128]{2,1,0:T(8,128)S(1)} %copy-done, f32[64,128]{1,0:T(8,128)S(1)} %copy-done.1, ...), custom_call_target="tpu_custom_call" | custom-call | tf_op jit(solution)/shard_map/forward_blocks/pallas_call | solution.py:374
  18.5 5.4 %all-to-all-start = ((bf16[32,8,640]{2,1,0:T(8,128)(2,1)}), bf16[32,8,640]{2,1,0:T(8,128)(2,1)S(1)}, u32[]{:S(2)}, u32[]{:S(2)}) async-start(bf16[32,8,640]{2,1,0:T(8,128)(2,1)} %get-tuple-element.41), calls=%async_computation | async-start | bytes 655360 | tf_op jit(solution)/shard_map/all_to_all | solution.py:778
  23.8 0.0 copy-start.2
  23.8 0.0 copy-start.3
  23.9 0.0 copy-start.4
  23.9 0.0 copy-start.5
  23.9 8.3 %columns_up.1.reduced = f32[2,64,64,128]{3,2,1,0:T(8,128)} custom-call(f32[2,64,64,128]{3,2,1,0:T(8,128)} %air.3, f32[63,64,128]{2,1,0:T(8,128)} %coupling.5, f32[64,64,128]{2,1,0:T(8,128)} %pivots.1.inverse, bf16[128,256]{1,0:T(8,128)(2,1)S(1)} %collective-permute-done.got_a, bf16[128,256]{1,0:T(8,128)(2,1)S(1)} %collective-permute-done.1.got_b, ...), custom_call_target="tpu_custom_call" | custom-call | flops 41943040 | bytes 12582912 | tf_op jit(solution)/shard_map/columns_up/pallas_call | solution.py:565
  32.2 3.3 %all-to-all-done.arrived = bf16[32,8,640]{2,1,0:T(8,128)(2,1)S(1)} async-done(((bf16[32,8,640]{2,1,0:T(8,128)(2,1)}), bf16[32,8,640]{2,1,0:T(8,128)(2,1)S(1)}, u32[]{:S(2)}, u32[]{:S(2)}) %all-to-all-start) | async-done | bytes 327712 | tf_op jit(solution)/shard_map/all_to_all | solution.py:778
  35.5 0.0 copy-done.2
  35.5 0.0 copy-done.3
  35.5 0.0 copy-done.4
  35.5 0.0 copy-done.5
  35.6 1.1 %ocean.1 = (f32[64,128]{1,0:T(8,128)}, f32[64,128]{1,0:T(8,128)}, bf16[32,8,256]{2,1,0:T(8,128)(2,1)}) custom-call(bf16[32,8,640]{2,1,0:T(8,128)(2,1)S(1)} %all-to-all-done.arrived, s32[64,128]{1,0:T(8,128)S(1)} %copy-done.2, f32[64,128]{1,0:T(8,128)S(1)} %copy-done.3, f32[64,128]{1,0:T(8,128)S(1)} %copy-done.4, f32[64,128]{1,0:T(8,128)S(1)} %copy-done.5), custom_call_target="tpu_custom_call" | custom-call | tf_op jit(solution)/shard_map/ocean/pallas_call | solution.py:667
  36.7 2.6 %all-to-all-start.1 = ((bf16[32,8,256]{2,1,0:T(8,128)(2,1)}), bf16[32,8,256]{2,1,0:T(8,128)(2,1)S(1)}, u32[]{:S(2)}, u32[]{:S(2)}) async-start(bf16[32,8,256]{2,1,0:T(8,128)(2,1)} %get-tuple-element.45), calls=%async_computation.1 | async-start | bytes 262144 | tf_op jit(solution)/shard_map/all_to_all | solution.py:784
  39.3 6.3 %columns_down.1 = (f32[2,64,64,128]{3,2,1,0:T(8,128)}, bf16[64,128,128]{2,1,0:T(8,128)(2,1)S(1)}) custom-call(f32[2,64,64,128]{3,2,1,0:T(8,128)} %columns_up.1.reduced, f32[63,64,128]{2,1,0:T(8,128)} %coupling.5, f32[64,64,128]{2,1,0:T(8,128)} %pivots.1.inverse, bf16[256,128,128]{2,1,0:T(8,128)(2,1)} %weight.7), custom_call_target="tpu_custom_call" | custom-call | flops 8388608 | bytes 12582912 | tf_op jit(solution)/shard_map/columns_down/pallas_call | solution.py:620
  45.6 1.9 %all-to-all-done.1.returned = bf16[32,8,256]{2,1,0:T(8,128)(2,1)S(1)} async-done(((bf16[32,8,256]{2,1,0:T(8,128)(2,1)}), bf16[32,8,256]{2,1,0:T(8,128)(2,1)S(1)}, u32[]{:S(2)}, u32[]{:S(2)}) %all-to-all-start.1) | async-done | bytes 131104 | tf_op jit(solution)/shard_map/all_to_all | solution.py:784
  47.5 3.9 %backward_blocks.1 = f32[2,64,128]{2,1,0:T(8,128)} custom-call(s32[256]{0:T(256)} %get-tuple-element.49.slots_far, s32[256]{0:T(256)} %column_far.3, bf16[32,8,256]{2,1,0:T(8,128)(2,1)S(1)} %all-to-all-done.1.returned, bf16[64,128,128]{2,1,0:T(8,128)(2,1)S(1)} %get-tuple-element.51.near, bf16[256,128,128]{2,1,0:T(8,128)(2,1)} %weight.7), custom_call_target="tpu_custom_call" | custom-call | tf_op jit(solution)/shard_map/backward_blocks/pallas_call | solution.py:728
Async XLA Ops:
  1.9 6.7 %collective-permute-start = (bf16[128,256]{1,0:T(8,128)(2,1)S(1)}, bf16[128,256]{1,0:T(8,128)(2,1)S(1)}, u32[]{:S(2)}, u32[]{:S(2)}) collective-permute-start(bf16[128,256]{1,0:T(8,128)(2,1)S(1)} %get-tuple-element.30), channel_id=1, source_target_pairs={{0,2},{1,3},{2,0},{3,1},{4,6},{5,7},{6,4},{7,5},{8,10},{9,11},{10,... | collective-permute-start | bytes 196616 | tf_op jit(solution)/shard_map/ppermute | solution.py:766
  4.9 3.7 %collective-permute-start.1 = (bf16[128,256]{1,0:T(8,128)(2,1)S(1)}, bf16[128,256]{1,0:T(8,128)(2,1)S(1)}, u32[]{:S(2)}, u32[]{:S(2)}) collective-permute-start(bf16[128,256]{1,0:T(8,128)(2,1)S(1)} %get-tuple-element.31), channel_id=1, source_target_pairs={{0,1},{1,0},{2,4},{3,5},{4,2},{5,3},{6,8},{7,9},{8,6},{9,7},{10,12... | collective-permute-start | bytes 196616 | tf_op jit(solution)/shard_map/ppermute | solution.py:765
  8.6 4.9 %copy-start = (f32[6,64,128]{2,1,0:T(8,128)S(1)}, f32[6,64,128]{2,1,0:T(8,128)}, u32[]{:S(2)}) copy-start(f32[6,64,128]{2,1,0:T(8,128)} %forcing.1) | copy-start | bytes 589828
  8.6 4.9 %copy-start.1 = (f32[64,128]{1,0:T(8,128)S(1)}, f32[64,128]{1,0:T(8,128)}, u32[]{:S(2)}) copy-start(f32[64,128]{1,0:T(8,128)} %surface_temp.1) | copy-start | bytes 98308
  8.9 4.6 %collective-permute-start.2 = (bf16[2,64,128]{2,1,0:T(8,128)(2,1)S(1)}, bf16[2,64,128]{2,1,0:T(8,128)(2,1)S(1)}, u32[]{:S(2)}, u32[]{:S(2)}) collective-permute-start(bf16[2,64,128]{2,1,0:T(8,128)(2,1)S(1)} %get-tuple-element.34), channel_id=1, source_target_pairs={{0,1},{1,0},{16,17},{17,16},{2,3},{3,2},{18,19},{19,18},{4,5},{5,4... | collective-permute-start | bytes 98312 | tf_op jit(solution)/shard_map/ppermute | solution.py:770
  9.4 4.0 %collective-permute-start.3 = (bf16[2,64,128]{2,1,0:T(8,128)(2,1)S(1)}, bf16[2,64,128]{2,1,0:T(8,128)(2,1)S(1)}, u32[]{:S(2)}, u32[]{:S(2)}) collective-permute-start(bf16[2,64,128]{2,1,0:T(8,128)(2,1)S(1)} %get-tuple-element.35), channel_id=1, source_target_pairs={{0,17},{1,16},{16,1},{17,0},{2,19},{3,18},{18,3},{19,2},{4,21},{5,... | collective-permute-start | bytes 98312 | tf_op jit(solution)/shard_map/ppermute | solution.py:769
  18.5 17.1 %all-to-all-start = ((bf16[32,8,640]{2,1,0:T(8,128)(2,1)}), bf16[32,8,640]{2,1,0:T(8,128)(2,1)S(1)}, u32[]{:S(2)}, u32[]{:S(2)}) async-start(bf16[32,8,640]{2,1,0:T(8,128)(2,1)} %get-tuple-element.41), calls=%async_computation | async-start | bytes 655360 | tf_op jit(solution)/shard_map/all_to_all | solution.py:778
  23.8 11.7 %copy-start.2 = (s32[64,128]{1,0:T(8,128)S(1)}, s32[64,128]{1,0:T(8,128)}, u32[]{:S(2)}) copy-start(s32[64,128]{1,0:T(8,128)} %land_mask.1) | copy-start | bytes 98308
  23.8 11.7 %copy-start.3 = (f32[64,128]{1,0:T(8,128)S(1)}, f32[64,128]{1,0:T(8,128)}, u32[]{:S(2)}) copy-start(f32[64,128]{1,0:T(8,128)} %ocean_temp.1) | copy-start | bytes 98308
  23.9 11.7 %copy-start.4 = (f32[64,128]{1,0:T(8,128)S(1)}, f32[64,128]{1,0:T(8,128)}, u32[]{:S(2)}) copy-start(f32[64,128]{1,0:T(8,128)} %ocean_ice.1) | copy-start | bytes 98308
  23.9 11.7 %copy-start.5 = (f32[64,128]{1,0:T(8,128)S(1)}, f32[64,128]{1,0:T(8,128)}, u32[]{:S(2)}) copy-start(f32[64,128]{1,0:T(8,128)} %layer_depth.1) | copy-start | bytes 98308
  36.7 10.8 %all-to-all-start.1 = ((bf16[32,8,256]{2,1,0:T(8,128)(2,1)}), bf16[32,8,256]{2,1,0:T(8,128)(2,1)S(1)}, u32[]{:S(2)}, u32[]{:S(2)}) async-start(bf16[32,8,256]{2,1,0:T(8,128)(2,1)} %get-tuple-element.45), calls=%async_computation.1 | async-start | bytes 262144 | tf_op jit(solution)/shard_map/all_to_all | solution.py:784

commit v6 on v5

--- a/solution.py
+++ b/solution.py
@@ -15,7 +15,7 @@
 SURFACE_STEP = 0.5
 MIX = 0.2
 MIB = 1 << 20
-PARTS = 8
+PARTS = 16
 STEP = 8
 GROUP = 4
 LAG = 8

time: 51.7 us -> 53.1 us (1.027)
  Pallas kernels: 32.6 us -> 34 us
    pallas_call x1, Pallas kernels: 3.91 us -> 5.05 us  [backward(): pl.pallas_call(backward_kernel, in_specs=[hbm, hbm, vmem, vmem, hbm], out...]
  transfers between devices with their start and end apart: 6 -> 6, of which waited for: 2 -> 2; matrix products, arithmetic and copies ran while one was open for 0% -> 0% of each run, Pallas kernels for 41% -> 40%
where the time goes in v6:
time: 53.1 us; the launch traced here: 52.8 us
  Pallas kernels  34 us (64%)
  starting transfers between devices  12.7 us (24%)
  waiting for transfers between devices  5.23 us (10%)
  between operations  0.81 us (2%)
    pallas_call x1, Pallas kernels, columns_up(): pl.pallas_call(up_kernel, in_specs=[hbm] * 3 + [pl.BlockSpec(memory_space...  8.3 us
    pallas_call x1, Pallas kernels, columns_down(): pl.pallas_call(down_kernel, in_specs=[hbm] * 4, out_specs=[hbm, pl.BlockS...  6.35 us
    all_to_all x1, starting transfers between devices, local(): lax.all_to_all(payload, ALL, split_axis=0, concat_axis=0, tiled=True)  5.37 us
    pallas_call x1, Pallas kernels, backward(): pl.pallas_call(backward_kernel, in_specs=[hbm, hbm, vmem, vmem, hbm], out...  5.05 us
    pallas_call x1, Pallas kernels, forward(): pl.pallas_call(functools.partial(forward_kernel, bound=bound, levels=leve...  5.05 us
    pallas_call x1, Pallas kernels, pack_cols(): pl.pallas_call(functools.partial(cols_kernel, chunk=chunk), in_specs=[pl....  3.81 us
    all_to_all x1, waiting for transfers between devices, local(): lax.all_to_all(payload, ALL, split_axis=0, concat_axis=0, tiled=True)  3.35 us
    ppermute x1, starting transfers between devices, local(): got_a = lax.ppermute(rows_a, ALL, row_swaps(0))  3 us
  transfers between devices with their start and end apart: 6, of which 2 were waited for; matrix products, arithmetic and copies ran while one was open for 0% of the time, Pallas kernels for 40%

profile of v6, /device:TPU:0, one launch (start us, length us, event | category | flops | bytes accessed | tf_op | source)
XLA Modules:
  0.0 52.8 jit_solution(9688279209632690036)
XLA Ops:
  0.6 1.3 %pack_rows.1 = (bf16[128,256]{1,0:T(8,128)(2,1)S(1)}, bf16[128,256]{1,0:T(8,128)(2,1)S(1)}) custom-call(f32[128,64,128]{2,1,0:T(8,128)} %bitcast.2), custom_call_target="tpu_custom_call" | custom-call | tf_op jit(solution)/shard_map/pack_rows/pallas_call | solution.py:82
  1.9 3.0 %collective-permute-start = (bf16[128,256]{1,0:T(8,128)(2,1)S(1)}, bf16[128,256]{1,0:T(8,128)(2,1)S(1)}, u32[]{:S(2)}, u32[]{:S(2)}) collective-permute-start(bf16[128,256]{1,0:T(8,128)(2,1)S(1)} %get-tuple-element.30), channel_id=1, source_target_pairs={{0,2},{1,3},{2,0},{3,1},{4,6},{5,7},{6,4},{7,5},{8,10},{9,11},{10,... | collective-permute-start | bytes 196616 | tf_op jit(solution)/shard_map/ppermute | solution.py:766
  4.9 0.0 collective-permute-start.1
  4.9 3.8 %pack_cols.1 = (f32[2,64,128]{2,1,0:T(8,128)S(1)}, f32[2,64,128]{2,1,0:T(8,128)S(1)}, f32[2,64,128]{2,1,0:T(8,128)S(1)}, bf16[128,128,128]{2,1,0:T(8,128)(2,1)S(1)}) custom-call(f32[2,64,64,128]{3,2,1,0:T(8,128)} %air.3, bf16[256,128,128]{2,1,0:T(8,128)(2,1)} %weight.7), custom_call_target="tpu_custom_call" | custom-call | flops 4194304 | bytes 4194304 | tf_op jit(solution)/shard_map/pack_cols/pallas_call | solution.py:124
  8.7 0.0 copy-start
  8.8 0.0 copy-start.1
  8.8 0.0 collective-permute-done.got_a
  8.8 0.0 collective-permute-done.1.got_b
  8.8 0.2 strips.1
  9.0 0.6 %collective-permute-start.2 = (bf16[2,64,128]{2,1,0:T(8,128)(2,1)S(1)}, bf16[2,64,128]{2,1,0:T(8,128)(2,1)S(1)}, u32[]{:S(2)}, u32[]{:S(2)}) collective-permute-start(bf16[2,64,128]{2,1,0:T(8,128)(2,1)S(1)} %get-tuple-element.34), channel_id=1, source_target_pairs={{0,1},{1,0},{16,17},{17,16},{2,3},{3,2},{18,19},{19,18},{4,5},{5,4... | collective-permute-start | bytes 98312 | tf_op jit(solution)/shard_map/ppermute | solution.py:770
  9.6 1.2 %collective-permute-start.3 = (bf16[2,64,128]{2,1,0:T(8,128)(2,1)S(1)}, bf16[2,64,128]{2,1,0:T(8,128)(2,1)S(1)}, u32[]{:S(2)}, u32[]{:S(2)}) collective-permute-start(bf16[2,64,128]{2,1,0:T(8,128)(2,1)S(1)} %get-tuple-element.35), channel_id=1, source_target_pairs={{0,17},{1,16},{16,1},{17,0},{2,19},{3,18},{18,3},{19,2},{4,21},{5,... | collective-permute-start | bytes 98312 | tf_op jit(solution)/shard_map/ppermute | solution.py:769
  10.8 2.8 %pivots.1.inverse = f32[64,64,128]{2,1,0:T(8,128)} custom-call(f32[63,64,128]{2,1,0:T(8,128)} %coupling.5), custom_call_target="tpu_custom_call" | custom-call | flops 4128768 | bytes 4128768 | tf_op jit(solution)/shard_map/pivots/pallas_call | solution.py:456
  13.6 0.0 collective-permute-done.2.got_g
  13.6 0.0 collective-permute-done.3.got_x
  13.6 0.0 copy-done
  13.6 0.0 copy-done.1
  13.7 5.0 %forward_blocks.1 = (bf16[32,8,640]{2,1,0:T(8,128)(2,1)}, s32[256]{0:T(256)}, f32[2,64,128]{2,1,0:T(8,128)S(1)}) custom-call(s32[256]{0:T(256)} %bitcast.3, s32[256]{0:T(256)} %row_far.1, s32[256]{0:T(256)} %column_far.3, f32[2,64,128]{2,1,0:T(8,128)S(1)} %get-tuple-element.29.air, f32[6,64,128]{2,1,0:T(8,128)S(1)} %copy-done, f32[64,128]{1,0:T(8,128)S(1)} %copy-done.1, ...), custom_call_target="tpu_custom_call" | custom-call | tf_op jit(solution)/shard_map/forward_blocks/pallas_call | solution.py:374
  18.7 5.4 %all-to-all-start = ((bf16[32,8,640]{2,1,0:T(8,128)(2,1)}), bf16[32,8,640]{2,1,0:T(8,128)(2,1)S(1)}, u32[]{:S(2)}, u32[]{:S(2)}) async-start(bf16[32,8,640]{2,1,0:T(8,128)(2,1)} %get-tuple-element.41), calls=%async_computation | async-start | bytes 655360 | tf_op jit(solution)/shard_map/all_to_all | solution.py:778
  24.1 0.0 copy-start.2
  24.1 0.0 copy-start.3
  24.1 0.0 copy-start.4
  24.1 0.0 copy-start.5
  24.1 8.3 %columns_up.1.reduced = f32[2,64,64,128]{3,2,1,0:T(8,128)} custom-call(f32[2,64,64,128]{3,2,1,0:T(8,128)} %air.3, f32[63,64,128]{2,1,0:T(8,128)} %coupling.5, f32[64,64,128]{2,1,0:T(8,128)} %pivots.1.inverse, bf16[128,256]{1,0:T(8,128)(2,1)S(1)} %collective-permute-done.got_a, bf16[128,256]{1,0:T(8,128)(2,1)S(1)} %collective-permute-done.1.got_b, ...), custom_call_target="tpu_custom_call" | custom-call | flops 41943040 | bytes 12582912 | tf_op jit(solution)/shard_map/columns_up/pallas_call | solution.py:565
  32.4 3.3 %all-to-all-done.arrived = bf16[32,8,640]{2,1,0:T(8,128)(2,1)S(1)} async-done(((bf16[32,8,640]{2,1,0:T(8,128)(2,1)}), bf16[32,8,640]{2,1,0:T(8,128)(2,1)S(1)}, u32[]{:S(2)}, u32[]{:S(2)}) %all-to-all-start) | async-done | bytes 327712 | tf_op jit(solution)/shard_map/all_to_all | solution.py:778
  35.8 0.0 copy-done.2
  35.8 0.0 copy-done.3
  35.8 0.0 copy-done.4
  35.8 0.0 copy-done.5
  35.8 1.1 %ocean.1 = (f32[64,128]{1,0:T(8,128)}, f32[64,128]{1,0:T(8,128)}, bf16[32,8,256]{2,1,0:T(8,128)(2,1)}) custom-call(bf16[32,8,640]{2,1,0:T(8,128)(2,1)S(1)} %all-to-all-done.arrived, s32[64,128]{1,0:T(8,128)S(1)} %copy-done.2, f32[64,128]{1,0:T(8,128)S(1)} %copy-done.3, f32[64,128]{1,0:T(8,128)S(1)} %copy-done.4, f32[64,128]{1,0:T(8,128)S(1)} %copy-done.5), custom_call_target="tpu_custom_call" | custom-call | tf_op jit(solution)/shard_map/ocean/pallas_call | solution.py:667
  36.9 2.6 %all-to-all-start.1 = ((bf16[32,8,256]{2,1,0:T(8,128)(2,1)}), bf16[32,8,256]{2,1,0:T(8,128)(2,1)S(1)}, u32[]{:S(2)}, u32[]{:S(2)}) async-start(bf16[32,8,256]{2,1,0:T(8,128)(2,1)} %get-tuple-element.45), calls=%async_computation.1 | async-start | bytes 262144 | tf_op jit(solution)/shard_map/all_to_all | solution.py:784
  39.5 6.3 %columns_down.1 = (f32[2,64,64,128]{3,2,1,0:T(8,128)}, bf16[64,128,128]{2,1,0:T(8,128)(2,1)S(1)}) custom-call(f32[2,64,64,128]{3,2,1,0:T(8,128)} %columns_up.1.reduced, f32[63,64,128]{2,1,0:T(8,128)} %coupling.5, f32[64,64,128]{2,1,0:T(8,128)} %pivots.1.inverse, bf16[256,128,128]{2,1,0:T(8,128)(2,1)} %weight.7), custom_call_target="tpu_custom_call" | custom-call | flops 8388608 | bytes 12582912 | tf_op jit(solution)/shard_map/columns_down/pallas_call | solution.py:620
  45.9 1.9 %all-to-all-done.1.returned = bf16[32,8,256]{2,1,0:T(8,128)(2,1)S(1)} async-done(((bf16[32,8,256]{2,1,0:T(8,128)(2,1)}), bf16[32,8,256]{2,1,0:T(8,128)(2,1)S(1)}, u32[]{:S(2)}, u32[]{:S(2)}) %all-to-all-start.1) | async-done | bytes 131104 | tf_op jit(solution)/shard_map/all_to_all | solution.py:784
  47.7 5.1 %backward_blocks.1 = f32[2,64,128]{2,1,0:T(8,128)} custom-call(s32[256]{0:T(256)} %get-tuple-element.49.slots_far, s32[256]{0:T(256)} %column_far.3, bf16[32,8,256]{2,1,0:T(8,128)(2,1)S(1)} %all-to-all-done.1.returned, bf16[64,128,128]{2,1,0:T(8,128)(2,1)S(1)} %get-tuple-element.51.near, bf16[256,128,128]{2,1,0:T(8,128)(2,1)} %weight.7), custom_call_target="tpu_custom_call" | custom-call | tf_op jit(solution)/shard_map/backward_blocks/pallas_call | solution.py:728
Async XLA Ops:
  1.9 6.8 %collective-permute-start = (bf16[128,256]{1,0:T(8,128)(2,1)S(1)}, bf16[128,256]{1,0:T(8,128)(2,1)S(1)}, u32[]{:S(2)}, u32[]{:S(2)}) collective-permute-start(bf16[128,256]{1,0:T(8,128)(2,1)S(1)} %get-tuple-element.30), channel_id=1, source_target_pairs={{0,2},{1,3},{2,0},{3,1},{4,6},{5,7},{6,4},{7,5},{8,10},{9,11},{10,... | collective-permute-start | bytes 196616 | tf_op jit(solution)/shard_map/ppermute | solution.py:766
  4.9 3.9 %collective-permute-start.1 = (bf16[128,256]{1,0:T(8,128)(2,1)S(1)}, bf16[128,256]{1,0:T(8,128)(2,1)S(1)}, u32[]{:S(2)}, u32[]{:S(2)}) collective-permute-start(bf16[128,256]{1,0:T(8,128)(2,1)S(1)} %get-tuple-element.31), channel_id=1, source_target_pairs={{0,1},{1,0},{2,4},{3,5},{4,2},{5,3},{6,8},{7,9},{8,6},{9,7},{10,12... | collective-permute-start | bytes 196616 | tf_op jit(solution)/shard_map/ppermute | solution.py:765
  8.7 4.9 %copy-start = (f32[6,64,128]{2,1,0:T(8,128)S(1)}, f32[6,64,128]{2,1,0:T(8,128)}, u32[]{:S(2)}) copy-start(f32[6,64,128]{2,1,0:T(8,128)} %forcing.1) | copy-start | bytes 589828
  8.8 4.9 %copy-start.1 = (f32[64,128]{1,0:T(8,128)S(1)}, f32[64,128]{1,0:T(8,128)}, u32[]{:S(2)}) copy-start(f32[64,128]{1,0:T(8,128)} %surface_temp.1) | copy-start | bytes 98308
  9.0 4.6 %collective-permute-start.2 = (bf16[2,64,128]{2,1,0:T(8,128)(2,1)S(1)}, bf16[2,64,128]{2,1,0:T(8,128)(2,1)S(1)}, u32[]{:S(2)}, u32[]{:S(2)}) collective-permute-start(bf16[2,64,128]{2,1,0:T(8,128)(2,1)S(1)} %get-tuple-element.34), channel_id=1, source_target_pairs={{0,1},{1,0},{16,17},{17,16},{2,3},{3,2},{18,19},{19,18},{4,5},{5,4... | collective-permute-start | bytes 98312 | tf_op jit(solution)/shard_map/ppermute | solution.py:770
  9.6 4.0 %collective-permute-start.3 = (bf16[2,64,128]{2,1,0:T(8,128)(2,1)S(1)}, bf16[2,64,128]{2,1,0:T(8,128)(2,1)S(1)}, u32[]{:S(2)}, u32[]{:S(2)}) collective-permute-start(bf16[2,64,128]{2,1,0:T(8,128)(2,1)S(1)} %get-tuple-element.35), channel_id=1, source_target_pairs={{0,17},{1,16},{16,1},{17,0},{2,19},{3,18},{18,3},{19,2},{4,21},{5,... | collective-permute-start | bytes 98312 | tf_op jit(solution)/shard_map/ppermute | solution.py:769
  18.7 17.1 %all-to-all-start = ((bf16[32,8,640]{2,1,0:T(8,128)(2,1)}), bf16[32,8,640]{2,1,0:T(8,128)(2,1)S(1)}, u32[]{:S(2)}, u32[]{:S(2)}) async-start(bf16[32,8,640]{2,1,0:T(8,128)(2,1)} %get-tuple-element.41), calls=%async_computation | async-start | bytes 655360 | tf_op jit(solution)/shard_map/all_to_all | solution.py:778
  24.1 11.7 %copy-start.2 = (s32[64,128]{1,0:T(8,128)S(1)}, s32[64,128]{1,0:T(8,128)}, u32[]{:S(2)}) copy-start(s32[64,128]{1,0:T(8,128)} %land_mask.1) | copy-start | bytes 98308
  24.1 11.7 %copy-start.3 = (f32[64,128]{1,0:T(8,128)S(1)}, f32[64,128]{1,0:T(8,128)}, u32[]{:S(2)}) copy-start(f32[64,128]{1,0:T(8,128)} %ocean_temp.1) | copy-start | bytes 98308
  24.1 11.7 %copy-start.4 = (f32[64,128]{1,0:T(8,128)S(1)}, f32[64,128]{1,0:T(8,128)}, u32[]{:S(2)}) copy-start(f32[64,128]{1,0:T(8,128)} %ocean_ice.1) | copy-start | bytes 98308
  24.1 11.7 %copy-start.5 = (f32[64,128]{1,0:T(8,128)S(1)}, f32[64,128]{1,0:T(8,128)}, u32[]{:S(2)}) copy-start(f32[64,128]{1,0:T(8,128)} %layer_depth.1) | copy-start | bytes 98308
  36.9 10.8 %all-to-all-start.1 = ((bf16[32,8,256]{2,1,0:T(8,128)(2,1)}), bf16[32,8,256]{2,1,0:T(8,128)(2,1)S(1)}, u32[]{:S(2)}, u32[]{:S(2)}) async-start(bf16[32,8,256]{2,1,0:T(8,128)(2,1)} %get-tuple-element.45), calls=%async_computation.1 | async-start | bytes 262144 | tf_op jit(solution)/shard_map/all_to_all | solution.py:784
